TPU v7x, 128 devices: a whole 4x4x4 slice. The times are simulated.
128 devices in a mesh: hg: 4 (over x), grp: 8 (over y, core), side: 4 (over z).
Axes of the slice: x: 4, y: 4, z: 4, core: 2. Of those that a mesh axis runs over, the one named last changes fastest.
Arguments:
- q_nope: bfloat16 [128, 8192], P(('grp', 'side'), 'hg'), may hold values from -6 to 6
- q_rope: bfloat16 [128, 4096], P(('grp', 'side'), 'hg'), may hold values from -16 to 16
- w_absorb: bfloat16 [64, 128, 512], P('hg'), may hold values from -0.5 to 0.5
- cache_latent: bfloat16 [64, 4096, 512], P(('grp', 'side')), may hold values from -6 to 6
- cache_rope: bfloat16 [64, 64, 4096], P(('grp', 'side')), may hold values from -512 to 512
- lengths: int32 [64], P(('grp', 'side')), may hold values from 4 to 4096, as said below
- w_value: bfloat16 [64, 512, 128], P('hg'), may hold values from -2 to 2
- w_out: bfloat16 [8192, 7168], P('hg', ('grp', 'side')), may hold values from -0.0625 to 0.0625
- residual: bfloat16 [128, 7168], P(('grp', 'side')), may hold values from -6 to 6
- norm_gain: bfloat16 [7168], replicated, may hold values from 0.5 to 1.5
- routes: int32 [128, 4], P(('grp', 'side')), may hold values from 0 to 15, all different within a row; in each aligned block of 4 rows (0 to 3, 4 to 7, ...) at most 2 rows name the same one
- gate_int: int32 [128, 4], P(('grp', 'side')), may hold values from 1 to 255
- w_gate: bfloat16 [16, 7168, 2048], P('grp', None, ('hg', 'side')), may hold values from -0.0625 to 0.0625
- w_up: bfloat16 [16, 7168, 2048], P('grp', None, ('hg', 'side')), may hold values from -0.0625 to 0.0625
- w_down: bfloat16 [16, 2048, 7168], P('grp', ('hg', 'side')), may hold values from -0.125 to 0.125
Outputs:
- layer_out: bfloat16 [128, 7168], P(('grp', 'side'), 'hg')
Inputs may be any that keep to these rules, and one draw needn't show every extreme that they name: `lengths`: one request in every draw has exactly 4096 filled positions. `routes`: each row names 4 different experts; among the 4 tokens of one index of grp and side, no expert is named by more than 2 tokens, a bound that some block reaches.
All inputs are finite; a program needn't handle non-finite values.
Results may differ from a plain program's by a relative error of at most 0.0095.
Values may be sent and summed in bfloat16 or wider, within the bound.
No kernel may reach another device: no remote copies, remote signals or barrier semaphores. Data moves between devices by JAX's collectives and lax.ppermute only.
A program may use at most 192 MiB of HBM per device.

v0:
```python
import jax
import jax.numpy as jnp
from jax import lax
from jax.sharding import PartitionSpec as P

LAT = 512
ROPE = 64
NOPE = 128
VDIM = 128
QPR = 2
LEN = 4096


EPS = 1e-06
ROUTE_SCALE = 2.5


def body(
    q_nope,
    q_rope,
    w_absorb,
    cache_latent,
    cache_rope,
    lengths,
    w_value,
    w_out,
    residual,
    norm_gain,
    routes,
    gate_int,
    w_gate,
    w_up,
    w_down,
):
    heads = w_absorb.shape[0]
    tok_rows = q_nope.shape[0]
    requests = cache_latent.shape[0]
    width = residual.shape[1]
    groups = lax.axis_size("grp")
    sides = lax.axis_size("side")
    hg_count = lax.axis_size("hg")
    query = q_nope.reshape(tok_rows, heads, NOPE)
    q_latent = jnp.einsum(
        "thn,hnc->thc", query, w_absorb, preferred_element_type=jnp.float32
    ).astype(jnp.bfloat16)
    q_latent = q_latent.reshape(requests, QPR, heads, LAT)
    q_pos = q_rope.reshape(requests, QPR, heads, ROPE)
    scale = (NOPE + ROPE) ** (-0.5)
    scores = jnp.einsum(
        "rqhc,rpc->rqhp", q_latent, cache_latent, preferred_element_type=jnp.float32
    )
    scores = scores + jnp.einsum(
        "rqhe,rep->rqhp", q_pos, cache_rope, preferred_element_type=jnp.float32
    )
    scores = scores * scale
    position = jnp.arange(LEN, dtype=jnp.int32)
    limit = lengths[:, None] - QPR + jnp.arange(QPR, dtype=jnp.int32)[None, :]
    valid = position[None, None, None, :] <= limit[:, :, None, None]
    scores = jnp.where(valid, scores, -jnp.inf)
    top = jnp.max(scores, axis=-1, keepdims=True)
    weights = jnp.exp(scores - top)
    probs = (weights / jnp.sum(weights, axis=-1, keepdims=True)).astype(jnp.bfloat16)
    latent_out = jnp.einsum(
        "rqhp,rpc->rqhc", probs, cache_latent, preferred_element_type=jnp.float32
    ).astype(jnp.bfloat16)
    latent_out = latent_out.reshape(tok_rows, heads, LAT)
    values = jnp.einsum(
        "thc,hcv->thv", latent_out, w_value, preferred_element_type=jnp.float32
    ).astype(jnp.bfloat16)
    values = values.reshape(tok_rows, heads * VDIM)
    partial_cols = jnp.dot(
        lax.all_gather(values, ("grp", "side"), axis=0, tiled=True),
        w_out,
        preferred_element_type=jnp.float32,
    )
    columns = lax.all_to_all(partial_cols, ("grp", "side"), split_axis=0, concat_axis=1, tiled=True)
    summed = lax.psum(columns, "hg")
    hidden = residual.astype(jnp.float32) + summed
    inverse = lax.rsqrt(jnp.mean(hidden * hidden, axis=-1, keepdims=True) + EPS)
    normed = (hidden * inverse * norm_gain.astype(jnp.float32)[None, :]).astype(jnp.bfloat16)
    local_experts = w_gate.shape[0]
    experts_all = local_experts * groups
    topk = routes.shape[1]
    capacity = min(tok_rows, max(2, tok_rows * topk * 2 // experts_all))
    expert_ids = jnp.arange(experts_all, dtype=jnp.int32)
    hits = (routes[:, :, None] == expert_ids[None, None, :]).astype(jnp.int32)
    named = jnp.sum(hits, axis=1)
    before = jnp.cumsum(named, axis=0) - named
    gates = gate_int.astype(jnp.float32)
    gates = gates / jnp.sum(gates, axis=1, keepdims=True)
    share = jnp.sum(hits.astype(jnp.float32) * gates[:, :, None], axis=1)
    slot_ids = jnp.arange(capacity, dtype=jnp.int32)
    place = (named[:, :, None] == 1) & (before[:, :, None] == slot_ids[None, None, :])
    select = jnp.transpose(place, (1, 2, 0)).astype(jnp.bfloat16)
    outgoing = jnp.einsum("ect,td->ecd", select, normed, preferred_element_type=jnp.float32).astype(
        jnp.bfloat16
    )
    outgoing = outgoing.reshape(groups, local_experts, capacity, width)
    copies_out = jnp.broadcast_to(outgoing[:, None], (groups, sides) + outgoing.shape[1:])
    copies_out = copies_out.reshape((groups * sides,) + outgoing.shape[1:])
    incoming = lax.all_to_all(copies_out, ("grp", "side"), split_axis=0, concat_axis=0, tiled=True)
    incoming = incoming.reshape((groups, sides) + outgoing.shape[1:])
    gate = jnp.einsum("gsjcd,jdf->gsjcf", incoming, w_gate, preferred_element_type=jnp.float32)
    up = jnp.einsum("gsjcd,jdf->gsjcf", incoming, w_up, preferred_element_type=jnp.float32)
    act = (jax.nn.silu(gate) * up).astype(jnp.bfloat16)
    expert_rows = jnp.einsum("gsjcf,jfd->gsjcd", act, w_down, preferred_element_type=jnp.float32)
    quarter = width // hg_count
    pieces = expert_rows.reshape(groups * sides, local_experts, capacity, hg_count, quarter)
    back = lax.all_to_all(
        lax.all_to_all(pieces, "hg", split_axis=3, concat_axis=3, tiled=True),
        ("grp", "side"),
        split_axis=0,
        concat_axis=0,
        tiled=True,
    )
    back = back.reshape(groups, sides, local_experts, capacity, hg_count, quarter)
    expert_out = jnp.sum(back, axis=(1, 4)).reshape(experts_all, capacity, quarter)
    slot_weight = place.astype(jnp.float32) * share[:, :, None]
    moe = ROUTE_SCALE * jnp.dot(
        slot_weight.reshape(tok_rows, experts_all * capacity),
        expert_out.reshape(experts_all * capacity, quarter),
        precision=lax.Precision.HIGHEST,
    )
    mine = lax.dynamic_slice_in_dim(hidden, lax.axis_index("hg") * quarter, quarter, 1)
    return (mine + moe).astype(jnp.bfloat16)


def solution(mesh):
    in_specs = (
        P(("grp", "side"), "hg"),
        P(("grp", "side"), "hg"),
        P("hg", None, None),
        P(("grp", "side"), None, None),
        P(("grp", "side"), None, None),
        P(("grp", "side")),
        P("hg", None, None),
        P("hg", ("grp", "side")),
        P(("grp", "side"), None),
        P(),
        P(("grp", "side"), None),
        P(("grp", "side"), None),
        P("grp", None, ("hg", "side")),
        P("grp", None, ("hg", "side")),
        P("grp", ("hg", "side"), None),
    )
    out_specs = P(("grp", "side"), "hg")
    return jax.shard_map(body, mesh=mesh, in_specs=in_specs, out_specs=out_specs, check_vma=False)
```

profile of v0, /device:TPU:0, one launch (start us, length us, event | category | flops | bytes accessed | tf_op | source)
XLA Modules:
  0.0 299.6 jit_solution(11541106606884350940)
XLA Ops:
  6.5 1.6 copy-done
  8.1 1.1 fusion.31
  9.2 0.7 broadcast_add_fusion
  9.9 0.1 iota_add_fusion
  10.0 0.1 iota_compare_fusion
  10.1 0.8 reshape.130
  10.9 6.0 %fusion.3 = f32[2,2,16,4096]{3,2,1,0:T(8,128)S(1)} fusion(bf16[2,2,16,512]{3,2,1,0:T(8,128)(2,1)S(1)} %bitcast.90, bf16[2,4096,512]{2,1,0:T(8,128)(2,1)} %param.18), kind=kOutput, calls=%fused_computation.4 | convolution fusion | flops 268435456 | bytes 9502720 | tf_op jit(solution)/shard_map/rqhc,rpc->rqhp/dot_general | solution.py:49
  16.9 0.3 fusion.7
  17.2 0.3 fusion.69
  17.5 5.0 %fusion.18 = bf16[2,2,16,512]{3,2,1,0:T(8,128)(2,1)S(1)} fusion(bf16[2,4096,512]{2,1,0:T(8,128)(2,1)} %param.18, f32[2,2,16]{2,1,0:T(2,128)S(1)} %fusion.69, f32[2,2,16,4096]{3,2,1,0:T(8,128)S(1)} %fusion.7), kind=kOutput, calls=%fused_computation.23 | convolution fusion | flops 269258816 | bytes 9502976 | tf_op jit(solution)/shard_map/rqhp,rpc->rqhc/dot_general | solution.py:63
  22.6 0.0 copy-start.5
  22.6 2.0 fusion.42
  24.6 45.0 %all-gather = bf16[32,4,2048]{2,1,0:T(4,128)(2,1)S(1)} all-gather(bf16[1,4,2048]{2,1,0:T(4,128)(2,1)S(1)} %fusion.42), channel_id=1, replica_groups=mesh['hg'=4,'grp'=8,'side'=4] {'grp','side'}, dimensions={0}, use_global_device_ids=true | all-gather | bytes 540672 | tf_op jit(solution)/shard_map/all_gather | solution.py:72
  69.6 0.1 reshape.137
  69.8 1.6 fusion.70
  71.4 0.7 all_to_all.23
  72.1 5.3 %all-to-all-start = ((f32[32,4,224]{2,1,0:T(4,128)}), f32[32,4,224]{2,1,0:T(4,128)S(1)}, u32[]{:S(2)}, u32[]{:S(2)}) async-start(f32[32,4,224]{2,1,0:T(4,128)} %all_to_all.23), calls=%async_computation | async-start | bytes 262144 | tf_op jit(solution)/shard_map/all_to_all | solution.py:76
  77.4 0.0 all-reduce.2.cloned.1.call-start
  77.4 0.1 convert_reduce_fusion
  77.6 7.6 %all-to-all-done = f32[32,4,224]{2,1,0:T(4,128)S(1)} async-done(((f32[32,4,224]{2,1,0:T(4,128)}), f32[32,4,224]{2,1,0:T(4,128)S(1)}, u32[]{:S(2)}, u32[]{:S(2)}) %all-to-all-start) | async-done | bytes 114720 | tf_op jit(solution)/shard_map/all_to_all | solution.py:76
  85.3 0.8 all_to_all.26
  86.0 0.0 all-reduce.2.cloned.1.call-update
  86.1 38.4 %all-reduce.2.cloned.1.call-done = f32[4,7168]{1,0:T(4,128)} async-done(((f32[4,7168]{1,0:T(4,128)}), f32[4,7168]{1,0:T(4,128)}) %all-reduce.2.cloned.1.call-update) | async-done | bytes 114704 | tf_op jit(solution)/shard_map/psum | solution.py:77
  124.5 1.1 multiply_reduce_fusion
  125.6 0.4 convolution_convert_fusion
  126.0 0.5 copy.95
  126.4 1.1 broadcast_in_dim.19
  127.5 32.7 %all_to_all.34 = bf16[32,2,2,7168]{3,2,1,0:T(2,128)(2,1)S(1)} all-to-all(bf16[32,2,2,7168]{3,2,1,0:T(2,128)(2,1)S(1)} %bitcast.87), channel_id=1, replica_groups=mesh['hg'=4,'grp'=8,'side'=4] {'grp','side'}, dimensions={0} | all-to-all | bytes 3670016 | tf_op jit(solution)/shard_map/all_to_all | solution.py:101
  160.3 1.3 copy-done.1
  161.5 1.3 fusion.21
  162.8 7.2 %convolution_bitcast_fusion = f32[8,4,2,2,7168]{4,0,3,1,2:T(8,128)} fusion(bf16[2,128,7168]{2,1,0:T(8,128)(2,1)} %param.29, bf16[2,7168,128]{2,1,0:T(8,128)(2,1)} %param.28, bf16[8,4,2,2,7168]{4,3,2,1,0:T(2,128)(2,1)} %bitcast.86, f32[8,4,2,2,128]{4,0,3,1,2:T(8,128)S(1)} %fusion.21), kind=kOutput, calls=%fused_computation.1 | convolution fusion | flops 469860352 | bytes 12910592 | tf_op jit(solution)/shard_map/gsjcf,jfd->gsjcd/dot_general | solution.py:106
  170.0 6.7 %copy.83 = f32[8,4,2,2,7168]{4,3,2,1,0:T(2,128)} copy(f32[8,4,2,2,7168]{4,0,3,1,2:T(8,128)} %convolution_bitcast_fusion) | data formatting | bytes 7340032 | tf_op jit(solution)/shard_map/gsjcf,jfd->gsjcd/transpose | solution.py:106
  176.7 6.3 %reshape.135 = f32[32,2,2,4,1792]{4,3,2,1,0:T(4,128)} reshape(f32[8,4,2,2,7168]{4,3,2,1,0:T(2,128)} %copy.83) | data formatting | bytes 7340032 | tf_op jit(solution)/shard_map/reshape | solution.py:108
  183.1 3.9 %copy.84 = f32[32,2,2,4,1792]{4,2,1,0,3:T(2,128)S(1)} copy(f32[32,2,2,4,1792]{4,3,2,1,0:T(4,128)} %reshape.135) | data formatting | bytes 7340032 | tf_op jit(solution)/shard_map/reshape | solution.py:108
  187.0 46.0 %all_to_all.35 = f32[32,2,2,4,1792]{4,2,1,0,3:T(2,128)S(1)} all-to-all(f32[32,2,2,4,1792]{4,2,1,0,3:T(2,128)S(1)} %copy.84), channel_id=1, replica_groups=mesh['hg'=4,'grp'=8,'side'=4] {'hg'}, dimensions={3} | all-to-all | bytes 7340032 | tf_op jit(solution)/shard_map/all_to_all | solution.py:110
  233.0 4.0 %copy.85 = f32[32,2,2,4,1792]{4,2,1,3,0:T(2,128)} copy(f32[32,2,2,4,1792]{4,2,1,0,3:T(2,128)S(1)} %all_to_all.35) | data formatting | bytes 7340032 | tf_op jit(solution)/shard_map/all_to_all | solution.py:110
  237.0 5.2 %all-to-all-start.3 = ((f32[32,2,2,4,1792]{4,2,1,3,0:T(2,128)}), f32[32,2,2,4,1792]{4,2,1,3,0:T(2,128)}, u32[]{:S(2)}, u32[]{:S(2)}) async-start(f32[32,2,2,4,1792]{4,2,1,3,0:T(2,128)} %copy.85), calls=%async_computation.3 | async-start | bytes 7340032 | tf_op jit(solution)/shard_map/all_to_all | solution.py:109
  242.2 0.1 copy.78
  242.3 0.1 copy.77
  242.4 0.1 convert_reduce_fusion.1
  242.5 0.1 convert_divide_fusion
  242.6 0.1 fusion.62
  242.7 0.1 copy.79
  242.8 44.6 %all-to-all-done.3 = f32[32,2,2,4,1792]{4,2,1,3,0:T(2,128)} async-done(((f32[32,2,2,4,1792]{4,2,1,3,0:T(2,128)}), f32[32,2,2,4,1792]{4,2,1,3,0:T(2,128)}, u32[]{:S(2)}, u32[]{:S(2)}) %all-to-all-start.3) | async-done | bytes 3670048 | tf_op jit(solution)/shard_map/all_to_all | solution.py:109
  287.4 4.1 %reduce_sum.66 = f32[32,2,2,1792]{3,2,1,0:T(2,128)S(1)} reduce(f32[32,2,2,4,1792]{4,2,1,3,0:T(2,128)} %all-to-all-done.3, f32[]{:T(128)} %constant.10.clone.1), dimensions={3}, to_apply=%region_8.9 | reduce | flops 688128 | bytes 4587524 | tf_op jit(solution)/shard_map/reduce_sum | solution.py:117
  291.5 0.3 bitcast_reduce_fusion
  291.7 0.2 reshape_reshape.3
  291.9 0.9 fusion.15
  (22 shorter events, 0.2 us)
Async XLA Ops:
  6.5 1.6 copy-start
  10.9 6.0 %copy-start.2 = (bf16[2,64,4096]{2,1,0:T(8,128)(2,1)S(1)}, bf16[2,64,4096]{2,1,0:T(8,128)(2,1)}, u32[]{:S(2)}) copy-start(bf16[2,64,4096]{2,1,0:T(8,128)(2,1)} %param.19) | copy-start | bytes 3145732
  22.6 54.9 %copy-start.5 = (s32[4,4]{1,0:T(4,128)S(1)}, s32[4,4]{1,0:T(4,128)}, u32[]{:S(2)}) copy-start(s32[4,4]{1,0:T(4,128)} %param.25) | copy-start | bytes 196
  22.6 55.0 %copy-start.4 = (bf16[7168]{0:T(1024)(128)(2,1)S(1)}, bf16[7168]{0:T(1024)(128)(2,1)}, u32[]{:S(2)}) copy-start(bf16[7168]{0:T(1024)(128)(2,1)} %param.24) | copy-start | bytes 43012
  22.6 101.9 %copy-start.3 = (bf16[4,7168]{1,0:T(4,128)(2,1)S(1)}, bf16[4,7168]{1,0:T(4,128)(2,1)}, u32[]{:S(2)}) copy-start(bf16[4,7168]{1,0:T(4,128)(2,1)} %param.23) | copy-start | bytes 172036
  72.1 13.1 %all-to-all-start = ((f32[32,4,224]{2,1,0:T(4,128)}), f32[32,4,224]{2,1,0:T(4,128)S(1)}, u32[]{:S(2)}, u32[]{:S(2)}) async-start(f32[32,4,224]{2,1,0:T(4,128)} %all_to_all.23), calls=%async_computation | async-start | bytes 262144 | tf_op jit(solution)/shard_map/all_to_all | solution.py:76
  77.4 47.1 %all-reduce.2.cloned.1.call-start = ((), (), s32[]{:S(2)}) async-start(), calls=%async_computation.4 | async-start | bytes 229376 | tf_op jit(solution)/shard_map/psum | solution.py:77
  125.6 35.9 %copy-start.7 = (bf16[2,7168,128]{2,1,0:T(8,128)(2,1)S(1)}, bf16[2,7168,128]{2,1,0:T(8,128)(2,1)}, u32[]{:S(2)}) copy-start(bf16[2,7168,128]{2,1,0:T(8,128)(2,1)} %param.27) | copy-start | bytes 11010052
  160.2 1.3 copy-start.1
  237.0 5.4 %copy-start.6 = (s32[4,4]{1,0:T(4,128)S(1)}, s32[4,4]{1,0:T(4,128)}, u32[]{:S(2)}) copy-start(s32[4,4]{1,0:T(4,128)} %param.26) | copy-start | bytes 196
  237.0 50.4 %all-to-all-start.3 = ((f32[32,2,2,4,1792]{4,2,1,3,0:T(2,128)}), f32[32,2,2,4,1792]{4,2,1,3,0:T(2,128)}, u32[]{:S(2)}, u32[]{:S(2)}) async-start(f32[32,2,2,4,1792]{4,2,1,3,0:T(2,128)} %copy.85), calls=%async_computation.3 | async-start | bytes 7340032 | tf_op jit(solution)/shard_map/all_to_all | solution.py:109
Sparse Core Ops, SparseCore 0:
  86.2 38.2 all-reduce.1
where the time goes:
time: 301 us; the launch traced here: 300 us
  blocking collectives  124 us (41%)
  waiting for transfers between devices  90.6 us (30%)
  local copies, waits for them, and re-layouts  28.2 us (9%)
  matrix products  25.8 us (9%)
  between operations  13.6 us (5%)
  starting transfers between devices  10.5 us (3%)
  other arithmetic  7.03 us (2%)
    all_to_all x1, blocking collectives, body(): lax.all_to_all(pieces, 'hg', split_axis=3, concat_axis=3, tiled=True)  46 us
    all_gather x1, blocking collectives, body(): lax.all_gather(values, ('grp', 'side'), axis=0, tiled=True)  45 us
    all_to_all x1, waiting for transfers between devices, body(): lax.all_to_all(lax.all_to_all(pieces, 'hg', split_axis=3, concat_axis=3,...  44.6 us
    psum x1, waiting for transfers between devices, body(): summed = lax.psum(columns, 'hg')  38.4 us
    all_to_all x1, blocking collectives, body(): lax.all_to_all(copies_out, ('grp', 'side'), split_axis=0, concat_axis=0,...  32.7 us
    reshape x2, local copies, waits for them, and re-layouts, body(): expert_rows.reshape(groups * sides, local_experts, capacity, hg_count, qu...  10.2 us
    all_to_all x1, waiting for transfers between devices, body(): lax.all_to_all(partial_cols, ('grp', 'side'), split_axis=0, concat_axis=1...  7.63 us
    dot_general x1, matrix products, body(): jnp.einsum('gsjcf,jfd->gsjcd', act, w_down, preferred_element_type=jnp.fl...  7.22 us
  transfers between devices with their start and end apart: 3, of which 3 were waited for; matrix products, arithmetic and copies ran while one was open for 0% of the time, Pallas kernels for 0%

commit v1 on v0

v1 whole, which is shorter than its diff:
```python
import jax
import jax.numpy as jnp
from jax import lax
from jax.experimental import pallas as pl
from jax.experimental.pallas import tpu as pltpu
from jax.sharding import Mesh
from jax.sharding import PartitionSpec as P

LAT = 512
ROPE = 64
NOPE = 128
VDIM = 128
QPR = 2
LEN = 4096
EPS = 1e-06
ROUTE_SCALE = 2.5
BF = jnp.bfloat16
F32 = jnp.float32

PAIRS_A = [(0, 1), (1, 0), (2, 3), (3, 2)]
PAIRS_B = [(1, 2), (2, 1), (3, 0), (0, 3)]
SWAP = [(0, 1), (1, 0)]


def attention(q_nope, q_rope, w_absorb, cache_latent, cache_rope, lengths, w_value):
    heads = w_absorb.shape[0]
    tok_rows = q_nope.shape[0]
    requests = cache_latent.shape[0]
    query = q_nope.reshape(tok_rows, heads, NOPE)
    q_latent = jnp.einsum("thn,hnc->thc", query, w_absorb, preferred_element_type=F32).astype(BF)
    q_latent = q_latent.reshape(requests, QPR, heads, LAT)
    q_pos = q_rope.reshape(requests, QPR, heads, ROPE)
    scale = (NOPE + ROPE) ** (-0.5)
    scores = jnp.einsum("rqhc,rpc->rqhp", q_latent, cache_latent, preferred_element_type=F32)
    scores = scores + jnp.einsum("rqhe,rep->rqhp", q_pos, cache_rope, preferred_element_type=F32)
    scores = scores * scale
    position = jnp.arange(LEN, dtype=jnp.int32)
    limit = lengths[:, None] - QPR + jnp.arange(QPR, dtype=jnp.int32)[None, :]
    valid = position[None, None, None, :] <= limit[:, :, None, None]
    scores = jnp.where(valid, scores, -jnp.inf)
    top = jnp.max(scores, axis=-1, keepdims=True)
    weights = jnp.exp(scores - top)
    probs = (weights / jnp.sum(weights, axis=-1, keepdims=True)).astype(BF)
    latent_out = jnp.einsum("rqhp,rpc->rqhc", probs, cache_latent, preferred_element_type=F32).astype(BF)
    latent_out = latent_out.reshape(tok_rows, heads, LAT)
    values = jnp.einsum("thc,hcv->thv", latent_out, w_value, preferred_element_type=F32).astype(BF)
    return values.reshape(tok_rows, heads * VDIM)


def ffn_kernel(own_ref, oth_ref, gain_ref, share_ref, wg_hbm, wu_hbm, wd_hbm, keep_ref, send_ref,
               wgu, wd, sem_up, sem_down):
    experts, depth, units = wg_hbm.shape
    blocks, rows, cols = own_ref.shape
    sides = 4
    ys = blocks // sides
    stripe = depth // ys
    half = rows // 2
    core = lax.axis_index("c")
    copies = []
    for y in range(ys):
        group = []
        for e in range(experts):
            for k, src in enumerate((wg_hbm, wu_hbm)):
                group.append(pltpu.make_async_copy(
                    src.at[e, pl.ds(y * stripe, stripe), :],
                    wgu.at[e, pl.ds(y * stripe, stripe), pl.ds(k * units, units)],
                    sem_up.at[(y * experts + e) * 2 + k],
                ))
        copies.append(group)
    downs = [
        pltpu.make_async_copy(wd_hbm.at[e], wd.at[pl.ds(e * units, units), :], sem_down.at[e])
        for e in range(experts)
    ]
    for group in copies:
        for copy in group:
            copy.start()
    for copy in downs:
        copy.start()
    acc = [jnp.zeros((rows, 2 * units), F32) for _ in range(experts)]
    square = jnp.zeros((rows, cols), F32)
    for y in range(ys):
        for copy in copies[y]:
            copy.wait()
        for other in range(2):
            part = core if other == 0 else 1 - core
            for s in range(sides):
                if other == 0:
                    block = own_ref[y * sides + s].astype(F32)
                else:
                    block = oth_ref[y * sides + s].astype(F32)
                    block = jnp.concatenate([block[half:], block[:half]], axis=0)
                square = square + block * block
                scaled = (block * gain_ref[y * 2 + part, pl.ds(s, 1), :]).astype(BF)
                start = pl.multiple_of(y * stripe + part * (stripe // 2) + s * cols, 16)
                for e in range(experts):
                    acc[e] = acc[e] + jnp.dot(scaled, wgu[e, pl.ds(start, cols), :], preferred_element_type=F32)
    inverse = lax.rsqrt(jnp.sum(square, axis=-1, keepdims=True) / depth + EPS)
    acts = []
    for e in range(experts):
        both = acc[e] * inverse
        gate, up = both[:, :units], both[:, units:]
        share = share_ref[:, e:e + 1]
        act = gate / (1.0 + jnp.exp(-gate)) * up
        acts.append(jnp.where(share > 0, act * share, 0.0).astype(BF))
    act = jnp.concatenate(acts, axis=1)
    for copy in downs:
        copy.wait()
    tile = 1024
    for n in range(depth // tile):
        out = jnp.dot(act, wd[:, n * tile:(n + 1) * tile], preferred_element_type=F32).astype(BF)
        keep_ref[:, n * tile:(n + 1) * tile] = out[:half]
        send_ref[:, n * tile:(n + 1) * tile] = out[half:]


def ffn(own, oth, gain, share, w_gate, w_up, w_down):
    experts, depth, units = w_gate.shape
    rows = own.shape[1]
    shape = jax.ShapeDtypeStruct((rows // 2, depth), BF)
    return pl.pallas_call(
        ffn_kernel,
        out_shape=(shape, shape),
        in_specs=[pl.BlockSpec(memory_space=pltpu.VMEM)] * 4 + [pl.BlockSpec(memory_space=pl.ANY)] * 3,
        out_specs=[pl.BlockSpec(memory_space=pltpu.VMEM)] * 2,
        scratch_shapes=[
            pltpu.VMEM((experts, depth, 2 * units), BF),
            pltpu.VMEM((experts * units, depth), BF),
            pltpu.SemaphoreType.DMA((16,)),
            pltpu.SemaphoreType.DMA((2,)),
        ],
        compiler_params=pltpu.CompilerParams(vmem_limit_bytes=40 * 1024 * 1024),
        cost_estimate=pl.CostEstimate(flops=2 * rows * depth * 768, bytes_accessed=15_000_000, transcendentals=0),
    )(own, oth, gain, share, w_gate, w_up, w_down)


def body(
    q_nope, q_rope, w_absorb, cache_latent, cache_rope, lengths, w_value, w_out, residual, norm_gain,
    routes, gate_int, w_gate, w_up, w_down,
):
    hgs, ys, cores, sides = (lax.axis_size(a) for a in ("hg", "y", "c", "side"))
    hg, y, core, side = (lax.axis_index(a) for a in ("hg", "y", "c", "side"))
    planes = ys * sides
    toks, width = residual.shape
    cols = w_out.shape[1]
    local_experts = w_gate.shape[0]
    experts_all = local_experts * ys * cores

    values = attention(q_nope, q_rope, w_absorb, cache_latent, cache_rope, lengths, w_value)

    expert_ids = jnp.arange(experts_all, dtype=jnp.int32)
    hits = routes[:, :, None] == expert_ids[None, None, :]
    dense = jnp.sum(jnp.where(hits, gate_int[:, :, None], 0), axis=1).astype(BF)
    row = lax.dynamic_slice_in_dim(residual, hg, 1, 0)
    row = row.reshape(ys, cores, sides, cols).transpose(0, 2, 1, 3).reshape(planes, cores * 2, cols // 2)
    message = jnp.concatenate(
        [
            jnp.broadcast_to(values[None], (planes,) + values.shape),
            row,
            jnp.broadcast_to(dense[None], (planes,) + dense.shape),
        ],
        axis=2,
    )
    here = lax.all_to_all(message, ("y", "side"), 0, 0, tiled=True)
    there = lax.ppermute(here, "c", SWAP)
    both = jnp.stack([here, there])
    n_val = values.shape[1]
    all_values = both[..., :n_val].reshape(cores * planes * toks, n_val)
    extra = both[..., n_val:]
    mine = lax.dynamic_slice_in_dim(extra[..., :cols // 2], core * 2, 2, 2).reshape(cores * planes, 1, cols)
    gates = extra[..., cols // 2:].reshape(cores * planes * toks, experts_all).astype(F32)
    total = jnp.sum(gates, axis=1, keepdims=True)
    first = (y * cores + core) * local_experts
    share = lax.dynamic_slice_in_dim(gates, first, local_experts, 1) * (ROUTE_SCALE / total)

    partial = jnp.dot(all_values, w_out, preferred_element_type=F32).reshape(cores * planes, toks, cols)
    is_row = (jnp.arange(toks) == hg)[None, :, None]
    partial = (partial + jnp.where(is_row, mine.astype(F32), 0.0)).astype(BF).reshape(-1, cols)
    pair = (partial.astype(F32) + lax.ppermute(partial, "hg", PAIRS_A).astype(F32)).astype(BF)
    hidden = (pair.astype(F32) + lax.ppermute(pair, "hg", PAIRS_B).astype(F32)).astype(BF)

    own = lax.all_to_all(jnp.broadcast_to(hidden[None], (planes,) + hidden.shape), ("y", "side"), 0, 0, tiled=True)
    oth = lax.ppermute(own, "c", SWAP)
    gain = norm_gain.astype(F32).reshape(ys * cores, sides, cols)
    keep, send = ffn(own, oth, gain, share, w_gate, w_up, w_down)
    got = lax.ppermute(send, "c", SWAP)
    quarter = width // hgs
    summed = (keep.astype(F32) + got.astype(F32)).astype(BF)
    summed = summed.reshape(planes, toks, hgs, quarter).transpose(2, 0, 1, 3).reshape(hgs * planes, toks, quarter)
    parts = lax.all_to_all(summed, ("hg", "y", "side"), 0, 0, tiled=True)

    at = (y * sides + side) * toks
    half = planes * toks
    first_half = lax.dynamic_slice(own, (hg * sides, at, 0), (sides, toks, cols))
    second_half = lax.dynamic_slice(oth, (hg * sides, half + at, 0), (sides, toks, cols))
    low = jnp.where(core == 0, first_half, second_half)
    high = jnp.where(core == 0, second_half, first_half)
    kept = jnp.concatenate([low, high], axis=0).transpose(1, 0, 2).reshape(toks, quarter)
    return (kept.astype(F32) + jnp.sum(parts.astype(F32), axis=0)).astype(BF)


def solution(mesh):
    devices = mesh.devices
    fine = Mesh(devices.reshape(4, 4, 2, 4), ("hg", "y", "c", "side"))
    grp = ("y", "c")
    plane = ("y", "c", "side")
    in_specs = (
        P(plane, "hg"),
        P(plane, "hg"),
        P("hg", None, None),
        P(plane, None, None),
        P(plane, None, None),
        P(plane),
        P("hg", None, None),
        P("hg", plane),
        P(plane, None),
        P(),
        P(plane, None),
        P(plane, None),
        P(grp, None, ("hg", "side")),
        P(grp, None, ("hg", "side")),
        P(grp, ("hg", "side"), None),
    )
    return jax.shard_map(body, mesh=fine, in_specs=in_specs, out_specs=P(plane, "hg"), check_vma=False)
```

time: 301 us -> 115 us (0.38)
  blocking collectives: 124 us -> 33.6 us
  waiting for transfers between devices: 90.6 us -> 26 us
  between operations: 13.6 us -> 0.27 us
  local copies, waits for them, and re-layouts: 28.2 us -> 16.8 us
  matrix products: 25.8 us -> 16 us
  Pallas kernels: 0 us -> 4.13 us
    all_to_all x2, blocking collectives: 78.8 us -> 33.6 us  [the longest x1 17 us: body(): lax.all_to_all(jnp.broadcast_to(hidden[None], (planes,) + hidden.shape),...]
    all_gather x1 -> x0, blocking collectives: 45 us -> none  [body(): lax.all_gather(values, ('grp', 'side'), axis=0, tiled=True)]
    psum x1 -> x0, waiting for transfers between devices: 38.4 us -> none  [body(): summed = lax.psum(columns, 'hg')]
    all_to_all x2 -> x1, waiting for transfers between devices: 52.2 us -> 15.8 us  [body(): parts = lax.all_to_all(summed, ('hg', 'y', 'side'), 0, 0, tiled=True)]
    ppermute x0 -> x5, waiting for transfers between devices: none -> 10.2 us  [the longest x1 2.78 us: body(): lax.ppermute(partial, 'hg', PAIRS_A).astype(F32)]
    dot_general x10 -> x6, matrix products: 25.8 us -> 16 us  [the longest x1 5.99 us: attention(): jnp.einsum('rqhc,rpc->rqhp', q_latent, cache_latent, preferred_element_ty...]
    transpose x1, local copies, waits for them, and re-layouts: 6.7 us -> 0.02 us  [body(): row.reshape(ys, cores, sides, cols).transpose(0, 2, 1, 3)]
    reshape x4 -> x9, local copies, waits for them, and re-layouts: 11 us -> 5.19 us  [the longest x3 4.06 us: body(): summed.reshape(planes, toks, hgs, quarter).transpose(2, 0, 1, 3)]
  transfers between devices with their start and end apart: 3 -> 6, of which waited for: 3 -> 6; matrix products, arithmetic and copies ran while one was open for 0% -> 3% of each run, Pallas kernels for 0% -> 0%
where the time goes in v1:
time: 115 us
  blocking collectives  33.6 us (29%)
  waiting for transfers between devices  26 us (23%)
  local copies, waits for them, and re-layouts  16.8 us (15%)
  matrix products  16 us (14%)
  starting transfers between devices  11.6 us (10%)
  other arithmetic  6.27 us (5%)
  Pallas kernels  4.13 us (4%)
    all_to_all x1, blocking collectives, body(): lax.all_to_all(jnp.broadcast_to(hidden[None], (planes,) + hidden.shape),...  17 us
    all_to_all x1, blocking collectives, body(): here = lax.all_to_all(message, ('y', 'side'), 0, 0, tiled=True)  16.6 us
    all_to_all x1, waiting for transfers between devices, body(): parts = lax.all_to_all(summed, ('hg', 'y', 'side'), 0, 0, tiled=True)  15.8 us
    all_to_all x1, starting transfers between devices, body(): parts = lax.all_to_all(summed, ('hg', 'y', 'side'), 0, 0, tiled=True)  6.84 us
    dot_general x1, matrix products, attention(): jnp.einsum('rqhc,rpc->rqhp', q_latent, cache_latent, preferred_element_ty...  5.99 us
    unnamed x12, local copies, waits for them, and re-layouts  5.32 us
    dot_general x1, matrix products, attention(): jnp.einsum('rqhp,rpc->rqhc', probs, cache_latent, preferred_element_type=...  5.02 us
    pallas_call x1, Pallas kernels, ffn(): pl.pallas_call(ffn_kernel, out_shape=(shape, shape), in_specs=[pl.BlockSp...  4.13 us
  transfers between devices with their start and end apart: 6, of which 6 were waited for; matrix products, arithmetic and copies ran while one was open for 3% of the time, Pallas kernels for 0%

profile of v1, /device:TPU:0, one launch (start us, length us, event | category | flops | bytes accessed | tf_op | source)
XLA Modules:
  0.0 114.7 jit_solution(14228321235283015134)
XLA Ops:
  0.0 0.8 broadcast_add_fusion
  0.9 0.8 select_reduce_fusion
  1.7 0.9 dynamic-slice_reduce_fusion
  2.8 0.8 reshape.106
  3.6 0.1 iota_compare_fusion
  3.7 1.1 fusion.13
  4.8 6.0 %fusion.3 = f32[2,2,16,4096]{3,2,1,0:T(8,128)S(1)} fusion(bf16[2,2,16,512]{3,2,1,0:T(8,128)(2,1)S(1)} %bitcast.53, bf16[2,4096,512]{2,1,0:T(8,128)(2,1)} %param.18), kind=kOutput, calls=%fused_computation.3 | convolution fusion | flops 268435456 | bytes 9502720 | tf_op jit(solution)/shard_map/rqhc,rpc->rqhp/dot_general | solution.py:34
  10.8 0.3 fusion.7
  11.2 0.3 fusion.26
  11.5 5.0 %fusion.10 = bf16[2,2,16,512]{3,2,1,0:T(8,128)(2,1)S(1)} fusion(bf16[2,4096,512]{2,1,0:T(8,128)(2,1)} %param.18, f32[2,2,16]{2,1,0:T(2,128)S(1)} %fusion.26, f32[2,2,16,4096]{3,2,1,0:T(8,128)S(1)} %fusion.7), kind=kOutput, calls=%fused_computation.15 | convolution fusion | flops 269258816 | bytes 9502976 | tf_op jit(solution)/shard_map/rqhp,rpc->rqhc/dot_general | solution.py:44
  16.5 2.0 %fusion.14 = bf16[4,2048]{1,0:T(4,128)(2,1)S(1)} fusion(bf16[16,512,128]{2,1,0:T(8,128)(2,1)} %param.21, bf16[4,16,512]{2,1,0:T(8,128)(2,1)S(1)} %bitcast.55), kind=kOutput, calls=%fused_computation.18 | convolution fusion | flops 8396800 | bytes 2179072 | tf_op jit(solution)/shard_map/thc,hcv->thv/dot_general | solution.py:46
  18.6 0.3 concatenate.6
  19.0 16.6 %all_to_all.15 = bf16[16,4,2176]{2,1,0:T(4,128)(2,1)S(1)} all-to-all(bf16[16,4,2176]{2,1,0:T(4,128)(2,1)S(1)} %concatenate.6), channel_id=1, replica_groups=mesh['hg'=4,'y'=4,'c'=2,'side'=4] {'y','side'}, dimensions={0} | all-to-all | bytes 557056 | tf_op jit(solution)/shard_map/all_to_all | solution.py:162
  35.6 1.5 %collective-permute-done = bf16[16,4,2176]{2,1,0:T(4,128)(2,1)S(1)} collective-permute-done((bf16[16,4,2176]{2,1,0:T(4,128)(2,1)S(1)}, bf16[16,4,2176]{2,1,0:T(4,128)(2,1)S(1)}, u32[]{:S(2)}, u32[]{:S(2)}) %collective-permute-start) | collective-permute-done | bytes 278560 | tf_op jit(solution)/shard_map/ppermute | solution.py:163
  37.2 0.4 fusion.17
  37.7 0.3 copy.64
  38.0 1.6 %fusion.9 = bf16[32,4,224]{2,0,1:T(8,128)(2,1)S(1)} fusion(bf16[32,4,2048]{2,0,1:T(8,128)(2,1)S(1)} %bitcast.52, bf16[2048,224]{0,1:T(8,128)(2,1)} %param.22, f32[32,224]{1,0:T(8,128)S(1)} %reshape.115, pred[4]{0:T(512)(128)(4,1)S(1)} %iota_compare_fusion.2), kind=kOutput, calls=%fused_computation.13 | convolution fusion | flops 117526528 | bytes 1527812 | tf_op jit(solution)/shard_map/dot_general | solution.py:174
  39.7 1.6 %collective-permute-start.1 = (bf16[128,224]{1,0:T(8,128)(2,1)S(1)}, bf16[128,224]{1,0:T(8,128)(2,1)S(1)}, u32[]{:S(2)}, u32[]{:S(2)}) collective-permute-start(bf16[128,224]{1,0:T(8,128)(2,1)S(1)} %reshape.110), channel_id=1, source_target_pairs={{0,32},{32,0},{64,96},{96,64},{1,33},{33,1},{65,97},{97,65},{2,34}... | collective-permute-start | bytes 172040 | tf_op jit(solution)/shard_map/ppermute | solution.py:177
  41.3 2.8 %collective-permute-done.1 = bf16[128,224]{1,0:T(8,128)(2,1)S(1)} collective-permute-done((bf16[128,224]{1,0:T(8,128)(2,1)S(1)}, bf16[128,224]{1,0:T(8,128)(2,1)S(1)}, u32[]{:S(2)}, u32[]{:S(2)}) %collective-permute-start.1) | collective-permute-done | bytes 57376 | tf_op jit(solution)/shard_map/ppermute | solution.py:177
  44.1 2.8 %collective-permute-start.2 = (bf16[128,224]{1,0:T(8,128)(2,1)S(1)}, bf16[128,224]{1,0:T(8,128)(2,1)S(1)}, u32[]{:S(2)}, u32[]{:S(2)}) collective-permute-start(bf16[128,224]{1,0:T(8,128)(2,1)S(1)} %add_convert_fusion.2), channel_id=1, source_target_pairs={{32,64},{64,32},{96,0},{0,96},{33,65},{65,33},{97,1},{1,97},{34,66... | collective-permute-start | bytes 172040 | tf_op jit(solution)/shard_map/ppermute | solution.py:178
  46.9 2.7 %collective-permute-done.2 = bf16[128,224]{1,0:T(8,128)(2,1)S(1)} collective-permute-done((bf16[128,224]{1,0:T(8,128)(2,1)S(1)}, bf16[128,224]{1,0:T(8,128)(2,1)S(1)}, u32[]{:S(2)}, u32[]{:S(2)}) %collective-permute-start.2) | collective-permute-done | bytes 57376 | tf_op jit(solution)/shard_map/ppermute | solution.py:178
  49.7 0.1 copy.66
  49.8 0.1 broadcast_in_dim.84
  49.9 17.0 %all_to_all.16 = bf16[16,128,224]{1,2,0:T(8,128)(2,1)} all-to-all(bf16[16,128,224]{1,2,0:T(8,128)(2,1)S(1)} %broadcast_in_dim.84), channel_id=1, replica_groups=mesh['hg'=4,'y'=4,'c'=2,'side'=4] {'y','side'}, dimensions={0} | all-to-all | bytes 1835008 | tf_op jit(solution)/shard_map/all_to_all | solution.py:180
  66.9 0.1 reshape.118.gain_ref
  67.0 0.2 fusion.24
  67.2 0.1 div.26
  67.3 0.1 dynamic-slice_multiply_fusion.share_ref
  67.4 1.5 %copy.69.own_ref = bf16[16,128,224]{2,1,0:T(8,128)(2,1)S(1)} copy(bf16[16,128,224]{1,2,0:T(8,128)(2,1)} %all_to_all.16) | data formatting | bytes 1835008 | tf_op jit(solution)/shard_map/all_to_all | solution.py:180
  68.9 0.8 collective-permute-done.3
  69.7 2.3 %copy.70.oth_ref = bf16[16,128,224]{2,1,0:T(8,128)(2,1)} copy(bf16[16,128,224]{1,2,0:T(8,128)(2,1)} %collective-permute-done.3) | data formatting | bytes 1835008 | tf_op jit(solution)/shard_map/ppermute | solution.py:181
  72.0 1.2 %copy-done.1 = bf16[16,128,224]{2,1,0:T(8,128)(2,1)S(1)} copy-done((bf16[16,128,224]{2,1,0:T(8,128)(2,1)S(1)}, bf16[16,128,224]{2,1,0:T(8,128)(2,1)}, u32[]{:S(2)}) %copy-start.1) | copy-done | bytes 917528
  73.2 2.0 %copy-done.2 = bf16[2,7168,128]{2,1,0:T(8,128)(2,1)S(1)} copy-done((bf16[2,7168,128]{2,1,0:T(8,128)(2,1)S(1)}, bf16[2,7168,128]{2,1,0:T(8,128)(2,1)}, u32[]{:S(2)}) %copy-start.2) | copy-done | bytes 3670040
  75.2 2.0 %copy-done.3 = bf16[2,7168,128]{2,1,0:T(8,128)(2,1)S(1)} copy-done((bf16[2,7168,128]{2,1,0:T(8,128)(2,1)S(1)}, bf16[2,7168,128]{2,1,0:T(8,128)(2,1)}, u32[]{:S(2)}) %copy-start.3) | copy-done | bytes 3670040
  77.3 4.1 %shard_map.145 = (bf16[64,7168]{1,0:T(8,128)(2,1)S(1)}, bf16[64,7168]{1,0:T(8,128)(2,1)S(1)}) custom-call(bf16[16,128,224]{2,1,0:T(8,128)(2,1)S(1)} %copy.69.own_ref, bf16[16,128,224]{2,1,0:T(8,128)(2,1)S(1)} %copy-done.1, f32[8,4,224]{2,1,0:T(4,128)S(1)} %reshape.118.gain_ref, f32[128,2]{1,0:T(8,128)S(1)} %dynamic-slice_multiply_fusion.share_ref, ...), custom_call_target="tpu_custom_call" | custom-call | flops 1409286144 | bytes 15000000 | tf_op jit(solution)/shard_map/pallas_call | solution.py:119
  81.4 0.4 collective-permute-start.4
  81.8 2.3 %collective-permute-done.4 = bf16[64,7168]{1,0:T(8,128)(2,1)S(1)} collective-permute-done((bf16[64,7168]{1,0:T(8,128)(2,1)S(1)}, bf16[64,7168]{1,0:T(8,128)(2,1)S(1)}, u32[]{:S(2)}, u32[]{:S(2)}) %collective-permute-start.4) | collective-permute-done | bytes 917536 | tf_op jit(solution)/shard_map/ppermute | solution.py:184
  84.2 1.1 add_convert_fusion
  85.3 2.1 %reshape.113 = bf16[16,4,4,1792]{3,2,1,0:T(4,128)(2,1)S(1)} reshape(bf16[64,7168]{1,0:T(8,128)(2,1)} %add_convert_fusion) | data formatting | bytes 1835008 | tf_op jit(solution)/shard_map/reshape | solution.py:187
  87.4 0.3 copy.71
  87.7 1.6 %copy.72 = bf16[64,4,1792]{2,1,0:T(4,128)(2,1)} copy(bf16[64,4,1792]{2,0,1:T(8,128)(2,1)S(1)} %bitcast.48) | data formatting | bytes 1835008 | tf_op jit(solution)/shard_map/reshape | solution.py:187
  89.4 6.8 %all-to-all-start.2 = ((bf16[64,4,1792]{2,1,0:T(4,128)(2,1)}), bf16[64,4,1792]{2,1,0:T(4,128)(2,1)S(1)}, u32[]{:S(2)}, u32[]{:S(2)}) async-start(bf16[64,4,1792]{2,1,0:T(4,128)(2,1)} %copy.72), calls=%async_computation.2 | async-start | bytes 1835008 | tf_op jit(solution)/shard_map/all_to_all | solution.py:188
  96.2 1.3 %broadcast_select_fusion.1 = (bf16[4,4,224]{1,2,0:T(8,128)(2,1)S(1)}, bf16[4,4,224]{1,2,0:T(8,128)(2,1)S(1)}) fusion(pred[]{:T(512)S(6)} %eq.27, bf16[16,128,224]{1,2,0:T(8,128)(2,1)} %collective-permute-done.3, s32[]{:T(128)S(6)} %select_n.49, s32[]{:T(128)S(6)} %select_n.51, bf16[16,128,224]{1,2,0:T(8,128)(2,1)} %all_to_all.16, s32[]{:T(128)S(6)} %select_n.50), kind=kLoop, calls=%fused_computation.29 | loop fusion | flops 7168 | bytes 28685 | tf_op jit(solution)/shard_map/jit(_where)/select_n | solution.py:194
  97.5 0.1 copy.67
  97.6 0.2 copy.68
  97.9 15.8 %all-to-all-done.2 = bf16[64,4,1792]{2,1,0:T(4,128)(2,1)S(1)} async-done(((bf16[64,4,1792]{2,1,0:T(4,128)(2,1)}), bf16[64,4,1792]{2,1,0:T(4,128)(2,1)S(1)}, u32[]{:S(2)}, u32[]{:S(2)}) %all-to-all-start.2) | async-done | bytes 917536 | tf_op jit(solution)/shard_map/all_to_all | solution.py:188
  113.7 0.4 convert_reduce_fusion
  114.1 0.6 add_convert_fusion.3
  (31 shorter events, 0.9 us)
Async XLA Ops:
  0.0 3.7 %copy-start = (bf16[16,128,512]{2,1,0:T(8,128)(2,1)S(1)}, bf16[16,128,512]{2,1,0:T(8,128)(2,1)}, u32[]{:S(2)}) copy-start(bf16[16,128,512]{2,1,0:T(8,128)(2,1)} %param.17) | copy-start | bytes 6291460
  4.8 6.0 %copy-start.4 = (bf16[2,64,4096]{2,1,0:T(8,128)(2,1)S(1)}, bf16[2,64,4096]{2,1,0:T(8,128)(2,1)}, u32[]{:S(2)}) copy-start(bf16[2,64,4096]{2,1,0:T(8,128)(2,1)} %param.19) | copy-start | bytes 3145732
  35.6 1.6 %collective-permute-start = (bf16[16,4,2176]{2,1,0:T(4,128)(2,1)S(1)}, bf16[16,4,2176]{2,1,0:T(4,128)(2,1)S(1)}, u32[]{:S(2)}, u32[]{:S(2)}) collective-permute-start(bf16[16,4,2176]{2,1,0:T(4,128)(2,1)S(1)} %all_to_all.15), channel_id=1, source_target_pairs={{0,4},{4,0},{1,5},{5,1},{2,6},{6,2},{3,7},{7,3},{8,12},{12,8},{9,1... | collective-permute-start | bytes 835592 | tf_op jit(solution)/shard_map/ppermute | solution.py:163
  39.6 27.3 %copy-start.5 = (bf16[7168]{0:T(1024)(128)(2,1)S(1)}, bf16[7168]{0:T(1024)(128)(2,1)}, u32[]{:S(2)}) copy-start(bf16[7168]{0:T(1024)(128)(2,1)} %param.24) | copy-start | bytes 43012
  39.7 4.3 %collective-permute-start.1 = (bf16[128,224]{1,0:T(8,128)(2,1)S(1)}, bf16[128,224]{1,0:T(8,128)(2,1)S(1)}, u32[]{:S(2)}, u32[]{:S(2)}) collective-permute-start(bf16[128,224]{1,0:T(8,128)(2,1)S(1)} %reshape.110), channel_id=1, source_target_pairs={{0,32},{32,0},{64,96},{96,64},{1,33},{33,1},{65,97},{97,65},{2,34}... | collective-permute-start | bytes 172040 | tf_op jit(solution)/shard_map/ppermute | solution.py:177
  44.1 5.6 %collective-permute-start.2 = (bf16[128,224]{1,0:T(8,128)(2,1)S(1)}, bf16[128,224]{1,0:T(8,128)(2,1)S(1)}, u32[]{:S(2)}, u32[]{:S(2)}) collective-permute-start(bf16[128,224]{1,0:T(8,128)(2,1)S(1)} %add_convert_fusion.2), channel_id=1, source_target_pairs={{32,64},{64,32},{96,0},{0,96},{33,65},{65,33},{97,1},{1,97},{34,66... | collective-permute-start | bytes 172040 | tf_op jit(solution)/shard_map/ppermute | solution.py:178
  66.9 2.8 %collective-permute-start.3 = (bf16[16,128,224]{1,2,0:T(8,128)(2,1)}, bf16[16,128,224]{1,2,0:T(8,128)(2,1)}, u32[]{:S(2)}, u32[]{:S(2)}) collective-permute-start(bf16[16,128,224]{1,2,0:T(8,128)(2,1)} %all_to_all.16), channel_id=1, source_target_pairs={{0,4},{4,0},{1,5},{5,1},{2,6},{6,2},{3,7},{7,3},{8,12},{12,8},{9,1... | collective-permute-start | bytes 2752520 | tf_op jit(solution)/shard_map/ppermute | solution.py:181
  72.0 1.2 %copy-start.1 = (bf16[16,128,224]{2,1,0:T(8,128)(2,1)S(1)}, bf16[16,128,224]{2,1,0:T(8,128)(2,1)}, u32[]{:S(2)}) copy-start(bf16[16,128,224]{2,1,0:T(8,128)(2,1)} %copy.70.oth_ref) | copy-start | bytes 2752516
  73.2 2.0 %copy-start.2 = (bf16[2,7168,128]{2,1,0:T(8,128)(2,1)S(1)}, bf16[2,7168,128]{2,1,0:T(8,128)(2,1)}, u32[]{:S(2)}) copy-start(bf16[2,7168,128]{2,1,0:T(8,128)(2,1)} %wg_hbm.1) | copy-start | bytes 11010052
  75.2 2.0 %copy-start.3 = (bf16[2,7168,128]{2,1,0:T(8,128)(2,1)S(1)}, bf16[2,7168,128]{2,1,0:T(8,128)(2,1)}, u32[]{:S(2)}) copy-start(bf16[2,7168,128]{2,1,0:T(8,128)(2,1)} %wu_hbm.1) | copy-start | bytes 11010052
  81.4 2.7 %collective-permute-start.4 = (bf16[64,7168]{1,0:T(8,128)(2,1)S(1)}, bf16[64,7168]{1,0:T(8,128)(2,1)S(1)}, u32[]{:S(2)}, u32[]{:S(2)}) collective-permute-start(bf16[64,7168]{1,0:T(8,128)(2,1)S(1)} %get-tuple-element.8), channel_id=1, source_target_pairs={{0,4},{4,0},{1,5},{5,1},{2,6},{6,2},{3,7},{7,3},{8,12},{12,8},{9,1... | collective-permute-start | bytes 2752520 | tf_op jit(solution)/shard_map/ppermute | solution.py:184
  89.4 24.3 %all-to-all-start.2 = ((bf16[64,4,1792]{2,1,0:T(4,128)(2,1)}), bf16[64,4,1792]{2,1,0:T(4,128)(2,1)S(1)}, u32[]{:S(2)}, u32[]{:S(2)}) async-start(bf16[64,4,1792]{2,1,0:T(4,128)(2,1)} %copy.72), calls=%async_computation.2 | async-start | bytes 1835008 | tf_op jit(solution)/shard_map/all_to_all | solution.py:188

commit v2 on v1

v2 whole, which is shorter than its diff:
```python
import functools

import jax
import jax.numpy as jnp
from jax import lax
from jax.experimental import pallas as pl
from jax.experimental.pallas import tpu as pltpu
from jax.sharding import Mesh
from jax.sharding import PartitionSpec as P

LAT = 512
ROPE = 64
NOPE = 128
VDIM = 128
QPR = 2
LEN = 4096
EPS = 1e-06
ROUTE_SCALE = 2.5
BF = jnp.bfloat16
F32 = jnp.float32

PAIRS_A = [(0, 1), (1, 0), (2, 3), (3, 2)]
PAIRS_B = [(1, 2), (2, 1), (3, 0), (0, 3)]
SWAP = [(0, 1), (1, 0)]


def attention_kernel(len_ref, qn_ref, qr_ref, res_ref, routes_ref, ints_ref, wa_hbm, lat_hbm, rope_hbm, wv_hbm, out_ref,
                     wa, wv, lat, rope, qs, qps, os, ext, sem_w, sem_l, sem_r, *, span, sides, experts):
    reqs, length, width = lat_hbm.shape
    heads = wa_hbm.shape[0]
    toks = qn_ref.shape[0]
    qpr = toks // reqs
    rows = qpr * heads
    spans = length // span
    lanes = width // 128
    scale = (NOPE + ROPE) ** (-0.5)
    absorb = pltpu.make_async_copy(wa_hbm, wa, sem_w.at[0])
    absorb.start()
    value = pltpu.make_async_copy(wv_hbm, wv, sem_w.at[1])

    def copies(r, i):
        at = pl.ds(i * span, span)
        return (
            pltpu.make_async_copy(lat_hbm.at[r, at, :], lat.at[r, at, :], sem_l.at[r * spans + i]),
            pltpu.make_async_copy(rope_hbm.at[r, :, at], rope.at[r, :, at], sem_r.at[r * spans + i]),
        )

    for r in range(reqs):
        for i in range(spans):
            def begin(r=r, i=i):
                for copy in copies(r, i):
                    copy.start()

            if i == 0:
                begin()
            else:
                pl.when(i * span < len_ref[r])(begin)
    value.start()
    planes = out_ref.shape[0]
    cores = 2
    n_val = heads * VDIM
    cols = res_ref.shape[1] // (planes * cores)
    which = lax.broadcasted_iota(jnp.int32, res_ref.shape, 0) == lax.axis_index("hg")
    row = jnp.sum(jnp.where(which, res_ref[...].astype(F32), 0.0), axis=0, keepdims=True)
    lane = lax.broadcasted_iota(jnp.int32, (1, 128), 1)
    dense = jnp.zeros((1, 128), jnp.int32)
    for j in range(toks):
        for k in range(routes_ref.shape[1]):
            dense = dense + jnp.where(lane == j * experts + routes_ref[j, k], ints_ref[j, k], 0)
    dense = dense.astype(F32)
    for p in range(planes):
        y, side = divmod(p, sides)
        for c in range(cores):
            start = ((y * cores + c) * sides + side) * cols // 128
            for t in range(3):
                tile = min(start + t, res_ref.shape[1] // 128 - 1)
                ext[p, pl.ds(t, 1), c * 128:(c + 1) * 128] = row[:, tile * 128:(tile + 1) * 128]
        ext[p, pl.ds(3, 1), :] = jnp.concatenate([dense, dense], axis=1)
    for p in range(planes):
        out_ref[p, :, n_val:] = ext[p].astype(BF)
    turned = qr_ref[...].astype(F32)
    for h in range(heads):
        pair = turned[:, (h // 2) * 2 * ROPE:(h // 2 + 1) * 2 * ROPE]
        if h % 2:
            pair = jnp.concatenate([pair[:, ROPE:], pair[:, :ROPE]], axis=1)
        qps[pl.ds(h, toks, stride=heads), :] = pair
    absorb.wait()
    for h in range(heads):
        latent = jnp.dot(qn_ref[:, h * NOPE:(h + 1) * NOPE], wa[h], preferred_element_type=F32)
        for c in range(lanes):
            qs[c, pl.ds(h, toks, stride=heads), :] = latent[:, c * 128:(c + 1) * 128]
    for r in range(reqs):
        at = pl.ds(r * rows, rows)
        query = jnp.concatenate([qs[c, at, :] for c in range(lanes)], axis=1).astype(BF)
        rotary = qps[at, :ROPE].astype(BF)
        filled = len_ref[r]
        limit = filled - qpr + lax.broadcasted_iota(jnp.int32, (rows, 1), 0) // heads

        def step(i, old, r=r, query=query, rotary=rotary, limit=limit):
            for copy in copies(r, i):
                copy.wait()
            keys = lat[r, pl.ds(i * span, span), :]
            s = lax.dot_general(query, keys, (((1,), (1,)), ((), ())), preferred_element_type=F32)
            s = s + jnp.dot(rotary, rope[r, :, pl.ds(i * span, span)], preferred_element_type=F32)
            position = i * span + lax.broadcasted_iota(jnp.int32, (rows, span), 1)
            s = jnp.where(position <= limit, s * scale, -jnp.inf)
            top = jnp.max(s, axis=1, keepdims=True)
            if old is not None:
                top = jnp.maximum(old[0], top)
            p = jnp.exp(s - top)
            norm = jnp.sum(p, axis=1, keepdims=True)
            acc = jnp.dot(p.astype(BF), keys, preferred_element_type=F32)
            if old is not None:
                fade = jnp.exp(old[0] - top)
                norm = norm + fade * old[1]
                acc = acc + fade * old[2]
            return top, norm, acc

        state = step(0, None)
        for i in range(1, spans):
            state = lax.cond(i * span < filled, functools.partial(step, i), lambda old: old, state)
        result = state[2] / state[1]
        for c in range(lanes):
            os[c, at, :] = result[:, c * 128:(c + 1) * 128]
    value.wait()
    for h in range(heads):
        at = pl.ds(h, toks, stride=heads)
        o = jnp.concatenate([os[c, at, :] for c in range(lanes)], axis=1).astype(BF)
        head = jnp.dot(o, wv[h], preferred_element_type=F32).astype(BF)
        for k in range(planes):
            out_ref[k, :, h * VDIM:(h + 1) * VDIM] = head


def attention(q_nope, q_rope, w_absorb, cache_latent, cache_rope, lengths, w_value, residual, routes, gate_int,
              planes, sides, experts, span=2048):
    reqs, length, width = cache_latent.shape
    spans = length // span
    heads = w_absorb.shape[0]
    toks = q_nope.shape[0]
    hbm = pl.BlockSpec(memory_space=pltpu.HBM)
    vmem = pl.BlockSpec(memory_space=pltpu.VMEM)
    smem = pl.BlockSpec(memory_space=pltpu.SMEM)
    return pl.pallas_call(
        functools.partial(attention_kernel, span=span, sides=sides, experts=experts),
        out_shape=jax.ShapeDtypeStruct((planes, toks, heads * VDIM + 256), BF),
        in_specs=[smem] + [vmem] * 3 + [smem] * 2 + [hbm] * 4,
        out_specs=vmem,
        scratch_shapes=[
            pltpu.VMEM(w_absorb.shape, BF),
            pltpu.VMEM(w_value.shape, BF),
            pltpu.VMEM(cache_latent.shape, BF),
            pltpu.VMEM(cache_rope.shape, BF),
            pltpu.VMEM((width // 128, toks * heads, 128), F32),
            pltpu.VMEM((toks * heads, 2 * ROPE), F32),
            pltpu.VMEM((width // 128, toks * heads, 128), F32),
            pltpu.VMEM((planes, toks, 256), F32),
            pltpu.SemaphoreType.DMA((2,)),
            pltpu.SemaphoreType.DMA((reqs * spans,)),
            pltpu.SemaphoreType.DMA((reqs * spans,)),
        ],
        compiler_params=pltpu.CompilerParams(vmem_limit_bytes=60 * 1024 * 1024),
        name="attention",
    )(lengths, q_nope, q_rope, residual, routes, gate_int, w_absorb, cache_latent, cache_rope, w_value)


def half_copies(wg_hbm, wu_hbm, wg, wu, sem, part, stripes):
    experts, depth, _ = wg_hbm.shape
    stripe = depth // stripes
    half = stripe // 2
    groups = []
    for y in range(stripes):
        at = pl.ds(pl.multiple_of(y * stripe + part * half, 16), half)
        to = pl.ds(y * half, half)
        groups.append([
            pltpu.make_async_copy(src.at[e, at, :], dst.at[e, to, :], sem.at[(y * experts + e) * 2 + k])
            for e in range(experts)
            for k, (src, dst) in enumerate(((wg_hbm, wg), (wu_hbm, wu)))
        ])
    return groups


def half_products(blocks_ref, gain_ref, wg, wu, groups, part, acc, swap):
    blocks, rows, _ = blocks_ref.shape
    stripes = len(groups)
    sides = blocks // stripes
    cols = gain_ref.shape[2]
    half = rows // 2
    square = jnp.zeros((rows, cols), F32)
    for y in range(stripes):
        for copy in groups[y]:
            copy.wait()
        for s in range(sides):
            block = blocks_ref[y * sides + s, :, :cols].astype(F32)
            if swap:
                block = jnp.concatenate([block[half:], block[:half]], axis=0)
            square = square + block * block
            scaled = (block * gain_ref[y * 2 + part, pl.ds(s, 1), :]).astype(BF)
            at = pl.ds((y * sides + s) * cols, cols)
            for e in range(len(acc)):
                both = jnp.concatenate([wg[e, at, :], wu[e, at, :]], axis=1)
                acc[e] = acc[e] + jnp.dot(scaled, both, preferred_element_type=F32)
    return acc, jnp.sum(square, axis=-1, keepdims=True)


def first_kernel(own_ref, gain_ref, wg_hbm, wu_hbm, acc_ref, sq_ref, wg, wu, sem):
    experts, depth, units = wg_hbm.shape
    rows = own_ref.shape[1]
    core = lax.axis_index("c")
    groups = half_copies(wg_hbm, wu_hbm, wg, wu, sem, core, gain_ref.shape[0] // 2)
    for group in groups:
        for copy in group:
            copy.start()
    acc = [jnp.zeros((rows, 2 * units), F32) for _ in range(experts)]
    acc, square = half_products(own_ref, gain_ref, wg, wu, groups, core, acc, False)
    for e in range(experts):
        acc_ref[e] = acc[e]
    sq_ref[...] = square


def second_kernel(oth_ref, gain_ref, share_ref, acc_ref, sq_ref, wg_hbm, wu_hbm, wd_hbm, keep_ref, send_ref,
                  wg, wu, wd, sem, sem_down):
    experts, depth, units = wg_hbm.shape
    blocks, rows, _ = oth_ref.shape
    half = rows // 2
    part = 1 - lax.axis_index("c")
    groups = half_copies(wg_hbm, wu_hbm, wg, wu, sem, part, gain_ref.shape[0] // 2)
    downs = [
        pltpu.make_async_copy(wd_hbm.at[e], wd.at[pl.ds(e * units, units), :], sem_down.at[e])
        for e in range(experts)
    ]
    for group in groups:
        for copy in group:
            copy.start()
    for copy in downs:
        copy.start()
    acc, square = half_products(oth_ref, gain_ref, wg, wu, groups, part, [acc_ref[e] for e in range(experts)], True)
    inverse = lax.rsqrt((square + sq_ref[...]) / depth + EPS)
    acts = []
    for e in range(experts):
        both = acc[e] * inverse
        gate, up = both[:, :units], both[:, units:]
        share = share_ref[:, e:e + 1]
        act = gate / (1.0 + jnp.exp(-gate)) * up
        acts.append(jnp.where(share > 0, act * share, 0.0).astype(BF))
    act = jnp.concatenate(acts, axis=1)
    for copy in downs:
        copy.wait()
    messages, lines, tile = keep_ref.shape
    toks = lines // 2
    for n in range(depth // (2 * tile)):
        left = jnp.dot(act, wd[:, 2 * n * tile:(2 * n + 1) * tile], preferred_element_type=F32)
        right = jnp.dot(act, wd[:, (2 * n + 1) * tile:(2 * n + 2) * tile], preferred_element_type=F32)
        for k in range(blocks):
            for ref, base in ((keep_ref, 0), (send_ref, half)):
                at = slice(base + k * toks, base + (k + 1) * toks)
                ref[n * blocks + k] = jnp.concatenate([left[at], right[at]], axis=0).astype(BF)


def own_half(own, gain, w_gate, w_up):
    experts, depth, units = w_gate.shape
    rows = own.shape[1]
    vmem = pl.BlockSpec(memory_space=pltpu.VMEM)
    hbm = pl.BlockSpec(memory_space=pltpu.HBM)
    w_gate, w_up = (pltpu.with_memory_space_constraint(a, pltpu.HBM) for a in (w_gate, w_up))
    return pl.pallas_call(
        first_kernel,
        out_shape=(jax.ShapeDtypeStruct((experts, rows, 2 * units), F32), jax.ShapeDtypeStruct((rows, 1), F32)),
        in_specs=[vmem] * 2 + [hbm] * 2,
        out_specs=[vmem] * 2,
        scratch_shapes=[
            pltpu.VMEM((experts, depth // 2, units), BF),
            pltpu.VMEM((experts, depth // 2, units), BF),
            pltpu.SemaphoreType.DMA((gain.shape[0] * experts,)),
        ],
        compiler_params=pltpu.CompilerParams(vmem_limit_bytes=16 * 1024 * 1024),
        cost_estimate=pl.CostEstimate(flops=rows * depth * 512, bytes_accessed=5_000_000, transcendentals=0),
        name="experts_first",
    )(own, gain, w_gate, w_up)


def other_half(oth, gain, share, acc, square, w_gate, w_up, w_down, hgs):
    experts, depth, units = w_gate.shape
    blocks, rows, _ = oth.shape
    shape = jax.ShapeDtypeStruct((hgs * blocks, rows // blocks, depth // hgs // 2), BF)
    vmem = pl.BlockSpec(memory_space=pltpu.VMEM)
    hbm = pl.BlockSpec(memory_space=pltpu.HBM)
    w_gate, w_up, w_down = (pltpu.with_memory_space_constraint(a, pltpu.HBM) for a in (w_gate, w_up, w_down))
    return pl.pallas_call(
        second_kernel,
        out_shape=(shape, shape),
        in_specs=[vmem] * 5 + [hbm] * 3,
        out_specs=[vmem] * 2,
        scratch_shapes=[
            pltpu.VMEM((experts, depth // 2, units), BF),
            pltpu.VMEM((experts, depth // 2, units), BF),
            pltpu.VMEM((experts * units, depth), BF),
            pltpu.SemaphoreType.DMA((gain.shape[0] * experts,)),
            pltpu.SemaphoreType.DMA((experts,)),
        ],
        compiler_params=pltpu.CompilerParams(vmem_limit_bytes=24 * 1024 * 1024),
        cost_estimate=pl.CostEstimate(flops=rows * depth * 1024, bytes_accessed=10_000_000, transcendentals=0),
        name="experts_second",
    )(oth, gain, share, acc, square, w_gate, w_up, w_down)


def body(
    q_nope, q_rope, w_absorb, cache_latent, cache_rope, lengths, w_value, w_out, residual, norm_gain,
    routes, gate_int, w_gate, w_up, w_down,
):
    hgs, ys, cores, sides = (lax.axis_size(a) for a in ("hg", "y", "c", "side"))
    hg, y, core, side = (lax.axis_index(a) for a in ("hg", "y", "c", "side"))
    planes = ys * sides
    toks, width = residual.shape
    cols = w_out.shape[1]
    local_experts = w_gate.shape[0]
    experts_all = local_experts * ys * cores

    message = attention(q_nope, q_rope, w_absorb, cache_latent, cache_rope, lengths, w_value, residual, routes, gate_int,
                        planes, sides, experts_all)
    here = lax.all_to_all(message, ("y", "side"), 0, 0, tiled=True)
    there = lax.ppermute(here, "c", SWAP)
    both = jnp.stack([here, there])
    n_val = w_absorb.shape[0] * VDIM
    all_values = both[..., :n_val].reshape(cores * planes * toks, n_val)
    extra = both[..., n_val:]
    window = lax.dynamic_slice_in_dim(extra[..., :3, :], core * 128, 128, 3).reshape(cores * planes, 3 * 128)
    block = (y * cores + core) * sides + side
    mine = lax.dynamic_slice_in_dim(window, lax.rem(block * cols, 128), cols, 1)[:, None]
    gates = extra[..., 3, :toks * experts_all].reshape(cores * planes * toks, experts_all).astype(F32)
    total = jnp.sum(gates, axis=1, keepdims=True)
    first = (y * cores + core) * local_experts
    share = lax.dynamic_slice_in_dim(gates, first, local_experts, 1) * (ROUTE_SCALE / total)

    partial = jnp.dot(all_values, w_out, preferred_element_type=F32).reshape(cores * planes, toks, cols)
    is_row = (jnp.arange(toks) == hg)[None, :, None]
    partial = (partial + jnp.where(is_row, mine.astype(F32), 0.0)).astype(BF).reshape(-1, cols)
    partial = jnp.pad(partial, ((0, 0), (0, -cols % 128)))
    pair = (partial.astype(F32) + lax.ppermute(partial, "hg", PAIRS_A).astype(F32)).astype(BF)
    hidden = (pair.astype(F32) + lax.ppermute(pair, "hg", PAIRS_B).astype(F32)).astype(BF)

    own = lax.all_to_all(jnp.broadcast_to(hidden[None], (planes,) + hidden.shape), ("y", "side"), 0, 0, tiled=True)
    oth = lax.ppermute(own, "c", SWAP)
    gain = norm_gain.astype(F32).reshape(ys * cores, sides, cols)
    acc, square = own_half(own, gain, w_gate, w_up)
    keep, send = other_half(oth, gain, share, acc, square, w_gate, w_up, w_down, hgs)
    got = lax.ppermute(send, "c", SWAP)
    quarter = width // hgs
    summed = keep + got
    at = (y * sides + side) * toks
    half = planes * toks
    own_piece = lax.dynamic_slice(own, (hg * sides, at, 0), (sides, toks, cols))
    oth_piece = lax.dynamic_slice(oth, (hg * sides, half + at, 0), (sides, toks, cols))
    low = jnp.where(core == 0, own_piece, oth_piece)
    high = jnp.where(core == 0, oth_piece, own_piece)
    kept = jnp.concatenate([low, high], axis=0).transpose(1, 0, 2).reshape(toks, quarter)
    summed, kept = lax.optimization_barrier((summed, kept))
    parts = lax.all_to_all(summed, ("hg", "y", "side"), 0, 0, tiled=True)
    moe = jnp.sum(parts.astype(F32), axis=0)
    moe = jnp.concatenate([moe[:toks], moe[toks:]], axis=1)
    return (kept.astype(F32) + moe).astype(BF)


def solution(mesh):
    devices = mesh.devices
    fine = Mesh(devices.reshape(4, 4, 2, 4), ("hg", "y", "c", "side"))
    grp = ("y", "c")
    plane = ("y", "c", "side")
    in_specs = (
        P(plane, "hg"),
        P(plane, "hg"),
        P("hg", None, None),
        P(plane, None, None),
        P(plane, None, None),
        P(plane),
        P("hg", None, None),
        P("hg", plane),
        P(plane, None),
        P(),
        P(plane, None),
        P(plane, None),
        P(grp, None, ("hg", "side")),
        P(grp, None, ("hg", "side")),
        P(grp, ("hg", "side"), None),
    )
    return jax.shard_map(body, mesh=fine, in_specs=in_specs, out_specs=P(plane, "hg"), check_vma=False)
```

time: 115 us -> 98.8 us (0.86)
  blocking collectives: 33.6 us -> 60.9 us
  waiting for transfers between devices: 26 us -> 9.32 us
  matrix products: 16 us -> 0.56 us
  local copies, waits for them, and re-layouts: 16.8 us -> 1.5 us
  Pallas kernels: 4.13 us -> 17.3 us
  starting transfers between devices: 11.6 us -> 4.91 us
  other arithmetic: 6.27 us -> 4.02 us
    all_to_all x0 -> x1, blocking collectives: none -> 24.1 us  [body(): parts = lax.all_to_all(summed, ('hg', 'y', 'side'), 0, 0, tiled=True)]
    all_to_all x1 -> x0, waiting for transfers between devices: 15.8 us -> none  [body(): parts = lax.all_to_all(summed, ('hg', 'y', 'side'), 0, 0, tiled=True)]
    dot_general x5 -> x0, matrix products: 14.4 us -> none  [the longest x1 5.99 us: attention(): jnp.einsum('rqhc,rpc->rqhp', q_latent, cache_latent, preferred_element_ty...]
    pallas_call x1 -> x3, Pallas kernels: 4.13 us -> 17.3 us  [the longest x1 9.45 us: attention(): pl.pallas_call(functools.partial(attention_kernel, span=span, sides=sides...]
    all_to_all x1 -> x0, starting transfers between devices: 6.84 us -> none  [body(): parts = lax.all_to_all(summed, ('hg', 'y', 'side'), 0, 0, tiled=True)]
    reshape x7 -> x1, local copies, waits for them, and re-layouts: 5.05 us -> 0.1 us  [body(): jnp.concatenate([low, high], axis=0).transpose(1, 0, 2)]
    unnamed x12 -> x9, local copies, waits for them, and re-layouts: 5.32 us -> 0.97 us
    ppermute x1 -> x0, local copies, waits for them, and re-layouts: 2.25 us -> none  [body(): oth = lax.ppermute(own, 'c', SWAP)]
  transfers between devices with their start and end apart: 6 -> 5, of which waited for: 6 -> 4; matrix products, arithmetic and copies ran while one was open for 3% -> 1% of each run, Pallas kernels for 0% -> 3%
where the time goes in v2:
time: 98.8 us; the launch traced here: 98.7 us
  blocking collectives  60.9 us (62%)
  Pallas kernels  17.3 us (18%)
  waiting for transfers between devices  9.32 us (9%)
  starting transfers between devices  4.91 us (5%)
  other arithmetic  4.02 us (4%)
  local copies, waits for them, and re-layouts  1.5 us (2%)
    all_to_all x1, blocking collectives, body(): parts = lax.all_to_all(summed, ('hg', 'y', 'side'), 0, 0, tiled=True)  24.1 us
    all_to_all x1, blocking collectives, body(): lax.all_to_all(jnp.broadcast_to(hidden[None], (planes,) + hidden.shape),...  18.6 us
    all_to_all x1, blocking collectives, body(): here = lax.all_to_all(message, ('y', 'side'), 0, 0, tiled=True)  18.3 us
    pallas_call x1, Pallas kernels, attention(): pl.pallas_call(functools.partial(attention_kernel, span=span, sides=sides...  9.45 us
    pallas_call x1, Pallas kernels, other_half(): pl.pallas_call(second_kernel, out_shape=(shape, shape), in_specs=[vmem] *...  5.28 us
    ppermute x1, starting transfers between devices, body(): lax.ppermute(pair, 'hg', PAIRS_B).astype(F32)  2.83 us
    ppermute x1, waiting for transfers between devices, body(): lax.ppermute(partial, 'hg', PAIRS_A).astype(F32)  2.78 us
    ppermute x1, waiting for transfers between devices, body(): lax.ppermute(pair, 'hg', PAIRS_B).astype(F32)  2.72 us
  transfers between devices with their start and end apart: 5, of which 4 were waited for; matrix products, arithmetic and copies ran while one was open for 1% of the time, Pallas kernels for 3%

profile of v2, /device:TPU:0, one launch (start us, length us, event | category | flops | bytes accessed | tf_op | source)
XLA Modules:
  0.0 98.7 jit_solution(15569214089629152575)
XLA Ops:
  0.0 0.0 copy-start
  0.0 9.5 %attention.1 = bf16[16,4,2304]{2,1,0:T(4,128)(2,1)} custom-call(s32[2]{0:T(128)} %len_ref.1, bf16[4,2048]{1,0:T(4,128)(2,1)} %qn_ref.1, bf16[4,1024]{1,0:T(4,128)(2,1)} %qr_ref.1, bf16[4,7168]{1,0:T(4,128)(2,1)} %res_ref.1, s32[4,4]{1,0:T(4,128)} %routes_ref.1, s32[4,4]{1,0:T(4,128)} %ints_ref.1, bf16[16,128,512]{2,1,0:T(8,128)(2,1)} %wa_hbm.1, ...), custom_call_target="tpu_custom_call" | custom-call | tf_op jit(solution)/shard_map/attention/pallas_call | solution.py:143
  9.5 18.3 %all_to_all.15 = bf16[16,4,2304]{2,1,0:T(4,128)(2,1)S(1)} all-to-all(bf16[16,4,2304]{2,1,0:T(4,128)(2,1)} %attention.1), channel_id=1, replica_groups=mesh['hg'=4,'y'=4,'c'=2,'side'=4] {'y','side'}, dimensions={0} | all-to-all | bytes 589824 | tf_op jit(solution)/shard_map/all_to_all | solution.py:320
  27.7 0.0 collective-permute-start
  27.8 0.0 copy-start.3
  27.8 1.5 %collective-permute-done = bf16[16,4,2304]{2,1,0:T(4,128)(2,1)S(1)} collective-permute-done((bf16[16,4,2304]{2,1,0:T(4,128)(2,1)S(1)}, bf16[16,4,2304]{2,1,0:T(4,128)(2,1)S(1)}, u32[]{:S(2)}, u32[]{:S(2)}) %collective-permute-start) | collective-permute-done | bytes 294944 | tf_op jit(solution)/shard_map/ppermute | solution.py:321
  29.3 0.0 copy-start.2
  29.3 0.4 fusion.2
  29.8 0.1 dynamic-slice_convert_fusion
  29.9 0.0 copy-done
  29.9 0.6 fusion
  30.4 0.1 copy.18
  30.6 1.6 %collective-permute-start.1 = (bf16[128,256]{1,0:T(8,128)(2,1)S(1)}, bf16[128,256]{1,0:T(8,128)(2,1)S(1)}, u32[]{:S(2)}, u32[]{:S(2)}) collective-permute-start(bf16[128,256]{1,0:T(8,128)(2,1)S(1)} %pad.4), channel_id=1, source_target_pairs={{0,32},{32,0},{64,96},{96,64},{1,33},{33,1},{65,97},{97,65},{2,34}... | collective-permute-start | bytes 196616 | tf_op jit(solution)/shard_map/ppermute | solution.py:338
  32.1 2.8 %collective-permute-done.1 = bf16[128,256]{1,0:T(8,128)(2,1)S(1)} collective-permute-done((bf16[128,256]{1,0:T(8,128)(2,1)S(1)}, bf16[128,256]{1,0:T(8,128)(2,1)S(1)}, u32[]{:S(2)}, u32[]{:S(2)}) %collective-permute-start.1) | collective-permute-done | bytes 65568 | tf_op jit(solution)/shard_map/ppermute | solution.py:338
  34.9 2.8 %collective-permute-start.2 = (bf16[128,256]{1,0:T(8,128)(2,1)S(1)}, bf16[128,256]{1,0:T(8,128)(2,1)S(1)}, u32[]{:S(2)}, u32[]{:S(2)}) collective-permute-start(bf16[128,256]{1,0:T(8,128)(2,1)S(1)} %add_convert_fusion.1), channel_id=1, source_target_pairs={{32,64},{64,32},{96,0},{0,96},{33,65},{65,33},{97,1},{1,97},{34,66... | collective-permute-start | bytes 196616 | tf_op jit(solution)/shard_map/ppermute | solution.py:339
  37.8 2.7 %collective-permute-done.2 = bf16[128,256]{1,0:T(8,128)(2,1)S(1)} collective-permute-done((bf16[128,256]{1,0:T(8,128)(2,1)S(1)}, bf16[128,256]{1,0:T(8,128)(2,1)S(1)}, u32[]{:S(2)}, u32[]{:S(2)}) %collective-permute-start.2) | collective-permute-done | bytes 65568 | tf_op jit(solution)/shard_map/ppermute | solution.py:339
  40.5 0.0 copy-done.2
  40.5 0.1 broadcast_in_dim.32
  40.6 18.6 %all_to_all.16.own_ref = bf16[16,128,256]{2,1,0:T(8,128)(2,1)S(1)} all-to-all(bf16[16,128,256]{2,1,0:T(8,128)(2,1)S(1)} %broadcast_in_dim.32), channel_id=1, replica_groups=mesh['hg'=4,'y'=4,'c'=2,'side'=4] {'y','side'}, dimensions={0} | all-to-all | bytes 2097152 | tf_op jit(solution)/shard_map/all_to_all | solution.py:341
  59.2 0.0 collective-permute-start.3
  59.2 0.0 copy-done.3
  59.2 0.1 reshape.37.gain_ref
  59.3 0.8 fusion.6
  60.1 0.1 reshape.38
  60.1 0.1 reduce_sum.18
  60.3 0.1 dynamic-slice_multiply_fusion.share_ref
  60.4 2.6 %experts_first.1 = (f32[2,128,256]{2,1,0:T(8,128)S(1)}, f32[128,1]{1,0:T(8,128)S(1)}) custom-call(bf16[16,128,256]{2,1,0:T(8,128)(2,1)S(1)} %all_to_all.16.own_ref, f32[8,4,224]{2,1,0:T(4,128)S(1)} %reshape.37.gain_ref, bf16[2,7168,128]{2,1,0:T(8,128)(2,1)} %wg_hbm.3, bf16[2,7168,128]{2,1,0:T(8,128)(2,1)} %wu_hbm.3), custom_call_target="tpu_custom_call" | custom-call | flops 469762048 | bytes 5000000 | tf_op jit(solution)/shard_map/experts_first/pallas_call | solution.py:265
  63.0 0.0 collective-permute-done.3.oth_ref
  63.0 5.3 %experts_second.1 = (bf16[64,8,896]{2,1,0:T(8,128)(2,1)S(1)}, bf16[64,8,896]{2,1,0:T(8,128)(2,1)}) custom-call(bf16[16,128,256]{2,1,0:T(8,128)(2,1)S(1)} %collective-permute-done.3.oth_ref, f32[8,4,224]{2,1,0:T(4,128)S(1)} %reshape.37.gain_ref, f32[128,2]{1,0:T(8,128)S(1)} %dynamic-slice_multiply_fusion.share_ref, ...), custom_call_target="tpu_custom_call" | custom-call | flops 939524096 | bytes 10000000 | tf_op jit(solution)/shard_map/experts_second/pallas_call | solution.py:288
  68.3 0.0 copy-start.1
  68.3 0.9 copy-done.1
  69.2 0.5 collective-permute-start.4
  69.8 0.1 reshape.35
  69.9 2.3 %collective-permute-done.4 = bf16[64,8,896]{2,1,0:T(8,128)(2,1)} collective-permute-done((bf16[64,8,896]{2,1,0:T(8,128)(2,1)}, bf16[64,8,896]{2,1,0:T(8,128)(2,1)}, u32[]{:S(2)}, u32[]{:S(2)}) %collective-permute-start.4) | collective-permute-done | bytes 917536 | tf_op jit(solution)/shard_map/ppermute | solution.py:346
  72.2 1.7 %add.56 = bf16[64,8,896]{2,1,0:T(8,128)(2,1)S(1)} add(bf16[64,8,896]{2,1,0:T(8,128)(2,1)} %copy-done.1, bf16[64,8,896]{2,1,0:T(8,128)(2,1)} %collective-permute-done.4) | non-fusion elementwise | flops 458752 | bytes 2752512 | tf_op jit(solution)/shard_map/add | solution.py:348
  73.8 24.1 %all_to_all.17 = bf16[64,8,896]{2,1,0:T(8,128)(2,1)S(1)} all-to-all(bf16[64,8,896]{2,1,0:T(8,128)(2,1)S(1)} %add.56), channel_id=1, replica_groups=mesh['hg'=4,'y'=4,'c'=2,'side'=4] {'hg','y','side'}, dimensions={0} | all-to-all | bytes 1835008 | tf_op jit(solution)/shard_map/all_to_all | solution.py:357
  97.9 0.2 convert_reduce_fusion
  98.1 0.6 fusion.4
  (14 shorter events, 0.2 us)
Async XLA Ops:
  0.0 29.9 %copy-start = (bf16[2048,224]{0,1:T(8,128)(2,1)S(1)}, bf16[2048,224]{0,1:T(8,128)(2,1)}, u32[]{:S(2)}) copy-start(bf16[2048,224]{0,1:T(8,128)(2,1)} %param.22) | copy-start | bytes 2752516
  27.7 1.6 %collective-permute-start = (bf16[16,4,2304]{2,1,0:T(4,128)(2,1)S(1)}, bf16[16,4,2304]{2,1,0:T(4,128)(2,1)S(1)}, u32[]{:S(2)}, u32[]{:S(2)}) collective-permute-start(bf16[16,4,2304]{2,1,0:T(4,128)(2,1)S(1)} %all_to_all.15), channel_id=1, source_target_pairs={{0,4},{4,0},{1,5},{5,1},{2,6},{6,2},{3,7},{7,3},{8,12},{12,8},{9,1... | collective-permute-start | bytes 884744 | tf_op jit(solution)/shard_map/ppermute | solution.py:321
  27.8 31.4 %copy-start.3 = (bf16[7168]{0:T(1024)(128)(2,1)S(1)}, bf16[7168]{0:T(1024)(128)(2,1)}, u32[]{:S(2)}) copy-start(bf16[7168]{0:T(1024)(128)(2,1)} %param.24) | copy-start | bytes 43012
  29.3 11.2 %copy-start.2 = (bf16[16,4,2304]{2,1,0:T(4,128)(2,1)}, bf16[16,4,2304]{2,1,0:T(4,128)(2,1)S(1)}, u32[]{:S(2)}) copy-start(bf16[16,4,2304]{2,1,0:T(4,128)(2,1)S(1)} %collective-permute-done) | copy-start | bytes 884740
  30.6 4.3 %collective-permute-start.1 = (bf16[128,256]{1,0:T(8,128)(2,1)S(1)}, bf16[128,256]{1,0:T(8,128)(2,1)S(1)}, u32[]{:S(2)}, u32[]{:S(2)}) collective-permute-start(bf16[128,256]{1,0:T(8,128)(2,1)S(1)} %pad.4), channel_id=1, source_target_pairs={{0,32},{32,0},{64,96},{96,64},{1,33},{33,1},{65,97},{97,65},{2,34}... | collective-permute-start | bytes 196616 | tf_op jit(solution)/shard_map/ppermute | solution.py:338
  34.9 5.6 %collective-permute-start.2 = (bf16[128,256]{1,0:T(8,128)(2,1)S(1)}, bf16[128,256]{1,0:T(8,128)(2,1)S(1)}, u32[]{:S(2)}, u32[]{:S(2)}) collective-permute-start(bf16[128,256]{1,0:T(8,128)(2,1)S(1)} %add_convert_fusion.1), channel_id=1, source_target_pairs={{32,64},{64,32},{96,0},{0,96},{33,65},{65,33},{97,1},{1,97},{34,66... | collective-permute-start | bytes 196616 | tf_op jit(solution)/shard_map/ppermute | solution.py:339
  59.2 3.8 %collective-permute-start.3 = (bf16[16,128,256]{2,1,0:T(8,128)(2,1)S(1)}, bf16[16,128,256]{2,1,0:T(8,128)(2,1)S(1)}, u32[]{:S(2)}, u32[]{:S(2)}) collective-permute-start(bf16[16,128,256]{2,1,0:T(8,128)(2,1)S(1)} %all_to_all.16.own_ref), channel_id=1, source_target_pairs={{0,4},{4,0},{1,5},{5,1},{2,6},{6,2},{3,7},{7,3},{8,12},{12,8},{9,1... | collective-permute-start | bytes 3145736 | tf_op jit(solution)/shard_map/ppermute | solution.py:342
  68.3 1.0 copy-start.1
  69.2 2.9 %collective-permute-start.4 = (bf16[64,8,896]{2,1,0:T(8,128)(2,1)}, bf16[64,8,896]{2,1,0:T(8,128)(2,1)}, u32[]{:S(2)}, u32[]{:S(2)}) collective-permute-start(bf16[64,8,896]{2,1,0:T(8,128)(2,1)} %get-tuple-element.14), channel_id=1, source_target_pairs={{0,4},{4,0},{1,5},{5,1},{2,6},{6,2},{3,7},{7,3},{8,12},{12,8},{9,1... | collective-permute-start | bytes 2752520 | tf_op jit(solution)/shard_map/ppermute | solution.py:346

commit v3 on v2

--- a/solution.py
+++ b/solution.py
@@ -24,17 +24,26 @@
 SWAP = [(0, 1), (1, 0)]
 
 
-def attention_kernel(len_ref, qn_ref, qr_ref, res_ref, routes_ref, ints_ref, wa_hbm, lat_hbm, rope_hbm, wv_hbm, out_ref,
-                     wa, wv, lat, rope, qs, qps, os, ext, sem_w, sem_l, sem_r, *, span, sides, experts):
+def attention_kernel(len_hbm, routes_hbm, ints_hbm, qn_hbm, qr_hbm, res_hbm, wa_hbm, lat_hbm, rope_hbm, wv_hbm, out_ref,
+                     len_ref, routes_ref, ints_ref, qn_ref, qr_ref, res_ref, sem_in, wa, wv, lat, rope, qs, qps, os, ext, sc, sem_w, sem_l, sem_r, *, span, ahead, sides, experts):
     reqs, length, width = lat_hbm.shape
     heads = wa_hbm.shape[0]
-    toks = qn_ref.shape[0]
+    toks = qn_hbm.shape[0]
     qpr = toks // reqs
     rows = qpr * heads
     spans = length // span
     lanes = width // 128
     scale = (NOPE + ROPE) ** (-0.5)
     absorb = pltpu.make_async_copy(wa_hbm, wa, sem_w.at[0])
+    small = [
+        pltpu.make_async_copy(a, b, sem_in.at[k])
+        for k, (a, b) in enumerate((
+            (len_hbm, len_ref), (routes_hbm, routes_ref), (ints_hbm, ints_ref),
+            (qn_hbm, qn_ref), (qr_hbm, qr_ref), (res_hbm, res_ref),
+        ))
+    ]
+    for copy in small:
+        copy.start()
     absorb.start()
     value = pltpu.make_async_copy(wv_hbm, wv, sem_w.at[1])
 
@@ -45,17 +54,28 @@
             pltpu.make_async_copy(rope_hbm.at[r, :, at], rope.at[r, :, at], sem_r.at[r * spans + i]),
         )
 
-    for r in range(reqs):
-        for i in range(spans):
-            def begin(r=r, i=i):
+    chunks = [(r, i) for r in range(reqs) for i in range(spans)]
+
+    def begin(k):
+        if k == len(chunks):
+            value.start(priority=1)
+        elif k < len(chunks):
+            r, i = chunks[k]
+
+            def go():
                 for copy in copies(r, i):
-                    copy.start()
+                    copy.start(priority=1)
 
             if i == 0:
-                begin()
+                go()
             else:
-                pl.when(i * span < len_ref[r])(begin)
-    value.start()
+                pl.when(i * span < len_ref[r])(go)
+
+    begin(0)
+    for copy in small:
+        copy.wait()
+    for k in range(1, ahead):
+        begin(k)
     planes = out_ref.shape[0]
     cores = 2
     n_val = heads * VDIM
@@ -95,31 +115,33 @@
         rotary = qps[at, :ROPE].astype(BF)
         filled = len_ref[r]
         limit = filled - qpr + lax.broadcasted_iota(jnp.int32, (rows, 1), 0) // heads
-
-        def step(i, old, r=r, query=query, rotary=rotary, limit=limit):
-            for copy in copies(r, i):
-                copy.wait()
-            keys = lat[r, pl.ds(i * span, span), :]
-            s = lax.dot_general(query, keys, (((1,), (1,)), ((), ())), preferred_element_type=F32)
-            s = s + jnp.dot(rotary, rope[r, :, pl.ds(i * span, span)], preferred_element_type=F32)
-            position = i * span + lax.broadcasted_iota(jnp.int32, (rows, span), 1)
-            s = jnp.where(position <= limit, s * scale, -jnp.inf)
-            top = jnp.max(s, axis=1, keepdims=True)
-            if old is not None:
-                top = jnp.maximum(old[0], top)
-            p = jnp.exp(s - top)
-            norm = jnp.sum(p, axis=1, keepdims=True)
-            acc = jnp.dot(p.astype(BF), keys, preferred_element_type=F32)
-            if old is not None:
-                fade = jnp.exp(old[0] - top)
-                norm = norm + fade * old[1]
-                acc = acc + fade * old[2]
-            return top, norm, acc
-
-        state = step(0, None)
+        for i in range(spans):
+            begin(r * spans + i + ahead)
+            to = pl.ds(i * span, span)
+
+            def score(r=r, i=i, to=to, query=query, rotary=rotary):
+                for copy in copies(r, i):
+                    copy.wait()
+                s = lax.dot_general(query, lat[r, to, :], (((1,), (1,)), ((), ())), preferred_element_type=F32)
+                sc[:, to] = (s + jnp.dot(rotary, rope[r, :, to], preferred_element_type=F32)) * scale
+
+            if i == 0:
+                score()
+            else:
+                pl.when(i * span < filled)(score)
+        position = lax.broadcasted_iota(jnp.int32, (rows, length), 1)
+        s = jnp.where(position <= limit, sc[...], -jnp.inf)
+        p = jnp.exp(s - jnp.max(s, axis=1, keepdims=True))
+        norm = jnp.sum(p, axis=1, keepdims=True)
+        p = p.astype(BF)
+        acc = jnp.dot(p[:, :span], lat[r, pl.ds(0, span), :], preferred_element_type=F32)
         for i in range(1, spans):
-            state = lax.cond(i * span < filled, functools.partial(step, i), lambda old: old, state)
-        result = state[2] / state[1]
+            def add(old, r=r, i=i, p=p):
+                return old + jnp.dot(p[:, i * span:(i + 1) * span], lat[r, pl.ds(i * span, span), :],
+                                     preferred_element_type=F32)
+
+            acc = lax.cond(i * span < filled, add, lambda old: old, acc)
+        result = acc / norm
         for c in range(lanes):
             os[c, at, :] = result[:, c * 128:(c + 1) * 128]
     value.wait()
@@ -132,20 +154,26 @@
 
 
 def attention(q_nope, q_rope, w_absorb, cache_latent, cache_rope, lengths, w_value, residual, routes, gate_int,
-              planes, sides, experts, span=2048):
+              planes, sides, experts, span=2048, ahead=5):
     reqs, length, width = cache_latent.shape
     spans = length // span
     heads = w_absorb.shape[0]
     toks = q_nope.shape[0]
     hbm = pl.BlockSpec(memory_space=pltpu.HBM)
     vmem = pl.BlockSpec(memory_space=pltpu.VMEM)
-    smem = pl.BlockSpec(memory_space=pltpu.SMEM)
     return pl.pallas_call(
-        functools.partial(attention_kernel, span=span, sides=sides, experts=experts),
-        out_shape=jax.ShapeDtypeStruct((planes, toks, heads * VDIM + 256), BF),
-        in_specs=[smem] + [vmem] * 3 + [smem] * 2 + [hbm] * 4,
+        functools.partial(attention_kernel, span=span, ahead=ahead, sides=sides, experts=experts),
+        out_shape=pltpu.VMEM((planes, toks, heads * VDIM + 256), BF),
+        in_specs=[hbm] * 10,
         out_specs=vmem,
         scratch_shapes=[
+            pltpu.SMEM(lengths.shape, jnp.int32),
+            pltpu.SMEM(routes.shape, jnp.int32),
+            pltpu.SMEM(gate_int.shape, jnp.int32),
+            pltpu.VMEM(q_nope.shape, BF),
+            pltpu.VMEM(q_rope.shape, BF),
+            pltpu.VMEM(residual.shape, BF),
+            pltpu.SemaphoreType.DMA((6,)),
             pltpu.VMEM(w_absorb.shape, BF),
             pltpu.VMEM(w_value.shape, BF),
             pltpu.VMEM(cache_latent.shape, BF),
@@ -154,13 +182,17 @@
             pltpu.VMEM((toks * heads, 2 * ROPE), F32),
             pltpu.VMEM((width // 128, toks * heads, 128), F32),
             pltpu.VMEM((planes, toks, 256), F32),
+            pltpu.VMEM((toks * heads // reqs, length), F32),
             pltpu.SemaphoreType.DMA((2,)),
             pltpu.SemaphoreType.DMA((reqs * spans,)),
             pltpu.SemaphoreType.DMA((reqs * spans,)),
         ],
-        compiler_params=pltpu.CompilerParams(vmem_limit_bytes=60 * 1024 * 1024),
+        compiler_params=pltpu.CompilerParams(vmem_limit_bytes=20 * 1024 * 1024),
         name="attention",
-    )(lengths, q_nope, q_rope, residual, routes, gate_int, w_absorb, cache_latent, cache_rope, w_value)
+    )(*(
+        pltpu.with_memory_space_constraint(a, pltpu.HBM)
+        for a in (lengths, routes, gate_int, q_nope, q_rope, residual, w_absorb, cache_latent, cache_rope, w_value)
+    ))
 
 
 def half_copies(wg_hbm, wu_hbm, wg, wu, sem, part, stripes):
@@ -202,7 +234,19 @@
     return acc, jnp.sum(square, axis=-1, keepdims=True)
 
 
-def first_kernel(own_ref, gain_ref, wg_hbm, wu_hbm, acc_ref, sq_ref, wg, wu, sem):
+def pick_rows(blocks_ref, kept_ref, base):
+    sides, toks, _ = kept_ref.shape
+    at = base + (lax.axis_index("y") * sides + lax.axis_index("side")) * toks
+    group = pl.multiple_of(at // 16 * 16, 16)
+    for s in range(sides):
+        rows = blocks_ref[lax.axis_index("hg") * sides + s, pl.ds(group, 16), :].astype(F32)
+        found = rows[:toks]
+        for k in range(1, 16 // toks):
+            found = jnp.where(at - group == k * toks, rows[k * toks:(k + 1) * toks], found)
+        kept_ref[s] = found.astype(BF)
+
+
+def first_kernel(own_ref, gain_ref, wg_hbm, wu_hbm, acc_ref, sq_ref, kept_ref, wg, wu, sem):
     experts, depth, units = wg_hbm.shape
     rows = own_ref.shape[1]
     core = lax.axis_index("c")
@@ -215,9 +259,10 @@
     for e in range(experts):
         acc_ref[e] = acc[e]
     sq_ref[...] = square
-
-
-def second_kernel(oth_ref, gain_ref, share_ref, acc_ref, sq_ref, wg_hbm, wu_hbm, wd_hbm, keep_ref, send_ref,
+    pick_rows(own_ref, kept_ref, 0)
+
+
+def second_kernel(oth_ref, gain_ref, share_ref, acc_ref, sq_ref, wg_hbm, wu_hbm, wd_hbm, keep_ref, send_ref, kept_ref,
                   wg, wu, wd, sem, sem_down):
     experts, depth, units = wg_hbm.shape
     blocks, rows, _ = oth_ref.shape
@@ -243,6 +288,7 @@
         act = gate / (1.0 + jnp.exp(-gate)) * up
         acts.append(jnp.where(share > 0, act * share, 0.0).astype(BF))
     act = jnp.concatenate(acts, axis=1)
+    pick_rows(oth_ref, kept_ref, half)
     for copy in downs:
         copy.wait()
     messages, lines, tile = keep_ref.shape
@@ -256,7 +302,7 @@
                 ref[n * blocks + k] = jnp.concatenate([left[at], right[at]], axis=0).astype(BF)
 
 
-def own_half(own, gain, w_gate, w_up):
+def own_half(own, gain, w_gate, w_up, toks):
     experts, depth, units = w_gate.shape
     rows = own.shape[1]
     vmem = pl.BlockSpec(memory_space=pltpu.VMEM)
@@ -264,15 +310,19 @@
     w_gate, w_up = (pltpu.with_memory_space_constraint(a, pltpu.HBM) for a in (w_gate, w_up))
     return pl.pallas_call(
         first_kernel,
-        out_shape=(jax.ShapeDtypeStruct((experts, rows, 2 * units), F32), jax.ShapeDtypeStruct((rows, 1), F32)),
+        out_shape=(
+            jax.ShapeDtypeStruct((experts, rows, 2 * units), F32),
+            jax.ShapeDtypeStruct((rows, 1), F32),
+            jax.ShapeDtypeStruct((gain.shape[1], toks, own.shape[2]), BF),
+        ),
         in_specs=[vmem] * 2 + [hbm] * 2,
-        out_specs=[vmem] * 2,
+        out_specs=[vmem] * 3,
         scratch_shapes=[
             pltpu.VMEM((experts, depth // 2, units), BF),
             pltpu.VMEM((experts, depth // 2, units), BF),
             pltpu.SemaphoreType.DMA((gain.shape[0] * experts,)),
         ],
-        compiler_params=pltpu.CompilerParams(vmem_limit_bytes=16 * 1024 * 1024),
+        compiler_params=pltpu.CompilerParams(vmem_limit_bytes=12 * 1024 * 1024),
         cost_estimate=pl.CostEstimate(flops=rows * depth * 512, bytes_accessed=5_000_000, transcendentals=0),
         name="experts_first",
     )(own, gain, w_gate, w_up)
@@ -287,9 +337,9 @@
     w_gate, w_up, w_down = (pltpu.with_memory_space_constraint(a, pltpu.HBM) for a in (w_gate, w_up, w_down))
     return pl.pallas_call(
         second_kernel,
-        out_shape=(shape, shape),
+        out_shape=(shape, shape, jax.ShapeDtypeStruct((gain.shape[1], rows // 2 // blocks, oth.shape[2]), BF)),
         in_specs=[vmem] * 5 + [hbm] * 3,
-        out_specs=[vmem] * 2,
+        out_specs=[vmem] * 3,
         scratch_shapes=[
             pltpu.VMEM((experts, depth // 2, units), BF),
             pltpu.VMEM((experts, depth // 2, units), BF),
@@ -297,7 +347,7 @@
             pltpu.SemaphoreType.DMA((gain.shape[0] * experts,)),
             pltpu.SemaphoreType.DMA((experts,)),
         ],
-        compiler_params=pltpu.CompilerParams(vmem_limit_bytes=24 * 1024 * 1024),
+        compiler_params=pltpu.CompilerParams(vmem_limit_bytes=18 * 1024 * 1024),
         cost_estimate=pl.CostEstimate(flops=rows * depth * 1024, bytes_accessed=10_000_000, transcendentals=0),
         name="experts_second",
     )(oth, gain, share, acc, square, w_gate, w_up, w_down)
@@ -335,21 +385,19 @@
     is_row = (jnp.arange(toks) == hg)[None, :, None]
     partial = (partial + jnp.where(is_row, mine.astype(F32), 0.0)).astype(BF).reshape(-1, cols)
     partial = jnp.pad(partial, ((0, 0), (0, -cols % 128)))
-    pair = (partial.astype(F32) + lax.ppermute(partial, "hg", PAIRS_A).astype(F32)).astype(BF)
+    gain = norm_gain.astype(F32).reshape(ys * cores, sides, cols)
+    other, share, gain = lax.optimization_barrier((lax.ppermute(partial, "hg", PAIRS_A), share, gain))
+    pair = (partial.astype(F32) + other.astype(F32)).astype(BF)
     hidden = (pair.astype(F32) + lax.ppermute(pair, "hg", PAIRS_B).astype(F32)).astype(BF)
 
     own = lax.all_to_all(jnp.broadcast_to(hidden[None], (planes,) + hidden.shape), ("y", "side"), 0, 0, tiled=True)
     oth = lax.ppermute(own, "c", SWAP)
-    gain = norm_gain.astype(F32).reshape(ys * cores, sides, cols)
-    acc, square = own_half(own, gain, w_gate, w_up)
-    keep, send = other_half(oth, gain, share, acc, square, w_gate, w_up, w_down, hgs)
+    acc, square, own_piece = own_half(own, gain, w_gate, w_up, toks)
+    keep, send, oth_piece = other_half(oth, gain, share, acc, square, w_gate, w_up, w_down, hgs)
     got = lax.ppermute(send, "c", SWAP)
     quarter = width // hgs
     summed = keep + got
-    at = (y * sides + side) * toks
-    half = planes * toks
-    own_piece = lax.dynamic_slice(own, (hg * sides, at, 0), (sides, toks, cols))
-    oth_piece = lax.dynamic_slice(oth, (hg * sides, half + at, 0), (sides, toks, cols))
+    own_piece, oth_piece = own_piece[..., :cols], oth_piece[..., :cols]
     low = jnp.where(core == 0, own_piece, oth_piece)
     high = jnp.where(core == 0, oth_piece, own_piece)
     kept = jnp.concatenate([low, high], axis=0).transpose(1, 0, 2).reshape(toks, quarter)

time: 98.8 us -> 92.7 us (0.938)
  Pallas kernels: 17.3 us -> 12.6 us
  other arithmetic: 4.02 us -> 3.01 us
    pallas_call x2, Pallas kernels: 14.7 us -> 10 us  [the longest x1 5.7 us: attention(): pl.pallas_call(functools.partial(attention_kernel, span=span, ahead=ahead...]
  transfers between devices with their start and end apart: 5 -> 5, of which waited for: 4 -> 5; matrix products, arithmetic and copies ran while one was open for 1% -> 0% of each run, Pallas kernels for 3% -> 3%
where the time goes in v3:
time: 92.7 us; the launch traced here: 92.4 us
  blocking collectives  61.6 us (66%)
  Pallas kernels  12.6 us (14%)
  waiting for transfers between devices  8.99 us (10%)
  starting transfers between devices  4.92 us (5%)
  other arithmetic  3.01 us (3%)
    all_to_all x1, blocking collectives, body(): parts = lax.all_to_all(summed, ('hg', 'y', 'side'), 0, 0, tiled=True)  24.1 us
    all_to_all x1, blocking collectives, body(): here = lax.all_to_all(message, ('y', 'side'), 0, 0, tiled=True)  19 us
    all_to_all x1, blocking collectives, body(): lax.all_to_all(jnp.broadcast_to(hidden[None], (planes,) + hidden.shape),...  18.6 us
    pallas_call x1, Pallas kernels, attention(): pl.pallas_call(functools.partial(attention_kernel, span=span, ahead=ahead...  5.7 us
    pallas_call x1, Pallas kernels, other_half(): pl.pallas_call(second_kernel, out_shape=(shape, shape, jax.ShapeDtypeStru...  4.33 us
    ppermute x1, starting transfers between devices, body(): lax.ppermute(pair, 'hg', PAIRS_B).astype(F32)  2.84 us
    ppermute x1, waiting for transfers between devices, body(): lax.ppermute(pair, 'hg', PAIRS_B).astype(F32)  2.72 us
    ppermute x1, waiting for transfers between devices, body(): lax.ppermute(partial, 'hg', PAIRS_A)  2.67 us
  transfers between devices with their start and end apart: 5, of which 5 were waited for; matrix products, arithmetic and copies ran while one was open for 0% of the time, Pallas kernels for 3%

profile of v3, /device:TPU:0, one launch (start us, length us, event | category | flops | bytes accessed | tf_op | source)
XLA Modules:
  0.0 92.4 jit_solution(952700664141320129)
XLA Ops:
  0.0 0.0 copy-start
  0.0 0.0 copy-start.1
  0.0 5.7 %attention.1 = bf16[16,4,2304]{2,1,0:T(4,128)(2,1)S(1)} custom-call(s32[2]{0:T(128)} %len_hbm.1, s32[4,4]{1,0:T(4,128)} %routes_hbm.1, s32[4,4]{1,0:T(4,128)} %ints_hbm.1, bf16[4,2048]{1,0:T(4,128)(2,1)} %qn_hbm.1, bf16[4,1024]{1,0:T(4,128)(2,1)} %qr_hbm.1, bf16[4,7168]{1,0:T(4,128)(2,1)} %res_hbm.1, bf16[16,128,512]{2,1,0:T(8,128)(2,1)} %wa_hbm.1, ...), custom_call_target="tpu_custom_call" | custom-call | tf_op jit(solution)/shard_map/attention/pallas_call | solution.py:164
  5.7 19.0 %all_to_all.15 = bf16[16,4,2304]{2,1,0:T(4,128)(2,1)S(1)} all-to-all(bf16[16,4,2304]{2,1,0:T(4,128)(2,1)S(1)} %attention.1), channel_id=1, replica_groups=mesh['hg'=4,'y'=4,'c'=2,'side'=4] {'y','side'}, dimensions={0} | all-to-all | bytes 589824 | tf_op jit(solution)/shard_map/all_to_all | solution.py:370
  24.7 0.0 collective-permute-start
  24.7 0.0 copy-done.1
  24.7 0.1 reshape.39.gain_ref
  24.9 1.4 %collective-permute-done = bf16[16,4,2304]{2,1,0:T(4,128)(2,1)S(1)} collective-permute-done((bf16[16,4,2304]{2,1,0:T(4,128)(2,1)S(1)}, bf16[16,4,2304]{2,1,0:T(4,128)(2,1)S(1)}, u32[]{:S(2)}, u32[]{:S(2)}) %collective-permute-start) | collective-permute-done | bytes 294944 | tf_op jit(solution)/shard_map/ppermute | solution.py:371
  26.3 0.1 fusion.6
  26.4 0.4 fusion.2
  26.8 0.1 reshape.37
  26.8 0.1 reduce_sum.18
  27.0 0.1 dynamic-slice_convert_fusion
  27.1 0.0 copy-done
  27.1 0.6 fusion
  27.7 0.1 copy.18
  27.8 1.6 %collective-permute-start.1 = (bf16[128,256]{1,0:T(8,128)(2,1)S(1)}, bf16[128,256]{1,0:T(8,128)(2,1)S(1)}, u32[]{:S(2)}, u32[]{:S(2)}) collective-permute-start(bf16[128,256]{1,0:T(8,128)(2,1)S(1)} %pad.4), channel_id=1, source_target_pairs={{0,32},{32,0},{64,96},{96,64},{1,33},{33,1},{65,97},{97,65},{2,34}... | collective-permute-start | bytes 196616 | tf_op jit(solution)/shard_map/ppermute | solution.py:389
  29.4 0.1 dynamic-slice_multiply_fusion.share_ref
  29.5 2.7 %collective-permute-done.1 = bf16[128,256]{1,0:T(8,128)(2,1)S(1)} collective-permute-done((bf16[128,256]{1,0:T(8,128)(2,1)S(1)}, bf16[128,256]{1,0:T(8,128)(2,1)S(1)}, u32[]{:S(2)}, u32[]{:S(2)}) %collective-permute-start.1) | collective-permute-done | bytes 65568 | tf_op jit(solution)/shard_map/ppermute | solution.py:389
  32.2 2.8 %collective-permute-start.2 = (bf16[128,256]{1,0:T(8,128)(2,1)S(1)}, bf16[128,256]{1,0:T(8,128)(2,1)S(1)}, u32[]{:S(2)}, u32[]{:S(2)}) collective-permute-start(bf16[128,256]{1,0:T(8,128)(2,1)S(1)} %add_convert_fusion.1), channel_id=1, source_target_pairs={{32,64},{64,32},{96,0},{0,96},{33,65},{65,33},{97,1},{1,97},{34,66... | collective-permute-start | bytes 196616 | tf_op jit(solution)/shard_map/ppermute | solution.py:391
  35.0 2.7 %collective-permute-done.2 = bf16[128,256]{1,0:T(8,128)(2,1)S(1)} collective-permute-done((bf16[128,256]{1,0:T(8,128)(2,1)S(1)}, bf16[128,256]{1,0:T(8,128)(2,1)S(1)}, u32[]{:S(2)}, u32[]{:S(2)}) %collective-permute-start.2) | collective-permute-done | bytes 65568 | tf_op jit(solution)/shard_map/ppermute | solution.py:391
  37.8 0.1 broadcast_in_dim.32
  37.9 18.6 %all_to_all.16.own_ref = bf16[16,128,256]{2,1,0:T(8,128)(2,1)S(1)} all-to-all(bf16[16,128,256]{2,1,0:T(8,128)(2,1)S(1)} %broadcast_in_dim.32), channel_id=1, replica_groups=mesh['hg'=4,'y'=4,'c'=2,'side'=4] {'y','side'}, dimensions={0} | all-to-all | bytes 2097152 | tf_op jit(solution)/shard_map/all_to_all | solution.py:393
  56.4 0.0 collective-permute-start.3
  56.4 2.6 %experts_first.1 = (f32[2,128,256]{2,1,0:T(8,128)S(1)}, f32[128,1]{1,0:T(8,128)S(1)}, bf16[4,4,256]{2,1,0:T(4,128)(2,1)S(1)}) custom-call(bf16[16,128,256]{2,1,0:T(8,128)(2,1)S(1)} %all_to_all.16.own_ref, f32[8,4,224]{2,1,0:T(4,128)S(1)} %reshape.39.gain_ref, bf16[2,7168,128]{2,1,0:T(8,128)(2,1)} %wg_hbm.3, bf16[2,7168,128]{2,1,0:T(8,128)(2,1)} %wu_hbm.3), custom_call_target="tpu_custom_call" | custom-call | flops 469762048 | bytes 5000000 | tf_op jit(solution)/shard_map/experts_first/pallas_call | solution.py:311
  59.0 0.1 collective-permute-done.3.oth_ref
  59.1 4.3 %experts_second.1 = (bf16[64,8,896]{2,1,0:T(8,128)(2,1)S(1)}, bf16[64,8,896]{2,1,0:T(8,128)(2,1)S(1)}, bf16[4,4,256]{2,1,0:T(4,128)(2,1)S(1)}) custom-call(bf16[16,128,256]{2,1,0:T(8,128)(2,1)S(1)} %collective-permute-done.3.oth_ref, f32[8,4,224]{2,1,0:T(4,128)S(1)} %reshape.39.gain_ref, f32[128,2]{1,0:T(8,128)S(1)} %dynamic-slice_multiply_fusion.share_ref, ...), custom_call_target="tpu_custom_call" | custom-call | flops 939524096 | bytes 10000000 | tf_op jit(solution)/shard_map/experts_second/pallas_call | solution.py:338
  63.4 0.5 collective-permute-start.4
  64.0 0.1 reshape.36
  64.1 2.1 %collective-permute-done.4 = bf16[64,8,896]{2,1,0:T(8,128)(2,1)} collective-permute-done((bf16[64,8,896]{2,1,0:T(8,128)(2,1)S(1)}, bf16[64,8,896]{2,1,0:T(8,128)(2,1)}, u32[]{:S(2)}, u32[]{:S(2)}) %collective-permute-start.4) | collective-permute-done | bytes 917536 | tf_op jit(solution)/shard_map/ppermute | solution.py:397
  66.2 1.4 %add.41 = bf16[64,8,896]{2,1,0:T(8,128)(2,1)S(1)} add(bf16[64,8,896]{2,1,0:T(8,128)(2,1)S(1)} %get-tuple-element.21, bf16[64,8,896]{2,1,0:T(8,128)(2,1)} %collective-permute-done.4) | non-fusion elementwise | flops 458752 | bytes 2752512 | tf_op jit(solution)/shard_map/add | solution.py:399
  67.6 24.1 %all_to_all.17 = bf16[64,8,896]{2,1,0:T(8,128)(2,1)S(1)} all-to-all(bf16[64,8,896]{2,1,0:T(8,128)(2,1)S(1)} %add.41), channel_id=1, replica_groups=mesh['hg'=4,'y'=4,'c'=2,'side'=4] {'hg','y','side'}, dimensions={0} | all-to-all | bytes 1835008 | tf_op jit(solution)/shard_map/all_to_all | solution.py:405
  91.6 0.2 convert_reduce_fusion
  91.8 0.6 fusion.4
  (14 shorter events, 0.2 us)
Async XLA Ops:
  0.0 27.1 %copy-start = (bf16[2048,224]{0,1:T(8,128)(2,1)S(1)}, bf16[2048,224]{0,1:T(8,128)(2,1)}, u32[]{:S(2)}) copy-start(bf16[2048,224]{0,1:T(8,128)(2,1)} %param.22) | copy-start | bytes 2752516
  0.0 24.7 %copy-start.1 = (bf16[7168]{0:T(1024)(128)(2,1)S(1)}, bf16[7168]{0:T(1024)(128)(2,1)}, u32[]{:S(2)}) copy-start(bf16[7168]{0:T(1024)(128)(2,1)} %param.24) | copy-start | bytes 43012
  24.7 1.6 %collective-permute-start = (bf16[16,4,2304]{2,1,0:T(4,128)(2,1)S(1)}, bf16[16,4,2304]{2,1,0:T(4,128)(2,1)S(1)}, u32[]{:S(2)}, u32[]{:S(2)}) collective-permute-start(bf16[16,4,2304]{2,1,0:T(4,128)(2,1)S(1)} %all_to_all.15), channel_id=1, source_target_pairs={{0,4},{4,0},{1,5},{5,1},{2,6},{6,2},{3,7},{7,3},{8,12},{12,8},{9,1... | collective-permute-start | bytes 884744 | tf_op jit(solution)/shard_map/ppermute | solution.py:371
  27.8 4.3 %collective-permute-start.1 = (bf16[128,256]{1,0:T(8,128)(2,1)S(1)}, bf16[128,256]{1,0:T(8,128)(2,1)S(1)}, u32[]{:S(2)}, u32[]{:S(2)}) collective-permute-start(bf16[128,256]{1,0:T(8,128)(2,1)S(1)} %pad.4), channel_id=1, source_target_pairs={{0,32},{32,0},{64,96},{96,64},{1,33},{33,1},{65,97},{97,65},{2,34}... | collective-permute-start | bytes 196616 | tf_op jit(solution)/shard_map/ppermute | solution.py:389
  32.2 5.6 %collective-permute-start.2 = (bf16[128,256]{1,0:T(8,128)(2,1)S(1)}, bf16[128,256]{1,0:T(8,128)(2,1)S(1)}, u32[]{:S(2)}, u32[]{:S(2)}) collective-permute-start(bf16[128,256]{1,0:T(8,128)(2,1)S(1)} %add_convert_fusion.1), channel_id=1, source_target_pairs={{32,64},{64,32},{96,0},{0,96},{33,65},{65,33},{97,1},{1,97},{34,66... | collective-permute-start | bytes 196616 | tf_op jit(solution)/shard_map/ppermute | solution.py:391
  56.4 2.7 %collective-permute-start.3 = (bf16[16,128,256]{2,1,0:T(8,128)(2,1)S(1)}, bf16[16,128,256]{2,1,0:T(8,128)(2,1)S(1)}, u32[]{:S(2)}, u32[]{:S(2)}) collective-permute-start(bf16[16,128,256]{2,1,0:T(8,128)(2,1)S(1)} %all_to_all.16.own_ref), channel_id=1, source_target_pairs={{0,4},{4,0},{1,5},{5,1},{2,6},{6,2},{3,7},{7,3},{8,12},{12,8},{9,1... | collective-permute-start | bytes 3145736 | tf_op jit(solution)/shard_map/ppermute | solution.py:394
  63.4 2.7 %collective-permute-start.4 = (bf16[64,8,896]{2,1,0:T(8,128)(2,1)S(1)}, bf16[64,8,896]{2,1,0:T(8,128)(2,1)}, u32[]{:S(2)}, u32[]{:S(2)}) collective-permute-start(bf16[64,8,896]{2,1,0:T(8,128)(2,1)S(1)} %get-tuple-element.22), channel_id=1, source_target_pairs={{0,4},{4,0},{1,5},{5,1},{2,6},{6,2},{3,7},{7,3},{8,12},{12,8},{9,1... | collective-permute-start | bytes 2752520 | tf_op jit(solution)/shard_map/ppermute | solution.py:397

commit v4 on v3

--- a/solution.py
+++ b/solution.py
@@ -109,41 +109,44 @@
         latent = jnp.dot(qn_ref[:, h * NOPE:(h + 1) * NOPE], wa[h], preferred_element_type=F32)
         for c in range(lanes):
             qs[c, pl.ds(h, toks, stride=heads), :] = latent[:, c * 128:(c + 1) * 128]
-    for r in range(reqs):
+    def scores(r, count):
         at = pl.ds(r * rows, rows)
         query = jnp.concatenate([qs[c, at, :] for c in range(lanes)], axis=1).astype(BF)
         rotary = qps[at, :ROPE].astype(BF)
-        filled = len_ref[r]
-        limit = filled - qpr + lax.broadcasted_iota(jnp.int32, (rows, 1), 0) // heads
-        for i in range(spans):
-            begin(r * spans + i + ahead)
+        limit = len_ref[r] - qpr + lax.broadcasted_iota(jnp.int32, (rows, 1), 0) // heads
+        out = []
+        for i in range(count):
             to = pl.ds(i * span, span)
-
-            def score(r=r, i=i, to=to, query=query, rotary=rotary):
-                for copy in copies(r, i):
-                    copy.wait()
-                s = lax.dot_general(query, lat[r, to, :], (((1,), (1,)), ((), ())), preferred_element_type=F32)
-                sc[:, to] = (s + jnp.dot(rotary, rope[r, :, to], preferred_element_type=F32)) * scale
-
-            if i == 0:
-                score()
-            else:
-                pl.when(i * span < filled)(score)
-        position = lax.broadcasted_iota(jnp.int32, (rows, length), 1)
-        s = jnp.where(position <= limit, sc[...], -jnp.inf)
-        p = jnp.exp(s - jnp.max(s, axis=1, keepdims=True))
-        norm = jnp.sum(p, axis=1, keepdims=True)
-        p = p.astype(BF)
-        acc = jnp.dot(p[:, :span], lat[r, pl.ds(0, span), :], preferred_element_type=F32)
-        for i in range(1, spans):
-            def add(old, r=r, i=i, p=p):
-                return old + jnp.dot(p[:, i * span:(i + 1) * span], lat[r, pl.ds(i * span, span), :],
-                                     preferred_element_type=F32)
-
-            acc = lax.cond(i * span < filled, add, lambda old: old, acc)
+            for copy in copies(r, i):
+                copy.wait()
+            s = lax.dot_general(query, lat[r, to, :], (((1,), (1,)), ((), ())), preferred_element_type=F32)
+            s = (s + jnp.dot(rotary, rope[r, :, to], preferred_element_type=F32)) * scale
+            position = i * span + lax.broadcasted_iota(jnp.int32, (rows, span), 1)
+            out.append(jnp.where(position <= limit, s, -jnp.inf))
+        return out
+
+    def mix(r, s):
+        top = functools.reduce(jnp.maximum, [jnp.max(x, axis=1, keepdims=True) for x in s])
+        p = [jnp.exp(x - top) for x in s]
+        norm = sum(jnp.sum(x, axis=1, keepdims=True) for x in p)
+        acc = sum(
+            jnp.dot(x.astype(BF), lat[r, pl.ds(i * span, span), :], preferred_element_type=F32)
+            for i, x in enumerate(p)
+        )
         result = acc / norm
         for c in range(lanes):
-            os[c, at, :] = result[:, c * 128:(c + 1) * 128]
+            os[c, pl.ds(r * rows, rows), :] = result[:, c * 128:(c + 1) * 128]
+
+    def attend(first, second):
+        one = scores(0, first)
+        two = scores(1, second)
+        mix(0, one)
+        mix(1, two)
+
+    counts = [(len_ref[r] + span - 1) // span for r in range(reqs)]
+    for first in range(1, spans + 1):
+        for second in range(1, spans + 1):
+            pl.when((counts[0] == first) & (counts[1] == second))(functools.partial(attend, first, second))
     value.wait()
     for h in range(heads):
         at = pl.ds(h, toks, stride=heads)
@@ -182,7 +185,7 @@
             pltpu.VMEM((toks * heads, 2 * ROPE), F32),
             pltpu.VMEM((width // 128, toks * heads, 128), F32),
             pltpu.VMEM((planes, toks, 256), F32),
-            pltpu.VMEM((toks * heads // reqs, length), F32),
+            pltpu.VMEM((reqs, toks * heads // reqs, length), F32),
             pltpu.SemaphoreType.DMA((2,)),
             pltpu.SemaphoreType.DMA((reqs * spans,)),
             pltpu.SemaphoreType.DMA((reqs * spans,)),
@@ -262,7 +265,7 @@
     pick_rows(own_ref, kept_ref, 0)
 
 
-def second_kernel(oth_ref, gain_ref, share_ref, acc_ref, sq_ref, wg_hbm, wu_hbm, wd_hbm, keep_ref, send_ref, kept_ref,
+def second_kernel(oth_ref, gain_ref, share_ref, acc_ref, sq_ref, wg_hbm, wu_hbm, wd_hbm, keep_ref, low_ref, high_ref, kept_ref,
                   wg, wu, wd, sem, sem_down):
     experts, depth, units = wg_hbm.shape
     blocks, rows, _ = oth_ref.shape
@@ -277,7 +280,7 @@
         for copy in group:
             copy.start()
     for copy in downs:
-        copy.start()
+        copy.start(priority=1)
     acc, square = half_products(oth_ref, gain_ref, wg, wu, groups, part, [acc_ref[e] for e in range(experts)], True)
     inverse = lax.rsqrt((square + sq_ref[...]) / depth + EPS)
     acts = []
@@ -297,9 +300,11 @@
         left = jnp.dot(act, wd[:, 2 * n * tile:(2 * n + 1) * tile], preferred_element_type=F32)
         right = jnp.dot(act, wd[:, (2 * n + 1) * tile:(2 * n + 2) * tile], preferred_element_type=F32)
         for k in range(blocks):
-            for ref, base in ((keep_ref, 0), (send_ref, half)):
-                at = slice(base + k * toks, base + (k + 1) * toks)
-                ref[n * blocks + k] = jnp.concatenate([left[at], right[at]], axis=0).astype(BF)
+            at = slice(k * toks, (k + 1) * toks)
+            keep_ref[n * blocks + k] = jnp.concatenate([left[at], right[at]], axis=0).astype(BF)
+            at = slice(half + k * toks, half + (k + 1) * toks)
+            send_ref, place = (low_ref, n) if n * blocks < low_ref.shape[0] else (high_ref, n - low_ref.shape[0] // blocks)
+            send_ref[place * blocks + k] = jnp.concatenate([left[at], right[at]], axis=0).astype(BF)
 
 
 def own_half(own, gain, w_gate, w_up, toks):
@@ -332,14 +337,15 @@
     experts, depth, units = w_gate.shape
     blocks, rows, _ = oth.shape
     shape = jax.ShapeDtypeStruct((hgs * blocks, rows // blocks, depth // hgs // 2), BF)
+    part = jax.ShapeDtypeStruct((hgs * blocks // 2,) + shape.shape[1:], BF)
     vmem = pl.BlockSpec(memory_space=pltpu.VMEM)
     hbm = pl.BlockSpec(memory_space=pltpu.HBM)
     w_gate, w_up, w_down = (pltpu.with_memory_space_constraint(a, pltpu.HBM) for a in (w_gate, w_up, w_down))
     return pl.pallas_call(
         second_kernel,
-        out_shape=(shape, shape, jax.ShapeDtypeStruct((gain.shape[1], rows // 2 // blocks, oth.shape[2]), BF)),
+        out_shape=(shape, part, part, jax.ShapeDtypeStruct((gain.shape[1], rows // 2 // blocks, oth.shape[2]), BF)),
         in_specs=[vmem] * 5 + [hbm] * 3,
-        out_specs=[vmem] * 3,
+        out_specs=[vmem] * 4,
         scratch_shapes=[
             pltpu.VMEM((experts, depth // 2, units), BF),
             pltpu.VMEM((experts, depth // 2, units), BF),
@@ -393,14 +399,13 @@
     own = lax.all_to_all(jnp.broadcast_to(hidden[None], (planes,) + hidden.shape), ("y", "side"), 0, 0, tiled=True)
     oth = lax.ppermute(own, "c", SWAP)
     acc, square, own_piece = own_half(own, gain, w_gate, w_up, toks)
-    keep, send, oth_piece = other_half(oth, gain, share, acc, square, w_gate, w_up, w_down, hgs)
-    got = lax.ppermute(send, "c", SWAP)
+    keep, low, high, oth_piece = other_half(oth, gain, share, acc, square, w_gate, w_up, w_down, hgs)
+    got = jnp.concatenate([lax.ppermute(low, "c", SWAP), lax.ppermute(high, "c", SWAP)], axis=0)
     quarter = width // hgs
     summed = keep + got
     own_piece, oth_piece = own_piece[..., :cols], oth_piece[..., :cols]
-    low = jnp.where(core == 0, own_piece, oth_piece)
-    high = jnp.where(core == 0, oth_piece, own_piece)
-    kept = jnp.concatenate([low, high], axis=0).transpose(1, 0, 2).reshape(toks, quarter)
+    kept = jnp.where(core == 0, jnp.concatenate([own_piece, oth_piece]), jnp.concatenate([oth_piece, own_piece]))
+    kept = kept.transpose(1, 0, 2).reshape(toks, quarter)
     summed, kept = lax.optimization_barrier((summed, kept))
     parts = lax.all_to_all(summed, ("hg", "y", "side"), 0, 0, tiled=True)
     moe = jnp.sum(parts.astype(F32), axis=0)

time: 92.7 us -> 91.8 us (level)
  blocking collectives: 61.6 us -> 59.3 us
  Pallas kernels: 12.6 us -> 14.3 us
    all_to_all x1, blocking collectives: 19 us -> 16.6 us  [body(): here = lax.all_to_all(message, ('y', 'side'), 0, 0, tiled=True)]
    pallas_call x1, Pallas kernels: 5.7 us -> 7.47 us  [attention(): pl.pallas_call(functools.partial(attention_kernel, span=span, ahead=ahead...]
    ppermute x1 -> x2, waiting for transfers between devices: 2.08 us -> 2.01 us  [the longest x1 1.22 us: body(): lax.ppermute(low, 'c', SWAP)]
  transfers between devices with their start and end apart: 5 -> 6, of which waited for: 5 -> 6; matrix products, arithmetic and copies ran while one was open for 0% -> 0% of each run, Pallas kernels for 3% -> 3%
where the time goes in v4:
time: 91.8 us; the launch traced here: 91.5 us
  blocking collectives  59.3 us (65%)
  Pallas kernels  14.3 us (16%)
  waiting for transfers between devices  8.91 us (10%)
  starting transfers between devices  5.02 us (5%)
  other arithmetic  2.74 us (3%)
    all_to_all x1, blocking collectives, body(): parts = lax.all_to_all(summed, ('hg', 'y', 'side'), 0, 0, tiled=True)  24.1 us
    all_to_all x1, blocking collectives, body(): lax.all_to_all(jnp.broadcast_to(hidden[None], (planes,) + hidden.shape),...  18.6 us
    all_to_all x1, blocking collectives, body(): here = lax.all_to_all(message, ('y', 'side'), 0, 0, tiled=True)  16.6 us
    pallas_call x1, Pallas kernels, attention(): pl.pallas_call(functools.partial(attention_kernel, span=span, ahead=ahead...  7.47 us
    pallas_call x1, Pallas kernels, other_half(): pl.pallas_call(second_kernel, out_shape=(shape, part, part, jax.ShapeDtyp...  4.3 us
    ppermute x1, starting transfers between devices, body(): lax.ppermute(pair, 'hg', PAIRS_B).astype(F32)  2.84 us
    ppermute x1, waiting for transfers between devices, body(): lax.ppermute(pair, 'hg', PAIRS_B).astype(F32)  2.71 us
    ppermute x1, waiting for transfers between devices, body(): lax.ppermute(partial, 'hg', PAIRS_A)  2.67 us
  transfers between devices with their start and end apart: 6, of which 6 were waited for; matrix products, arithmetic and copies ran while one was open for 0% of the time, Pallas kernels for 3%

profile of v4, /device:TPU:0, one launch (start us, length us, event | category | flops | bytes accessed | tf_op | source)
XLA Modules:
  0.0 91.5 jit_solution(8494468928912019904)
XLA Ops:
  0.0 0.0 copy-start
  0.0 0.0 copy-start.1
  0.0 7.5 %attention.1 = bf16[16,4,2304]{2,1,0:T(4,128)(2,1)S(1)} custom-call(s32[2]{0:T(128)} %len_hbm.1, s32[4,4]{1,0:T(4,128)} %routes_hbm.1, s32[4,4]{1,0:T(4,128)} %ints_hbm.1, bf16[4,2048]{1,0:T(4,128)(2,1)} %qn_hbm.1, bf16[4,1024]{1,0:T(4,128)(2,1)} %qr_hbm.1, bf16[4,7168]{1,0:T(4,128)(2,1)} %res_hbm.1, bf16[16,128,512]{2,1,0:T(8,128)(2,1)} %wa_hbm.1, ...), custom_call_target="tpu_custom_call" | custom-call | tf_op jit(solution)/shard_map/attention/pallas_call | solution.py:167
  7.5 16.6 %all_to_all.15 = bf16[16,4,2304]{2,1,0:T(4,128)(2,1)S(1)} all-to-all(bf16[16,4,2304]{2,1,0:T(4,128)(2,1)S(1)} %attention.1), channel_id=1, replica_groups=mesh['hg'=4,'y'=4,'c'=2,'side'=4] {'y','side'}, dimensions={0} | all-to-all | bytes 589824 | tf_op jit(solution)/shard_map/all_to_all | solution.py:376
  24.1 0.0 collective-permute-start
  24.1 0.0 copy-done.1
  24.1 0.1 reshape.39.gain_ref
  24.2 1.4 %collective-permute-done = bf16[16,4,2304]{2,1,0:T(4,128)(2,1)S(1)} collective-permute-done((bf16[16,4,2304]{2,1,0:T(4,128)(2,1)S(1)}, bf16[16,4,2304]{2,1,0:T(4,128)(2,1)S(1)}, u32[]{:S(2)}, u32[]{:S(2)}) %collective-permute-start) | collective-permute-done | bytes 294944 | tf_op jit(solution)/shard_map/ppermute | solution.py:377
  25.7 0.1 fusion.6
  25.8 0.4 fusion.2
  26.1 0.1 reshape.37
  26.2 0.1 reduce_sum.18
  26.4 0.1 dynamic-slice_convert_fusion
  26.5 0.0 copy-done
  26.5 0.6 fusion
  27.1 0.1 copy.18
  27.2 1.6 %collective-permute-start.1 = (bf16[128,256]{1,0:T(8,128)(2,1)S(1)}, bf16[128,256]{1,0:T(8,128)(2,1)S(1)}, u32[]{:S(2)}, u32[]{:S(2)}) collective-permute-start(bf16[128,256]{1,0:T(8,128)(2,1)S(1)} %pad.4), channel_id=1, source_target_pairs={{0,32},{32,0},{64,96},{96,64},{1,33},{33,1},{65,97},{97,65},{2,34}... | collective-permute-start | bytes 196616 | tf_op jit(solution)/shard_map/ppermute | solution.py:395
  28.8 0.1 dynamic-slice_multiply_fusion.share_ref
  28.9 2.7 %collective-permute-done.1 = bf16[128,256]{1,0:T(8,128)(2,1)S(1)} collective-permute-done((bf16[128,256]{1,0:T(8,128)(2,1)S(1)}, bf16[128,256]{1,0:T(8,128)(2,1)S(1)}, u32[]{:S(2)}, u32[]{:S(2)}) %collective-permute-start.1) | collective-permute-done | bytes 65568 | tf_op jit(solution)/shard_map/ppermute | solution.py:395
  31.6 2.8 %collective-permute-start.2 = (bf16[128,256]{1,0:T(8,128)(2,1)S(1)}, bf16[128,256]{1,0:T(8,128)(2,1)S(1)}, u32[]{:S(2)}, u32[]{:S(2)}) collective-permute-start(bf16[128,256]{1,0:T(8,128)(2,1)S(1)} %add_convert_fusion.1), channel_id=1, source_target_pairs={{32,64},{64,32},{96,0},{0,96},{33,65},{65,33},{97,1},{1,97},{34,66... | collective-permute-start | bytes 196616 | tf_op jit(solution)/shard_map/ppermute | solution.py:397
  34.4 2.7 %collective-permute-done.2 = bf16[128,256]{1,0:T(8,128)(2,1)S(1)} collective-permute-done((bf16[128,256]{1,0:T(8,128)(2,1)S(1)}, bf16[128,256]{1,0:T(8,128)(2,1)S(1)}, u32[]{:S(2)}, u32[]{:S(2)}) %collective-permute-start.2) | collective-permute-done | bytes 65568 | tf_op jit(solution)/shard_map/ppermute | solution.py:397
  37.1 0.1 broadcast_in_dim.32
  37.2 18.6 %all_to_all.16.own_ref = bf16[16,128,256]{2,1,0:T(8,128)(2,1)S(1)} all-to-all(bf16[16,128,256]{2,1,0:T(8,128)(2,1)S(1)} %broadcast_in_dim.32), channel_id=1, replica_groups=mesh['hg'=4,'y'=4,'c'=2,'side'=4] {'y','side'}, dimensions={0} | all-to-all | bytes 2097152 | tf_op jit(solution)/shard_map/all_to_all | solution.py:399
  55.8 0.0 collective-permute-start.3
  55.8 2.6 %experts_first.1 = (f32[2,128,256]{2,1,0:T(8,128)S(1)}, f32[128,1]{1,0:T(8,128)S(1)}, bf16[4,4,256]{2,1,0:T(4,128)(2,1)S(1)}) custom-call(bf16[16,128,256]{2,1,0:T(8,128)(2,1)S(1)} %all_to_all.16.own_ref, f32[8,4,224]{2,1,0:T(4,128)S(1)} %reshape.39.gain_ref, bf16[2,7168,128]{2,1,0:T(8,128)(2,1)} %wg_hbm.3, bf16[2,7168,128]{2,1,0:T(8,128)(2,1)} %wu_hbm.3), custom_call_target="tpu_custom_call" | custom-call | flops 469762048 | bytes 5000000 | tf_op jit(solution)/shard_map/experts_first/pallas_call | solution.py:316
  58.4 0.1 collective-permute-done.3.oth_ref
  58.5 4.3 %experts_second.1 = (bf16[64,8,896]{2,1,0:T(8,128)(2,1)S(1)}, bf16[32,8,896]{2,1,0:T(8,128)(2,1)S(1)}, bf16[32,8,896]{2,1,0:T(8,128)(2,1)S(1)}, bf16[4,4,256]{2,1,0:T(4,128)(2,1)S(1)}) custom-call(bf16[16,128,256]{2,1,0:T(8,128)(2,1)S(1)} %collective-permute-done.3.oth_ref, f32[8,4,224]{2,1,0:T(4,128)S(1)} %reshape.39.gain_ref, ...), custom_call_target="tpu_custom_call" | custom-call | flops 939524096 | bytes 10000000 | tf_op jit(solution)/shard_map/experts_second/pallas_call | solution.py:344
  62.8 0.5 collective-permute-start.4
  63.3 0.1 collective-permute-start.5
  63.4 0.1 reshape.36
  63.5 1.2 %collective-permute-done.4 = bf16[32,8,896]{2,1,0:T(8,128)(2,1)S(1)} collective-permute-done((bf16[32,8,896]{2,1,0:T(8,128)(2,1)S(1)}, bf16[32,8,896]{2,1,0:T(8,128)(2,1)S(1)}, u32[]{:S(2)}, u32[]{:S(2)}) %collective-permute-start.4) | collective-permute-done | bytes 458784 | tf_op jit(solution)/shard_map/ppermute | solution.py:403
  64.7 0.8 collective-permute-done.5
  65.5 1.1 %maximum_add_fusion = bf16[64,8,896]{2,1,0:T(8,128)(2,1)S(1)} fusion(bf16[64,8,896]{2,1,0:T(8,128)(2,1)S(1)} %get-tuple-element.22, bf16[32,8,896]{2,1,0:T(8,128)(2,1)} %collective-permute-done.5, bf16[32,8,896]{2,1,0:T(8,128)(2,1)S(1)} %collective-permute-done.4), kind=kLoop, calls=%fused_computation.3 | loop fusion | flops 917504 | bytes 2752512 | tf_op jit(solution)/shard_map/add | solution.py:405
  66.6 24.1 %all_to_all.17 = bf16[64,8,896]{2,1,0:T(8,128)(2,1)S(1)} all-to-all(bf16[64,8,896]{2,1,0:T(8,128)(2,1)S(1)} %maximum_add_fusion), channel_id=1, replica_groups=mesh['hg'=4,'y'=4,'c'=2,'side'=4] {'hg','y','side'}, dimensions={0} | all-to-all | bytes 1835008 | tf_op jit(solution)/shard_map/all_to_all | solution.py:410
  90.7 0.2 convert_reduce_fusion
  90.9 0.6 fusion.4
  (13 shorter events, 0.2 us)
Async XLA Ops:
  0.0 26.5 %copy-start = (bf16[2048,224]{0,1:T(8,128)(2,1)S(1)}, bf16[2048,224]{0,1:T(8,128)(2,1)}, u32[]{:S(2)}) copy-start(bf16[2048,224]{0,1:T(8,128)(2,1)} %param.22) | copy-start | bytes 2752516
  0.0 24.1 %copy-start.1 = (bf16[7168]{0:T(1024)(128)(2,1)S(1)}, bf16[7168]{0:T(1024)(128)(2,1)}, u32[]{:S(2)}) copy-start(bf16[7168]{0:T(1024)(128)(2,1)} %param.24) | copy-start | bytes 43012
  24.1 1.6 %collective-permute-start = (bf16[16,4,2304]{2,1,0:T(4,128)(2,1)S(1)}, bf16[16,4,2304]{2,1,0:T(4,128)(2,1)S(1)}, u32[]{:S(2)}, u32[]{:S(2)}) collective-permute-start(bf16[16,4,2304]{2,1,0:T(4,128)(2,1)S(1)} %all_to_all.15), channel_id=1, source_target_pairs={{0,4},{4,0},{1,5},{5,1},{2,6},{6,2},{3,7},{7,3},{8,12},{12,8},{9,1... | collective-permute-start | bytes 884744 | tf_op jit(solution)/shard_map/ppermute | solution.py:377
  27.2 4.3 %collective-permute-start.1 = (bf16[128,256]{1,0:T(8,128)(2,1)S(1)}, bf16[128,256]{1,0:T(8,128)(2,1)S(1)}, u32[]{:S(2)}, u32[]{:S(2)}) collective-permute-start(bf16[128,256]{1,0:T(8,128)(2,1)S(1)} %pad.4), channel_id=1, source_target_pairs={{0,32},{32,0},{64,96},{96,64},{1,33},{33,1},{65,97},{97,65},{2,34}... | collective-permute-start | bytes 196616 | tf_op jit(solution)/shard_map/ppermute | solution.py:395
  31.6 5.6 %collective-permute-start.2 = (bf16[128,256]{1,0:T(8,128)(2,1)S(1)}, bf16[128,256]{1,0:T(8,128)(2,1)S(1)}, u32[]{:S(2)}, u32[]{:S(2)}) collective-permute-start(bf16[128,256]{1,0:T(8,128)(2,1)S(1)} %add_convert_fusion.1), channel_id=1, source_target_pairs={{32,64},{64,32},{96,0},{0,96},{33,65},{65,33},{97,1},{1,97},{34,66... | collective-permute-start | bytes 196616 | tf_op jit(solution)/shard_map/ppermute | solution.py:397
  55.8 2.7 %collective-permute-start.3 = (bf16[16,128,256]{2,1,0:T(8,128)(2,1)S(1)}, bf16[16,128,256]{2,1,0:T(8,128)(2,1)S(1)}, u32[]{:S(2)}, u32[]{:S(2)}) collective-permute-start(bf16[16,128,256]{2,1,0:T(8,128)(2,1)S(1)} %all_to_all.16.own_ref), channel_id=1, source_target_pairs={{0,4},{4,0},{1,5},{5,1},{2,6},{6,2},{3,7},{7,3},{8,12},{12,8},{9,1... | collective-permute-start | bytes 3145736 | tf_op jit(solution)/shard_map/ppermute | solution.py:400
  62.8 1.9 %collective-permute-start.4 = (bf16[32,8,896]{2,1,0:T(8,128)(2,1)S(1)}, bf16[32,8,896]{2,1,0:T(8,128)(2,1)S(1)}, u32[]{:S(2)}, u32[]{:S(2)}) collective-permute-start(bf16[32,8,896]{2,1,0:T(8,128)(2,1)S(1)} %get-tuple-element.23), channel_id=1, source_target_pairs={{0,4},{4,0},{1,5},{5,1},{2,6},{6,2},{3,7},{7,3},{8,12},{12,8},{9,1... | collective-permute-start | bytes 1376264 | tf_op jit(solution)/shard_map/ppermute | solution.py:403
  63.3 2.2 %collective-permute-start.5 = (bf16[32,8,896]{2,1,0:T(8,128)(2,1)S(1)}, bf16[32,8,896]{2,1,0:T(8,128)(2,1)}, u32[]{:S(2)}, u32[]{:S(2)}) collective-permute-start(bf16[32,8,896]{2,1,0:T(8,128)(2,1)S(1)} %get-tuple-element.24), channel_id=1, source_target_pairs={{0,4},{4,0},{1,5},{5,1},{2,6},{6,2},{3,7},{7,3},{8,12},{12,8},{9,1... | collective-permute-start | bytes 1376264 | tf_op jit(solution)/shard_map/ppermute | solution.py:403

commit v5 on v4

--- a/solution.py
+++ b/solution.py
@@ -198,91 +198,57 @@
     ))
 
 
-def half_copies(wg_hbm, wu_hbm, wg, wu, sem, part, stripes):
-    experts, depth, _ = wg_hbm.shape
+def experts_kernel(rows_ref, gain_ref, share_ref, wg0, wu0, wd0, wg1, wu1, wd1, out_ref, kept_ref,
+                   wg, wu, wd, sem, sem_down, *, ahead):
+    local, depth, units = wg0.shape
+    experts = 2 * local
+    blocks, rows, lanes = rows_ref.shape
+    sides, cols = gain_ref.shape[1:]
+    stripes = blocks // sides
     stripe = depth // stripes
-    half = stripe // 2
+    core = lax.axis_index("c")
     groups = []
     for y in range(stripes):
-        at = pl.ds(pl.multiple_of(y * stripe + part * half, 16), half)
-        to = pl.ds(y * half, half)
+        at = pl.ds(y * stripe, stripe)
         groups.append([
-            pltpu.make_async_copy(src.at[e, at, :], dst.at[e, to, :], sem.at[(y * experts + e) * 2 + k])
-            for e in range(experts)
-            for k, (src, dst) in enumerate(((wg_hbm, wg), (wu_hbm, wu)))
+            pltpu.make_async_copy(src.at[:, at, :], dst.at[pl.ds(k * local, local), at, :], sem.at[y * 4 + 2 * k + j])
+            for k in range(2)
+            for j, (src, dst) in enumerate((((wg0, wg1)[k], wg), ((wu0, wu1)[k], wu)))
         ])
-    return groups
-
-
-def half_products(blocks_ref, gain_ref, wg, wu, groups, part, acc, swap):
-    blocks, rows, _ = blocks_ref.shape
-    stripes = len(groups)
-    sides = blocks // stripes
-    cols = gain_ref.shape[2]
-    half = rows // 2
+    messages, lines, tile = out_ref.shape
+    toks = lines // 2
+    parts = depth // (2 * tile)
+    downs = []
+    for n in range(parts):
+        at = pl.ds(2 * n * tile, 2 * tile)
+        downs.append([
+            pltpu.make_async_copy(src.at[:, :, at], wd.at[pl.ds(k * local, local), :, at], sem_down.at[n * 2 + k])
+            for k, src in enumerate((wd0, wd1))
+        ])
+    queue = groups + downs
+    for y in range(ahead):
+        for copy in groups[y]:
+            copy.start()
+    pick_rows(rows_ref, kept_ref)
+    acc = [jnp.zeros((rows, 2 * units), F32) for _ in range(experts)]
     square = jnp.zeros((rows, cols), F32)
     for y in range(stripes):
+        for copy in queue[y + ahead]:
+            copy.start()
         for copy in groups[y]:
             copy.wait()
         for s in range(sides):
-            block = blocks_ref[y * sides + s, :, :cols].astype(F32)
-            if swap:
-                block = jnp.concatenate([block[half:], block[:half]], axis=0)
-            square = square + block * block
-            scaled = (block * gain_ref[y * 2 + part, pl.ds(s, 1), :]).astype(BF)
-            at = pl.ds((y * sides + s) * cols, cols)
-            for e in range(len(acc)):
-                both = jnp.concatenate([wg[e, at, :], wu[e, at, :]], axis=1)
-                acc[e] = acc[e] + jnp.dot(scaled, both, preferred_element_type=F32)
-    return acc, jnp.sum(square, axis=-1, keepdims=True)
-
-
-def pick_rows(blocks_ref, kept_ref, base):
-    sides, toks, _ = kept_ref.shape
-    at = base + (lax.axis_index("y") * sides + lax.axis_index("side")) * toks
-    group = pl.multiple_of(at // 16 * 16, 16)
-    for s in range(sides):
-        rows = blocks_ref[lax.axis_index("hg") * sides + s, pl.ds(group, 16), :].astype(F32)
-        found = rows[:toks]
-        for k in range(1, 16 // toks):
-            found = jnp.where(at - group == k * toks, rows[k * toks:(k + 1) * toks], found)
-        kept_ref[s] = found.astype(BF)
-
-
-def first_kernel(own_ref, gain_ref, wg_hbm, wu_hbm, acc_ref, sq_ref, kept_ref, wg, wu, sem):
-    experts, depth, units = wg_hbm.shape
-    rows = own_ref.shape[1]
-    core = lax.axis_index("c")
-    groups = half_copies(wg_hbm, wu_hbm, wg, wu, sem, core, gain_ref.shape[0] // 2)
-    for group in groups:
-        for copy in group:
-            copy.start()
-    acc = [jnp.zeros((rows, 2 * units), F32) for _ in range(experts)]
-    acc, square = half_products(own_ref, gain_ref, wg, wu, groups, core, acc, False)
-    for e in range(experts):
-        acc_ref[e] = acc[e]
-    sq_ref[...] = square
-    pick_rows(own_ref, kept_ref, 0)
-
-
-def second_kernel(oth_ref, gain_ref, share_ref, acc_ref, sq_ref, wg_hbm, wu_hbm, wd_hbm, keep_ref, low_ref, high_ref, kept_ref,
-                  wg, wu, wd, sem, sem_down):
-    experts, depth, units = wg_hbm.shape
-    blocks, rows, _ = oth_ref.shape
-    half = rows // 2
-    part = 1 - lax.axis_index("c")
-    groups = half_copies(wg_hbm, wu_hbm, wg, wu, sem, part, gain_ref.shape[0] // 2)
-    downs = [
-        pltpu.make_async_copy(wd_hbm.at[e], wd.at[pl.ds(e * units, units), :], sem_down.at[e])
-        for e in range(experts)
-    ]
-    for group in groups:
-        for copy in group:
-            copy.start()
-    for copy in downs:
-        copy.start(priority=1)
-    acc, square = half_products(oth_ref, gain_ref, wg, wu, groups, part, [acc_ref[e] for e in range(experts)], True)
-    inverse = lax.rsqrt((square + sq_ref[...]) / depth + EPS)
+            for other in range(2):
+                part = core if other == 0 else 1 - core
+                first = other * (lanes // 2)
+                block = rows_ref[y * sides + s, :, first:first + cols].astype(F32)
+                square = square + block * block
+                scaled = (block * gain_ref[y * 2 + part, pl.ds(s, 1), :]).astype(BF)
+                at = pl.ds(pl.multiple_of(y * stripe + part * (stripe // 2) + s * cols, 16), cols)
+                for e in range(experts):
+                    both = jnp.concatenate([wg[e, at, :], wu[e, at, :]], axis=1)
+                    acc[e] = acc[e] + jnp.dot(scaled, both, preferred_element_type=F32)
+    inverse = lax.rsqrt(jnp.sum(square, axis=-1, keepdims=True) / depth + EPS)
     acts = []
     for e in range(experts):
         both = acc[e] * inverse
@@ -291,72 +257,59 @@
         act = gate / (1.0 + jnp.exp(-gate)) * up
         acts.append(jnp.where(share > 0, act * share, 0.0).astype(BF))
     act = jnp.concatenate(acts, axis=1)
-    pick_rows(oth_ref, kept_ref, half)
-    for copy in downs:
-        copy.wait()
-    messages, lines, tile = keep_ref.shape
-    toks = lines // 2
-    for n in range(depth // (2 * tile)):
-        left = jnp.dot(act, wd[:, 2 * n * tile:(2 * n + 1) * tile], preferred_element_type=F32)
-        right = jnp.dot(act, wd[:, (2 * n + 1) * tile:(2 * n + 2) * tile], preferred_element_type=F32)
+    for n in range(parts):
+        if stripes + n + ahead < len(queue):
+            for copy in queue[stripes + n + ahead]:
+                copy.start()
+        for copy in downs[n]:
+            copy.wait()
+        down = wd[:, :, 2 * n * tile:(2 * n + 2) * tile].reshape(experts * units, 2 * tile)
+        left = jnp.dot(act, down[:, :tile], preferred_element_type=F32)
+        right = jnp.dot(act, down[:, tile:], preferred_element_type=F32)
         for k in range(blocks):
             at = slice(k * toks, (k + 1) * toks)
-            keep_ref[n * blocks + k] = jnp.concatenate([left[at], right[at]], axis=0).astype(BF)
-            at = slice(half + k * toks, half + (k + 1) * toks)
-            send_ref, place = (low_ref, n) if n * blocks < low_ref.shape[0] else (high_ref, n - low_ref.shape[0] // blocks)
-            send_ref[place * blocks + k] = jnp.concatenate([left[at], right[at]], axis=0).astype(BF)
-
-
-def own_half(own, gain, w_gate, w_up, toks):
-    experts, depth, units = w_gate.shape
-    rows = own.shape[1]
+            out_ref[n * blocks + k] = jnp.concatenate([left[at], right[at]], axis=0).astype(BF)
+
+
+def pick_rows(blocks_ref, kept_ref):
+    sides, toks, _ = kept_ref.shape
+    at = (lax.axis_index("y") * sides + lax.axis_index("side")) * toks
+    group = pl.multiple_of(at // 16 * 16, 16)
+    for s in range(sides):
+        rows = blocks_ref[lax.axis_index("hg") * sides + s, pl.ds(group, 16), :].astype(F32)
+        found = rows[:toks]
+        for k in range(1, 16 // toks):
+            found = jnp.where(at - group == k * toks, rows[k * toks:(k + 1) * toks], found)
+        kept_ref[s] = found.astype(BF)
+
+
+def run_experts(rows, gain, share, own, other, hgs, ahead=3):
+    local, depth, units = own[0].shape
+    experts = 2 * local
+    blocks, count, lanes = rows.shape
+    toks = count // blocks
     vmem = pl.BlockSpec(memory_space=pltpu.VMEM)
     hbm = pl.BlockSpec(memory_space=pltpu.HBM)
-    w_gate, w_up = (pltpu.with_memory_space_constraint(a, pltpu.HBM) for a in (w_gate, w_up))
+    weights = [pltpu.with_memory_space_constraint(a, pltpu.HBM) for a in (*own, *other)]
     return pl.pallas_call(
-        first_kernel,
+        functools.partial(experts_kernel, ahead=ahead),
         out_shape=(
-            jax.ShapeDtypeStruct((experts, rows, 2 * units), F32),
-            jax.ShapeDtypeStruct((rows, 1), F32),
-            jax.ShapeDtypeStruct((gain.shape[1], toks, own.shape[2]), BF),
+            pltpu.VMEM((hgs * blocks, 2 * toks, depth // hgs // 2), BF),
+            jax.ShapeDtypeStruct((gain.shape[1], toks, lanes), BF),
         ),
-        in_specs=[vmem] * 2 + [hbm] * 2,
-        out_specs=[vmem] * 3,
+        in_specs=[vmem] * 3 + [hbm] * 6,
+        out_specs=[vmem] * 2,
         scratch_shapes=[
-            pltpu.VMEM((experts, depth // 2, units), BF),
-            pltpu.VMEM((experts, depth // 2, units), BF),
-            pltpu.SemaphoreType.DMA((gain.shape[0] * experts,)),
+            pltpu.VMEM((experts, depth, units), BF),
+            pltpu.VMEM((experts, depth, units), BF),
+            pltpu.VMEM((experts, units, depth), BF),
+            pltpu.SemaphoreType.DMA((blocks // gain.shape[1] * 4,)),
+            pltpu.SemaphoreType.DMA((hgs * 2,)),
         ],
-        compiler_params=pltpu.CompilerParams(vmem_limit_bytes=12 * 1024 * 1024),
-        cost_estimate=pl.CostEstimate(flops=rows * depth * 512, bytes_accessed=5_000_000, transcendentals=0),
-        name="experts_first",
-    )(own, gain, w_gate, w_up)
-
-
-def other_half(oth, gain, share, acc, square, w_gate, w_up, w_down, hgs):
-    experts, depth, units = w_gate.shape
-    blocks, rows, _ = oth.shape
-    shape = jax.ShapeDtypeStruct((hgs * blocks, rows // blocks, depth // hgs // 2), BF)
-    part = jax.ShapeDtypeStruct((hgs * blocks // 2,) + shape.shape[1:], BF)
-    vmem = pl.BlockSpec(memory_space=pltpu.VMEM)
-    hbm = pl.BlockSpec(memory_space=pltpu.HBM)
-    w_gate, w_up, w_down = (pltpu.with_memory_space_constraint(a, pltpu.HBM) for a in (w_gate, w_up, w_down))
-    return pl.pallas_call(
-        second_kernel,
-        out_shape=(shape, part, part, jax.ShapeDtypeStruct((gain.shape[1], rows // 2 // blocks, oth.shape[2]), BF)),
-        in_specs=[vmem] * 5 + [hbm] * 3,
-        out_specs=[vmem] * 4,
-        scratch_shapes=[
-            pltpu.VMEM((experts, depth // 2, units), BF),
-            pltpu.VMEM((experts, depth // 2, units), BF),
-            pltpu.VMEM((experts * units, depth), BF),
-            pltpu.SemaphoreType.DMA((gain.shape[0] * experts,)),
-            pltpu.SemaphoreType.DMA((experts,)),
-        ],
-        compiler_params=pltpu.CompilerParams(vmem_limit_bytes=18 * 1024 * 1024),
-        cost_estimate=pl.CostEstimate(flops=rows * depth * 1024, bytes_accessed=10_000_000, transcendentals=0),
-        name="experts_second",
-    )(oth, gain, share, acc, square, w_gate, w_up, w_down)
+        compiler_params=pltpu.CompilerParams(vmem_limit_bytes=32 * 1024 * 1024),
+        cost_estimate=pl.CostEstimate(flops=count * depth * 3072, bytes_accessed=24_000_000, transcendentals=0),
+        name="experts",
+    )(rows, gain, share, *weights)
 
 
 def body(
@@ -373,40 +326,45 @@
 
     message = attention(q_nope, q_rope, w_absorb, cache_latent, cache_rope, lengths, w_value, residual, routes, gate_int,
                         planes, sides, experts_all)
+    message, w_out_, norm_gain = lax.optimization_barrier((message, w_out, norm_gain))
+    out_there = lax.ppermute(w_out_, "c", SWAP)
+    gain = norm_gain.astype(F32).reshape(ys * cores, sides, cols)
+    gain, w_gate_, w_up_, w_down_ = lax.optimization_barrier((gain, w_gate, w_up, w_down))
+    other = tuple(lax.ppermute(w, "c", SWAP) for w in (w_gate_, w_up_, w_down_))
     here = lax.all_to_all(message, ("y", "side"), 0, 0, tiled=True)
-    there = lax.ppermute(here, "c", SWAP)
-    both = jnp.stack([here, there])
     n_val = w_absorb.shape[0] * VDIM
-    all_values = both[..., :n_val].reshape(cores * planes * toks, n_val)
-    extra = both[..., n_val:]
-    window = lax.dynamic_slice_in_dim(extra[..., :3, :], core * 128, 128, 3).reshape(cores * planes, 3 * 128)
-    block = (y * cores + core) * sides + side
-    mine = lax.dynamic_slice_in_dim(window, lax.rem(block * cols, 128), cols, 1)[:, None]
-    gates = extra[..., 3, :toks * experts_all].reshape(cores * planes * toks, experts_all).astype(F32)
+    values = here[..., :n_val].reshape(planes * toks, n_val)
+    extra = here[..., n_val:]
+    is_row = (jnp.arange(toks) == hg)[None, :, None]
+    halves = []
+    for part, weights in ((core, w_out), (1 - core, out_there)):
+        window = lax.dynamic_slice_in_dim(extra[:, :3], part * 128, 128, 2).reshape(planes, 3 * 128)
+        block = (y * cores + part) * sides + side
+        mine = lax.dynamic_slice_in_dim(window, lax.rem(block * cols, 128), cols, 1)[:, None]
+        half = jnp.dot(values, weights, preferred_element_type=F32).reshape(planes, toks, cols)
+        half = (half + jnp.where(is_row, mine.astype(F32), 0.0)).astype(BF).reshape(planes * toks, cols)
+        halves.append(jnp.pad(half, ((0, 0), (0, -cols % 128))))
+    partial = jnp.concatenate(halves, axis=1)
+    gates = extra[:, 3, :toks * experts_all].reshape(planes * toks, experts_all).astype(F32)
     total = jnp.sum(gates, axis=1, keepdims=True)
-    first = (y * cores + core) * local_experts
-    share = lax.dynamic_slice_in_dim(gates, first, local_experts, 1) * (ROUTE_SCALE / total)
-
-    partial = jnp.dot(all_values, w_out, preferred_element_type=F32).reshape(cores * planes, toks, cols)
-    is_row = (jnp.arange(toks) == hg)[None, :, None]
-    partial = (partial + jnp.where(is_row, mine.astype(F32), 0.0)).astype(BF).reshape(-1, cols)
-    partial = jnp.pad(partial, ((0, 0), (0, -cols % 128)))
-    gain = norm_gain.astype(F32).reshape(ys * cores, sides, cols)
-    other, share, gain = lax.optimization_barrier((lax.ppermute(partial, "hg", PAIRS_A), share, gain))
-    pair = (partial.astype(F32) + other.astype(F32)).astype(BF)
+    share = jnp.concatenate(
+        [
+            lax.dynamic_slice_in_dim(gates, (y * cores + part) * local_experts, local_experts, 1)
+            for part in (core, 1 - core)
+        ],
+        axis=1,
+    ) * (ROUTE_SCALE / total)
+    got, share = lax.optimization_barrier((lax.ppermute(partial, "hg", PAIRS_A), share))
+    pair = (partial.astype(F32) + got.astype(F32)).astype(BF)
     hidden = (pair.astype(F32) + lax.ppermute(pair, "hg", PAIRS_B).astype(F32)).astype(BF)
 
-    own = lax.all_to_all(jnp.broadcast_to(hidden[None], (planes,) + hidden.shape), ("y", "side"), 0, 0, tiled=True)
-    oth = lax.ppermute(own, "c", SWAP)
-    acc, square, own_piece = own_half(own, gain, w_gate, w_up, toks)
-    keep, low, high, oth_piece = other_half(oth, gain, share, acc, square, w_gate, w_up, w_down, hgs)
-    got = jnp.concatenate([lax.ppermute(low, "c", SWAP), lax.ppermute(high, "c", SWAP)], axis=0)
+    rows = lax.all_to_all(jnp.broadcast_to(hidden[None], (planes,) + hidden.shape), ("y", "side"), 0, 0, tiled=True)
+    summed, kept = run_experts(rows, gain, share, (w_gate, w_up, w_down), other, hgs)
     quarter = width // hgs
-    summed = keep + got
-    own_piece, oth_piece = own_piece[..., :cols], oth_piece[..., :cols]
+    lanes = kept.shape[2] // 2
+    own_piece, oth_piece = kept[..., :cols], kept[..., lanes:lanes + cols]
     kept = jnp.where(core == 0, jnp.concatenate([own_piece, oth_piece]), jnp.concatenate([oth_piece, own_piece]))
     kept = kept.transpose(1, 0, 2).reshape(toks, quarter)
-    summed, kept = lax.optimization_barrier((summed, kept))
     parts = lax.all_to_all(summed, ("hg", "y", "side"), 0, 0, tiled=True)
     moe = jnp.sum(parts.astype(F32), axis=0)
     moe = jnp.concatenate([moe[:toks], moe[toks:]], axis=1)

time: 91.8 us -> 86.8 us (0.946)
  blocking collectives: 59.3 us -> 18 us
  waiting for transfers between devices: 8.91 us -> 28.1 us
  starting transfers between devices: 5.02 us -> 21 us
  Pallas kernels: 14.3 us -> 16.2 us
  other arithmetic: 2.74 us -> 1.25 us
    all_to_all x2 -> x0, blocking collectives: 40.7 us -> none  [the longest x1 24.1 us: body(): parts = lax.all_to_all(summed, ('hg', 'y', 'side'), 0, 0, tiled=True)]
    all_to_all x0 -> x2, waiting for transfers between devices: none -> 22.7 us  [the longest x1 13.5 us: body(): parts = lax.all_to_all(summed, ('hg', 'y', 'side'), 0, 0, tiled=True)]
    all_to_all x0 -> x2, starting transfers between devices: none -> 15.7 us  [the longest x1 9.12 us: body(): here = lax.all_to_all(message, ('y', 'side'), 0, 0, tiled=True)]
    ppermute x4, waiting for transfers between devices: 3.53 us -> 0.01 us  [the longest x3 0.01 us: body(): lax.ppermute(w, 'c', SWAP)]
    pallas_call x2 -> x1, Pallas kernels: 6.85 us -> 9.1 us  [run_experts(): pl.pallas_call(functools.partial(experts_kernel, ahead=ahead), out_shape=...]
    add x1 -> x0, other arithmetic: 1.14 us -> none  [body(): summed = keep + got]
  transfers between devices with their start and end apart: 6 -> 8, of which waited for: 6 -> 4; matrix products, arithmetic and copies ran while one was open for 0% -> 2% of each run, Pallas kernels for 3% -> 0%
where the time goes in v5:
time: 86.8 us; the launch traced here: 86.4 us
  waiting for transfers between devices  28.1 us (32%)
  starting transfers between devices  21 us (24%)
  blocking collectives  18 us (21%)
  Pallas kernels  16.2 us (19%)
  other arithmetic  1.25 us (1%)
    all_to_all x1, blocking collectives, body(): lax.all_to_all(jnp.broadcast_to(hidden[None], (planes,) + hidden.shape),...  18 us
    all_to_all x1, waiting for transfers between devices, body(): parts = lax.all_to_all(summed, ('hg', 'y', 'side'), 0, 0, tiled=True)  13.5 us
    all_to_all x1, waiting for transfers between devices, body(): here = lax.all_to_all(message, ('y', 'side'), 0, 0, tiled=True)  9.18 us
    all_to_all x1, starting transfers between devices, body(): here = lax.all_to_all(message, ('y', 'side'), 0, 0, tiled=True)  9.12 us
    pallas_call x1, Pallas kernels, run_experts(): pl.pallas_call(functools.partial(experts_kernel, ahead=ahead), out_shape=...  9.1 us
    pallas_call x1, Pallas kernels, attention(): pl.pallas_call(functools.partial(attention_kernel, span=span, ahead=ahead...  7.07 us
    all_to_all x1, starting transfers between devices, body(): parts = lax.all_to_all(summed, ('hg', 'y', 'side'), 0, 0, tiled=True)  6.6 us
    ppermute x1, starting transfers between devices, body(): lax.ppermute(pair, 'hg', PAIRS_B).astype(F32)  2.84 us
  transfers between devices with their start and end apart: 8, of which 4 were waited for; matrix products, arithmetic and copies ran while one was open for 2% of the time, Pallas kernels for 0%

profile of v5, /device:TPU:0, one launch (start us, length us, event | category | flops | bytes accessed | tf_op | source)
XLA Modules:
  0.0 86.4 jit_solution(9939995492560117836)
XLA Ops:
  0.0 0.0 copy-start
  0.0 0.0 copy-start.1
  0.0 7.1 %attention.1 = bf16[16,4,2304]{2,1,0:T(4,128)(2,1)} custom-call(s32[2]{0:T(128)} %len_hbm.1, s32[4,4]{1,0:T(4,128)} %routes_hbm.1, s32[4,4]{1,0:T(4,128)} %ints_hbm.1, bf16[4,2048]{1,0:T(4,128)(2,1)} %qn_hbm.1, bf16[4,1024]{1,0:T(4,128)(2,1)} %qr_hbm.1, bf16[4,7168]{1,0:T(4,128)(2,1)} %res_hbm.1, bf16[16,128,512]{2,1,0:T(8,128)(2,1)} %wa_hbm.1, ...), custom_call_target="tpu_custom_call" | custom-call | tf_op jit(solution)/shard_map/attention/pallas_call | solution.py:167
  7.1 0.0 copy-done.1
  7.1 0.1 reshape.51.gain_ref
  7.2 0.1 collective-permute-start.3
  7.3 0.5 collective-permute-start.4
  7.8 0.1 collective-permute-start.5
  7.9 9.1 %all-to-all-start = ((bf16[16,4,2304]{2,1,0:T(4,128)(2,1)}), bf16[16,4,2304]{2,1,0:T(4,128)(2,1)S(1)}, u32[]{:S(2)}, u32[]{:S(2)}) async-start(bf16[16,4,2304]{2,1,0:T(4,128)(2,1)} %attention.1), calls=%async_computation | async-start | bytes 589824 | tf_op jit(solution)/shard_map/all_to_all | solution.py:334
  17.0 0.0 copy-done
  17.0 0.2 collective-permute-start
  17.2 9.2 %all-to-all-done = bf16[16,4,2304]{2,1,0:T(4,128)(2,1)S(1)} async-done(((bf16[16,4,2304]{2,1,0:T(4,128)(2,1)}), bf16[16,4,2304]{2,1,0:T(4,128)(2,1)S(1)}, u32[]{:S(2)}, u32[]{:S(2)}) %all-to-all-start) | async-done | bytes 294944 | tf_op jit(solution)/shard_map/all_to_all | solution.py:334
  26.5 0.1 reshape.49
  26.6 0.1 slice.32
  26.7 0.1 dynamic-slice_convert_fusion.1
  26.8 0.4 fusion
  27.3 0.1 reduce_sum.18
  27.4 0.1 dynamic-slice_convert_fusion
  27.5 0.1 constant_dynamic-slice_fusion.1
  27.6 0.0 collective-permute-done
  27.6 0.4 fusion.1
  28.1 1.6 %collective-permute-start.1 = (bf16[64,512]{1,0:T(8,128)(2,1)S(1)}, bf16[64,512]{1,0:T(8,128)(2,1)S(1)}, u32[]{:S(2)}, u32[]{:S(2)}) collective-permute-start(bf16[64,512]{1,0:T(8,128)(2,1)S(1)} %fusion.8), channel_id=1, source_target_pairs={{0,32},{32,0},{64,96},{96,64},{1,33},{33,1},{65,97},{97,65},{2,34}... | collective-permute-start | bytes 196616 | tf_op jit(solution)/shard_map/ppermute | solution.py:357
  29.7 0.1 maximum_multiply_fusion.share_ref
  29.8 2.7 %collective-permute-done.1 = bf16[64,512]{1,0:T(8,128)(2,1)S(1)} collective-permute-done((bf16[64,512]{1,0:T(8,128)(2,1)S(1)}, bf16[64,512]{1,0:T(8,128)(2,1)S(1)}, u32[]{:S(2)}, u32[]{:S(2)}) %collective-permute-start.1) | collective-permute-done | bytes 65568 | tf_op jit(solution)/shard_map/ppermute | solution.py:357
  32.5 2.8 %collective-permute-start.2 = (bf16[64,512]{1,0:T(8,128)(2,1)S(1)}, bf16[64,512]{1,0:T(8,128)(2,1)S(1)}, u32[]{:S(2)}, u32[]{:S(2)}) collective-permute-start(bf16[64,512]{1,0:T(8,128)(2,1)S(1)} %add_convert_fusion.1), channel_id=1, source_target_pairs={{32,64},{64,32},{96,0},{0,96},{33,65},{65,33},{97,1},{1,97},{34,66... | collective-permute-start | bytes 196616 | tf_op jit(solution)/shard_map/ppermute | solution.py:359
  35.3 2.7 %collective-permute-done.2 = bf16[64,512]{1,0:T(8,128)(2,1)S(1)} collective-permute-done((bf16[64,512]{1,0:T(8,128)(2,1)S(1)}, bf16[64,512]{1,0:T(8,128)(2,1)S(1)}, u32[]{:S(2)}, u32[]{:S(2)}) %collective-permute-start.2) | collective-permute-done | bytes 65568 | tf_op jit(solution)/shard_map/ppermute | solution.py:359
  38.1 0.1 broadcast_in_dim.43
  38.2 18.0 %all_to_all.15.rows_ref = bf16[16,64,512]{2,1,0:T(8,128)(2,1)S(1)} all-to-all(bf16[16,64,512]{2,1,0:T(8,128)(2,1)S(1)} %broadcast_in_dim.43), channel_id=1, replica_groups=mesh['hg'=4,'y'=4,'c'=2,'side'=4] {'y','side'}, dimensions={0} | all-to-all | bytes 2097152 | tf_op jit(solution)/shard_map/all_to_all | solution.py:361
  56.1 0.0 collective-permute-done.3.wg1
  56.1 0.0 collective-permute-done.4.wu1
  56.1 0.0 collective-permute-done.5.wd1
  56.2 9.1 %experts.1 = (bf16[64,8,896]{2,1,0:T(8,128)(2,1)}, bf16[4,4,512]{2,1,0:T(4,128)(2,1)S(1)}) custom-call(bf16[16,64,512]{2,1,0:T(8,128)(2,1)S(1)} %all_to_all.15.rows_ref, f32[8,4,224]{2,1,0:T(4,128)S(1)} %reshape.51.gain_ref, f32[64,4]{1,0:T(8,128)S(1)} %maximum_multiply_fusion.share_ref, bf16[2,7168,128]{2,1,0:T(8,128)(2,1)} %wg0.1, ...), custom_call_target="tpu_custom_call" | custom-call | flops 1409286144 | bytes 24000000 | tf_op jit(solution)/shard_map/experts/pallas_call | solution.py:294
  65.3 6.6 %all-to-all-start.2 = ((bf16[64,8,896]{2,1,0:T(8,128)(2,1)}), bf16[64,8,896]{2,1,0:T(8,128)(2,1)S(1)}, u32[]{:S(2)}, u32[]{:S(2)}) async-start(bf16[64,8,896]{2,1,0:T(8,128)(2,1)} %get-tuple-element.26), calls=%async_computation.2 | async-start | bytes 1835008 | tf_op jit(solution)/shard_map/all_to_all | solution.py:368
  71.9 0.1 reshape.52
  72.0 13.5 %all-to-all-done.2 = bf16[64,8,896]{2,1,0:T(8,128)(2,1)S(1)} async-done(((bf16[64,8,896]{2,1,0:T(8,128)(2,1)}), bf16[64,8,896]{2,1,0:T(8,128)(2,1)S(1)}, u32[]{:S(2)}, u32[]{:S(2)}) %all-to-all-start.2) | async-done | bytes 917536 | tf_op jit(solution)/shard_map/all_to_all | solution.py:368
  85.6 0.2 convert_reduce_fusion
  85.7 0.6 fusion.9
  (18 shorter events, 0.3 us)
Async XLA Ops:
  0.0 17.0 %copy-start = (bf16[2048,224]{0,1:T(8,128)(2,1)S(1)}, bf16[2048,224]{0,1:T(8,128)(2,1)}, u32[]{:S(2)}) copy-start(bf16[2048,224]{0,1:T(8,128)(2,1)} %param.22) | copy-start | bytes 2752516
  0.0 7.1 %copy-start.1 = (bf16[7168]{0:T(1024)(128)(2,1)S(1)}, bf16[7168]{0:T(1024)(128)(2,1)}, u32[]{:S(2)}) copy-start(bf16[7168]{0:T(1024)(128)(2,1)} %param.24) | copy-start | bytes 43012
  7.2 48.9 %collective-permute-start.3 = (bf16[2,7168,128]{2,1,0:T(8,128)(2,1)}, bf16[2,7168,128]{2,1,0:T(8,128)(2,1)}, u32[]{:S(2)}, u32[]{:S(2)}) collective-permute-start(bf16[2,7168,128]{2,1,0:T(8,128)(2,1)} %wg0.1), channel_id=1, source_target_pairs={{0,4},{4,0},{1,5},{5,1},{2,6},{6,2},{3,7},{7,3},{8,12},{12,8},{9,1... | collective-permute-start | bytes 11010056 | tf_op jit(solution)/shard_map/ppermute | solution.py:333
  7.3 48.9 %collective-permute-start.4 = (bf16[2,7168,128]{2,1,0:T(8,128)(2,1)}, bf16[2,7168,128]{2,1,0:T(8,128)(2,1)}, u32[]{:S(2)}, u32[]{:S(2)}) collective-permute-start(bf16[2,7168,128]{2,1,0:T(8,128)(2,1)} %wu0.1), channel_id=1, source_target_pairs={{0,4},{4,0},{1,5},{5,1},{2,6},{6,2},{3,7},{7,3},{8,12},{12,8},{9,1... | collective-permute-start | bytes 11010056 | tf_op jit(solution)/shard_map/ppermute | solution.py:333
  7.8 48.4 %collective-permute-start.5 = (bf16[2,128,7168]{2,1,0:T(8,128)(2,1)}, bf16[2,128,7168]{2,1,0:T(8,128)(2,1)}, u32[]{:S(2)}, u32[]{:S(2)}) collective-permute-start(bf16[2,128,7168]{2,1,0:T(8,128)(2,1)} %wd0.1), channel_id=1, source_target_pairs={{0,4},{4,0},{1,5},{5,1},{2,6},{6,2},{3,7},{7,3},{8,12},{12,8},{9,1... | collective-permute-start | bytes 11010056 | tf_op jit(solution)/shard_map/ppermute | solution.py:333
  7.9 18.6 %all-to-all-start = ((bf16[16,4,2304]{2,1,0:T(4,128)(2,1)}), bf16[16,4,2304]{2,1,0:T(4,128)(2,1)S(1)}, u32[]{:S(2)}, u32[]{:S(2)}) async-start(bf16[16,4,2304]{2,1,0:T(4,128)(2,1)} %attention.1), calls=%async_computation | async-start | bytes 589824 | tf_op jit(solution)/shard_map/all_to_all | solution.py:334
  17.0 10.6 %collective-permute-start = (bf16[2048,224]{0,1:T(8,128)(2,1)S(1)}, bf16[2048,224]{0,1:T(8,128)(2,1)S(1)}, u32[]{:S(2)}, u32[]{:S(2)}) collective-permute-start(bf16[2048,224]{0,1:T(8,128)(2,1)S(1)} %copy-done), channel_id=1, source_target_pairs={{0,4},{4,0},{1,5},{5,1},{2,6},{6,2},{3,7},{7,3},{8,12},{12,8},{9,1... | collective-permute-start | bytes 2752520 | tf_op jit(solution)/shard_map/ppermute | solution.py:330
  28.1 4.3 %collective-permute-start.1 = (bf16[64,512]{1,0:T(8,128)(2,1)S(1)}, bf16[64,512]{1,0:T(8,128)(2,1)S(1)}, u32[]{:S(2)}, u32[]{:S(2)}) collective-permute-start(bf16[64,512]{1,0:T(8,128)(2,1)S(1)} %fusion.8), channel_id=1, source_target_pairs={{0,32},{32,0},{64,96},{96,64},{1,33},{33,1},{65,97},{97,65},{2,34}... | collective-permute-start | bytes 196616 | tf_op jit(solution)/shard_map/ppermute | solution.py:357
  32.5 5.6 %collective-permute-start.2 = (bf16[64,512]{1,0:T(8,128)(2,1)S(1)}, bf16[64,512]{1,0:T(8,128)(2,1)S(1)}, u32[]{:S(2)}, u32[]{:S(2)}) collective-permute-start(bf16[64,512]{1,0:T(8,128)(2,1)S(1)} %add_convert_fusion.1), channel_id=1, source_target_pairs={{32,64},{64,32},{96,0},{0,96},{33,65},{65,33},{97,1},{1,97},{34,66... | collective-permute-start | bytes 196616 | tf_op jit(solution)/shard_map/ppermute | solution.py:359
  65.3 20.3 %all-to-all-start.2 = ((bf16[64,8,896]{2,1,0:T(8,128)(2,1)}), bf16[64,8,896]{2,1,0:T(8,128)(2,1)S(1)}, u32[]{:S(2)}, u32[]{:S(2)}) async-start(bf16[64,8,896]{2,1,0:T(8,128)(2,1)} %get-tuple-element.26), calls=%async_computation.2 | async-start | bytes 1835008 | tf_op jit(solution)/shard_map/all_to_all | solution.py:368

commit v6 on v5

--- a/solution.py
+++ b/solution.py
@@ -202,9 +202,10 @@
                    wg, wu, wd, sem, sem_down, *, ahead):
     local, depth, units = wg0.shape
     experts = 2 * local
-    blocks, rows, lanes = rows_ref.shape
-    sides, cols = gain_ref.shape[1:]
-    stripes = blocks // sides
+    blocks = rows_ref.shape[0]
+    stripes, sides, span = gain_ref.shape
+    cols = span // 2
+    rows = blocks * kept_ref.shape[1]
     stripe = depth // stripes
     core = lax.axis_index("c")
     groups = []
@@ -231,23 +232,25 @@
             copy.start()
     pick_rows(rows_ref, kept_ref)
     acc = [jnp.zeros((rows, 2 * units), F32) for _ in range(experts)]
-    square = jnp.zeros((rows, cols), F32)
+    square = jnp.zeros((rows, span), F32)
     for y in range(stripes):
         for copy in queue[y + ahead]:
             copy.start()
         for copy in groups[y]:
             copy.wait()
         for s in range(sides):
-            for other in range(2):
-                part = core if other == 0 else 1 - core
-                first = other * (lanes // 2)
-                block = rows_ref[y * sides + s, :, first:first + cols].astype(F32)
-                square = square + block * block
-                scaled = (block * gain_ref[y * 2 + part, pl.ds(s, 1), :]).astype(BF)
-                at = pl.ds(pl.multiple_of(y * stripe + part * (stripe // 2) + s * cols, 16), cols)
-                for e in range(experts):
-                    both = jnp.concatenate([wg[e, at, :], wu[e, at, :]], axis=1)
-                    acc[e] = acc[e] + jnp.dot(scaled, both, preferred_element_type=F32)
+            block = unpack(rows_ref[y * sides + s])
+            square = square + block * block
+            scaled = (block * gain_ref[y, pl.ds(s, 1), :]).astype(BF)
+            own, oth = (
+                pl.ds(pl.multiple_of(y * stripe + part * (stripe // 2) + s * cols, 16), cols)
+                for part in (core, 1 - core)
+            )
+            for e in range(experts):
+                both = jnp.concatenate(
+                    [jnp.concatenate([wg[e, at, :], wu[e, at, :]], axis=1) for at in (own, oth)], axis=0
+                )
+                acc[e] = acc[e] + jnp.dot(scaled, both, preferred_element_type=F32)
     inverse = lax.rsqrt(jnp.sum(square, axis=-1, keepdims=True) / depth + EPS)
     acts = []
     for e in range(experts):
@@ -271,23 +274,32 @@
             out_ref[n * blocks + k] = jnp.concatenate([left[at], right[at]], axis=0).astype(BF)
 
 
+def unpack(block):
+    block = block.astype(F32)
+    rows = block.shape[0] * 2 // 7
+    last = block[3 * rows:]
+    last = jnp.concatenate([last, pltpu.roll(last, 64, 1)], axis=0)
+    return jnp.concatenate([block[:rows], block[rows:2 * rows], block[2 * rows:3 * rows], last[:, :64]], axis=1)
+
+
 def pick_rows(blocks_ref, kept_ref):
     sides, toks, _ = kept_ref.shape
     at = (lax.axis_index("y") * sides + lax.axis_index("side")) * toks
-    group = pl.multiple_of(at // 16 * 16, 16)
     for s in range(sides):
-        rows = blocks_ref[lax.axis_index("hg") * sides + s, pl.ds(group, 16), :].astype(F32)
+        rows = unpack(blocks_ref[lax.axis_index("hg") * sides + s])
         found = rows[:toks]
-        for k in range(1, 16 // toks):
-            found = jnp.where(at - group == k * toks, rows[k * toks:(k + 1) * toks], found)
+        for k in range(1, rows.shape[0] // toks):
+            found = jnp.where(at == k * toks, rows[k * toks:(k + 1) * toks], found)
         kept_ref[s] = found.astype(BF)
 
 
 def run_experts(rows, gain, share, own, other, hgs, ahead=3):
     local, depth, units = own[0].shape
     experts = 2 * local
-    blocks, count, lanes = rows.shape
-    toks = count // blocks
+    blocks = rows.shape[0]
+    stripes, sides, span = gain.shape
+    toks = rows.shape[1] * rows.shape[2] // span // blocks
+    count = blocks * toks
     vmem = pl.BlockSpec(memory_space=pltpu.VMEM)
     hbm = pl.BlockSpec(memory_space=pltpu.HBM)
     weights = [pltpu.with_memory_space_constraint(a, pltpu.HBM) for a in (*own, *other)]
@@ -295,7 +307,7 @@
         functools.partial(experts_kernel, ahead=ahead),
         out_shape=(
             pltpu.VMEM((hgs * blocks, 2 * toks, depth // hgs // 2), BF),
-            jax.ShapeDtypeStruct((gain.shape[1], toks, lanes), BF),
+            jax.ShapeDtypeStruct((sides, toks, span), BF),
         ),
         in_specs=[vmem] * 3 + [hbm] * 6,
         out_specs=[vmem] * 2,
@@ -303,13 +315,59 @@
             pltpu.VMEM((experts, depth, units), BF),
             pltpu.VMEM((experts, depth, units), BF),
             pltpu.VMEM((experts, units, depth), BF),
-            pltpu.SemaphoreType.DMA((blocks // gain.shape[1] * 4,)),
+            pltpu.SemaphoreType.DMA((stripes * 4,)),
             pltpu.SemaphoreType.DMA((hgs * 2,)),
         ],
         compiler_params=pltpu.CompilerParams(vmem_limit_bytes=32 * 1024 * 1024),
         cost_estimate=pl.CostEstimate(flops=count * depth * 3072, bytes_accessed=24_000_000, transcendentals=0),
         name="experts",
     )(rows, gain, share, *weights)
+
+
+def project_kernel(here_ref, own_ref, oth_ref, out_ref, xs, ext, *, n_val):
+    planes, toks, _ = here_ref.shape
+    cols = own_ref.shape[0]
+    rows = planes * toks
+    core = lax.axis_index("c")
+    for p in range(planes):
+        xs[pl.ds(p * toks, toks), :] = here_ref[p, :, :n_val].astype(F32)
+        for c in range(2):
+            tiles = here_ref[p, :, n_val + c * 128:n_val + (c + 1) * 128].astype(F32)
+            for t in range(3):
+                ext[c, pl.ds(p, 1), t * 128:(t + 1) * 128] = tiles[t:t + 1]
+    x = xs[...].astype(BF)
+    row = lax.broadcasted_iota(jnp.int32, (rows, planes), 0)
+    col = lax.broadcasted_iota(jnp.int32, (rows, planes), 1)
+    place = (row == col * toks + lax.axis_index("hg")).astype(BF)
+    parts = []
+    for w_ref, part in ((own_ref, core), (oth_ref, 1 - core)):
+        block = (lax.axis_index("y") * 2 + part) * 4 + lax.axis_index("side")
+        shift = lax.rem(block * cols, 128)
+        window = jnp.where(part == 0, ext[0], ext[1])
+        window = pltpu.roll(window, lax.rem(384 - shift, 384), 1)[:, :cols].astype(BF)
+        product = lax.dot_general(x, w_ref[...], (((1,), (1,)), ((), ())), preferred_element_type=F32)
+        parts.append(product + jnp.dot(place, window, preferred_element_type=F32))
+    whole = jnp.concatenate(parts, axis=1)
+    for t in range(3):
+        out_ref[pl.ds(t * rows, rows), :] = whole[:, t * 128:(t + 1) * 128].astype(BF)
+    last = jnp.concatenate([whole[:rows // 2, 384:], whole[rows // 2:, 384:]], axis=1)
+    out_ref[pl.ds(3 * rows, rows // 2), :] = last.astype(BF)
+
+
+def project(here, w_out, out_there, n_val):
+    planes, toks, _ = here.shape
+    vmem = pl.BlockSpec(memory_space=pltpu.VMEM)
+    rows = planes * toks
+    return pl.pallas_call(
+        functools.partial(project_kernel, n_val=n_val),
+        out_shape=pltpu.VMEM((rows * 7 // 2, 128), BF),
+        in_specs=[vmem] * 3,
+        out_specs=vmem,
+        scratch_shapes=[pltpu.VMEM((rows, n_val), F32), pltpu.VMEM((2, planes, 384), F32)],
+        compiler_params=pltpu.CompilerParams(vmem_limit_bytes=12 * 1024 * 1024),
+        cost_estimate=pl.CostEstimate(flops=4 * rows * n_val * 224, bytes_accessed=2_500_000, transcendentals=0),
+        name="project",
+    )(here, w_out.T, out_there.T)
 
 
 def body(
@@ -326,25 +384,13 @@
 
     message = attention(q_nope, q_rope, w_absorb, cache_latent, cache_rope, lengths, w_value, residual, routes, gate_int,
                         planes, sides, experts_all)
-    message, w_out_, norm_gain = lax.optimization_barrier((message, w_out, norm_gain))
+    message, w_out_, w_gate_, w_up_, w_down_ = lax.optimization_barrier((message, w_out, w_gate, w_up, w_down))
     out_there = lax.ppermute(w_out_, "c", SWAP)
-    gain = norm_gain.astype(F32).reshape(ys * cores, sides, cols)
-    gain, w_gate_, w_up_, w_down_ = lax.optimization_barrier((gain, w_gate, w_up, w_down))
     other = tuple(lax.ppermute(w, "c", SWAP) for w in (w_gate_, w_up_, w_down_))
     here = lax.all_to_all(message, ("y", "side"), 0, 0, tiled=True)
     n_val = w_absorb.shape[0] * VDIM
-    values = here[..., :n_val].reshape(planes * toks, n_val)
+    partial = project(here, w_out, out_there, n_val)
     extra = here[..., n_val:]
-    is_row = (jnp.arange(toks) == hg)[None, :, None]
-    halves = []
-    for part, weights in ((core, w_out), (1 - core, out_there)):
-        window = lax.dynamic_slice_in_dim(extra[:, :3], part * 128, 128, 2).reshape(planes, 3 * 128)
-        block = (y * cores + part) * sides + side
-        mine = lax.dynamic_slice_in_dim(window, lax.rem(block * cols, 128), cols, 1)[:, None]
-        half = jnp.dot(values, weights, preferred_element_type=F32).reshape(planes, toks, cols)
-        half = (half + jnp.where(is_row, mine.astype(F32), 0.0)).astype(BF).reshape(planes * toks, cols)
-        halves.append(jnp.pad(half, ((0, 0), (0, -cols % 128))))
-    partial = jnp.concatenate(halves, axis=1)
     gates = extra[:, 3, :toks * experts_all].reshape(planes * toks, experts_all).astype(F32)
     total = jnp.sum(gates, axis=1, keepdims=True)
     share = jnp.concatenate(
@@ -354,15 +400,16 @@
         ],
         axis=1,
     ) * (ROUTE_SCALE / total)
-    got, share = lax.optimization_barrier((lax.ppermute(partial, "hg", PAIRS_A), share))
+    gain = norm_gain.astype(F32).reshape(ys, cores, sides, cols)
+    gain = jnp.where(core == 0, gain, gain[:, ::-1]).transpose(0, 2, 1, 3).reshape(ys, sides, cores * cols)
+    got, share, gain = lax.optimization_barrier((lax.ppermute(partial, "hg", PAIRS_A), share, gain))
     pair = (partial.astype(F32) + got.astype(F32)).astype(BF)
     hidden = (pair.astype(F32) + lax.ppermute(pair, "hg", PAIRS_B).astype(F32)).astype(BF)
 
     rows = lax.all_to_all(jnp.broadcast_to(hidden[None], (planes,) + hidden.shape), ("y", "side"), 0, 0, tiled=True)
     summed, kept = run_experts(rows, gain, share, (w_gate, w_up, w_down), other, hgs)
     quarter = width // hgs
-    lanes = kept.shape[2] // 2
-    own_piece, oth_piece = kept[..., :cols], kept[..., lanes:lanes + cols]
+    own_piece, oth_piece = kept[..., :cols], kept[..., cols:]
     kept = jnp.where(core == 0, jnp.concatenate([own_piece, oth_piece]), jnp.concatenate([oth_piece, own_piece]))
     kept = kept.transpose(1, 0, 2).reshape(toks, quarter)
     parts = lax.all_to_all(summed, ("hg", "y", "side"), 0, 0, tiled=True)

time: 86.8 us -> 83.6 us (0.963)
  blocking collectives: 18 us -> 15.7 us
    all_to_all x1, blocking collectives: 18 us -> 15.7 us  [body(): lax.all_to_all(jnp.broadcast_to(hidden[None], (planes,) + hidden.shape),...]
    ppermute x3, starting transfers between devices: 0.68 us -> 1.96 us  [body(): lax.ppermute(w, 'c', SWAP)]
    pallas_call x1, Pallas kernels: 7.07 us -> 5.96 us  [attention(): pl.pallas_call(functools.partial(attention_kernel, span=span, ahead=ahead...]
    pallas_call x0 -> x1, Pallas kernels: none -> 0.98 us  [project(): pl.pallas_call(functools.partial(project_kernel, n_val=n_val), out_shape=...]
    all_to_all x1, starting transfers between devices: 9.12 us -> 8.15 us  [body(): here = lax.all_to_all(message, ('y', 'side'), 0, 0, tiled=True)]
  transfers between devices with their start and end apart: 8 -> 8, of which waited for: 4 -> 4; matrix products, arithmetic and copies ran while one was open for 2% -> 1% of each run, Pallas kernels for 0% -> 1%
where the time goes in v6:
time: 83.6 us; the launch traced here: 82.6 us
  waiting for transfers between devices  27.6 us (33%)
  starting transfers between devices  21.4 us (26%)
  Pallas kernels  16.1 us (19%)
  blocking collectives  15.7 us (19%)
  other arithmetic  1.06 us (1%)
    all_to_all x1, blocking collectives, body(): lax.all_to_all(jnp.broadcast_to(hidden[None], (planes,) + hidden.shape),...  15.7 us
    all_to_all x1, waiting for transfers between devices, body(): parts = lax.all_to_all(summed, ('hg', 'y', 'side'), 0, 0, tiled=True)  13.5 us
    pallas_call x1, Pallas kernels, run_experts(): pl.pallas_call(functools.partial(experts_kernel, ahead=ahead), out_shape=...  9.12 us
    all_to_all x1, waiting for transfers between devices, body(): here = lax.all_to_all(message, ('y', 'side'), 0, 0, tiled=True)  8.82 us
    all_to_all x1, starting transfers between devices, body(): here = lax.all_to_all(message, ('y', 'side'), 0, 0, tiled=True)  8.15 us
    all_to_all x1, starting transfers between devices, body(): parts = lax.all_to_all(summed, ('hg', 'y', 'side'), 0, 0, tiled=True)  6.83 us
    pallas_call x1, Pallas kernels, attention(): pl.pallas_call(functools.partial(attention_kernel, span=span, ahead=ahead...  5.96 us
    ppermute x1, starting transfers between devices, body(): lax.ppermute(pair, 'hg', PAIRS_B).astype(F32)  2.84 us
  transfers between devices with their start and end apart: 8, of which 4 were waited for; matrix products, arithmetic and copies ran while one was open for 1% of the time, Pallas kernels for 1%

profile of v6, /device:TPU:0, one launch (start us, length us, event | category | flops | bytes accessed | tf_op | source)
XLA Modules:
  0.0 82.6 jit_solution(12058025918708957262)
XLA Ops:
  0.0 0.0 copy-start
  0.0 0.0 copy-start.1
  0.0 6.0 %attention.1 = bf16[16,4,2304]{2,1,0:T(4,128)(2,1)} custom-call(s32[2]{0:T(128)} %len_hbm.1, s32[4,4]{1,0:T(4,128)} %routes_hbm.1, s32[4,4]{1,0:T(4,128)} %ints_hbm.1, bf16[4,2048]{1,0:T(4,128)(2,1)} %qn_hbm.1, bf16[4,1024]{1,0:T(4,128)(2,1)} %qr_hbm.1, bf16[4,7168]{1,0:T(4,128)(2,1)} %res_hbm.1, bf16[16,128,512]{2,1,0:T(8,128)(2,1)} %wa_hbm.1, ...), custom_call_target="tpu_custom_call" | custom-call | tf_op jit(solution)/shard_map/attention/pallas_call | solution.py:167
  6.0 1.4 %collective-permute-start.3 = (bf16[2,7168,128]{2,1,0:T(8,128)(2,1)}, bf16[2,7168,128]{2,1,0:T(8,128)(2,1)}, u32[]{:S(2)}, u32[]{:S(2)}) collective-permute-start(bf16[2,7168,128]{2,1,0:T(8,128)(2,1)} %wg0.1), channel_id=1, source_target_pairs={{0,4},{4,0},{1,5},{5,1},{2,6},{6,2},{3,7},{7,3},{8,12},{12,8},{9,1... | collective-permute-start | bytes 11010056 | tf_op jit(solution)/shard_map/ppermute | solution.py:389
  7.4 0.1 collective-permute-start.4
  7.5 0.4 collective-permute-start.5
  7.9 0.0 copy-done
  7.9 0.1 collective-permute-start
  8.0 8.2 %all-to-all-start = ((bf16[16,4,2304]{2,1,0:T(4,128)(2,1)}), bf16[16,4,2304]{2,1,0:T(4,128)(2,1)S(1)}, u32[]{:S(2)}, u32[]{:S(2)}) async-start(bf16[16,4,2304]{2,1,0:T(4,128)(2,1)} %attention.1), calls=%async_computation | async-start | bytes 589824 | tf_op jit(solution)/shard_map/all_to_all | solution.py:390
  16.2 0.0 copy-done.1
  16.2 0.1 reshape.24
  16.4 0.1 reshape.21.gain_ref
  16.5 8.8 %all-to-all-done.here_ref = bf16[16,4,2304]{2,1,0:T(4,128)(2,1)S(1)} async-done(((bf16[16,4,2304]{2,1,0:T(4,128)(2,1)}), bf16[16,4,2304]{2,1,0:T(4,128)(2,1)S(1)}, u32[]{:S(2)}, u32[]{:S(2)}) %all-to-all-start) | async-done | bytes 294944 | tf_op jit(solution)/shard_map/all_to_all | solution.py:390
  25.3 0.1 reshape.22
  25.4 0.1 reduce_sum.18
  25.5 0.1 constant_dynamic-slice_fusion.1
  25.6 0.0 collective-permute-done
  25.6 1.0 %project.1 = bf16[224,128]{1,0:T(8,128)(2,1)S(1)} custom-call(bf16[16,4,2304]{2,1,0:T(4,128)(2,1)S(1)} %all-to-all-done.here_ref, bf16[224,2048]{1,0:T(8,128)(2,1)S(1)} %bitcast.6, bf16[224,2048]{1,0:T(8,128)(2,1)S(1)} %bitcast.7), custom_call_target="tpu_custom_call" | custom-call | flops 117440512 | bytes 2500000 | tf_op jit(solution)/shard_map/project/pallas_call | solution.py:361
  26.6 1.5 %collective-permute-start.1 = (bf16[224,128]{1,0:T(8,128)(2,1)S(1)}, bf16[224,128]{1,0:T(8,128)(2,1)S(1)}, u32[]{:S(2)}, u32[]{:S(2)}) collective-permute-start(bf16[224,128]{1,0:T(8,128)(2,1)S(1)} %project.1), channel_id=1, source_target_pairs={{0,32},{32,0},{64,96},{96,64},{1,33},{33,1},{65,97},{97,65},{2,34}... | collective-permute-start | bytes 172040 | tf_op jit(solution)/shard_map/ppermute | solution.py:405
  28.1 0.1 maximum_multiply_fusion.share_ref
  28.2 2.6 %collective-permute-done.1 = bf16[224,128]{1,0:T(8,128)(2,1)S(1)} collective-permute-done((bf16[224,128]{1,0:T(8,128)(2,1)S(1)}, bf16[224,128]{1,0:T(8,128)(2,1)S(1)}, u32[]{:S(2)}, u32[]{:S(2)}) %collective-permute-start.1) | collective-permute-done | bytes 57376 | tf_op jit(solution)/shard_map/ppermute | solution.py:405
  30.8 2.8 %collective-permute-start.2 = (bf16[224,128]{1,0:T(8,128)(2,1)S(1)}, bf16[224,128]{1,0:T(8,128)(2,1)S(1)}, u32[]{:S(2)}, u32[]{:S(2)}) collective-permute-start(bf16[224,128]{1,0:T(8,128)(2,1)S(1)} %add_convert_fusion.1), channel_id=1, source_target_pairs={{32,64},{64,32},{96,0},{0,96},{33,65},{65,33},{97,1},{1,97},{34,66... | collective-permute-start | bytes 172040 | tf_op jit(solution)/shard_map/ppermute | solution.py:407
  33.7 2.6 %collective-permute-done.2 = bf16[224,128]{1,0:T(8,128)(2,1)S(1)} collective-permute-done((bf16[224,128]{1,0:T(8,128)(2,1)S(1)}, bf16[224,128]{1,0:T(8,128)(2,1)S(1)}, u32[]{:S(2)}, u32[]{:S(2)}) %collective-permute-start.2) | collective-permute-done | bytes 57376 | tf_op jit(solution)/shard_map/ppermute | solution.py:407
  36.3 0.1 broadcast_in_dim.2
  36.4 15.7 %all_to_all.15.rows_ref = bf16[16,224,128]{2,1,0:T(8,128)(2,1)S(1)} all-to-all(bf16[16,224,128]{2,1,0:T(8,128)(2,1)S(1)} %broadcast_in_dim.2), channel_id=1, replica_groups=mesh['hg'=4,'y'=4,'c'=2,'side'=4] {'y','side'}, dimensions={0} | all-to-all | bytes 1835008 | tf_op jit(solution)/shard_map/all_to_all | solution.py:409
  52.1 0.0 collective-permute-done.3.wg1
  52.1 0.0 collective-permute-done.4.wu1
  52.2 0.0 collective-permute-done.5.wd1
  52.2 9.1 %experts.1 = (bf16[64,8,896]{2,1,0:T(8,128)(2,1)}, bf16[4,4,448]{2,1,0:T(4,128)(2,1)S(1)}) custom-call(bf16[16,224,128]{2,1,0:T(8,128)(2,1)S(1)} %all_to_all.15.rows_ref, f32[4,4,448]{2,1,0:T(4,128)S(1)} %reshape.21.gain_ref, f32[64,4]{1,0:T(8,128)S(1)} %maximum_multiply_fusion.share_ref, bf16[2,7168,128]{2,1,0:T(8,128)(2,1)} %wg0.1, ...), custom_call_target="tpu_custom_call" | custom-call | flops 1409286144 | bytes 24000000 | tf_op jit(solution)/shard_map/experts/pallas_call | solution.py:306
  61.3 6.8 %all-to-all-start.2 = ((bf16[64,8,896]{2,1,0:T(8,128)(2,1)}), bf16[64,8,896]{2,1,0:T(8,128)(2,1)S(1)}, u32[]{:S(2)}, u32[]{:S(2)}) async-start(bf16[64,8,896]{2,1,0:T(8,128)(2,1)} %get-tuple-element.24), calls=%async_computation.2 | async-start | bytes 1835008 | tf_op jit(solution)/shard_map/all_to_all | solution.py:415
  68.1 0.1 fusion.4
  68.2 0.1 reshape.25
  68.3 13.5 %all-to-all-done.2 = bf16[64,8,896]{2,1,0:T(8,128)(2,1)S(1)} async-done(((bf16[64,8,896]{2,1,0:T(8,128)(2,1)}), bf16[64,8,896]{2,1,0:T(8,128)(2,1)S(1)}, u32[]{:S(2)}, u32[]{:S(2)}) %all-to-all-start.2) | async-done | bytes 917536 | tf_op jit(solution)/shard_map/all_to_all | solution.py:415
  81.8 0.2 convert_reduce_fusion
  82.0 0.6 fusion.1
  (9 shorter events, 0.1 us)
Async XLA Ops:
  0.0 7.9 %copy-start = (bf16[2048,224]{0,1:T(8,128)(2,1)S(1)}, bf16[2048,224]{0,1:T(8,128)(2,1)}, u32[]{:S(2)}) copy-start(bf16[2048,224]{0,1:T(8,128)(2,1)} %param.22) | copy-start | bytes 2752516
  0.0 16.2 %copy-start.1 = (bf16[7168]{0:T(1024)(128)(2,1)S(1)}, bf16[7168]{0:T(1024)(128)(2,1)}, u32[]{:S(2)}) copy-start(bf16[7168]{0:T(1024)(128)(2,1)} %param.24) | copy-start | bytes 43012
  6.0 46.2 %collective-permute-start.3 = (bf16[2,7168,128]{2,1,0:T(8,128)(2,1)}, bf16[2,7168,128]{2,1,0:T(8,128)(2,1)}, u32[]{:S(2)}, u32[]{:S(2)}) collective-permute-start(bf16[2,7168,128]{2,1,0:T(8,128)(2,1)} %wg0.1), channel_id=1, source_target_pairs={{0,4},{4,0},{1,5},{5,1},{2,6},{6,2},{3,7},{7,3},{8,12},{12,8},{9,1... | collective-permute-start | bytes 11010056 | tf_op jit(solution)/shard_map/ppermute | solution.py:389
  7.4 44.7 %collective-permute-start.4 = (bf16[2,7168,128]{2,1,0:T(8,128)(2,1)}, bf16[2,7168,128]{2,1,0:T(8,128)(2,1)}, u32[]{:S(2)}, u32[]{:S(2)}) collective-permute-start(bf16[2,7168,128]{2,1,0:T(8,128)(2,1)} %wu0.1), channel_id=1, source_target_pairs={{0,4},{4,0},{1,5},{5,1},{2,6},{6,2},{3,7},{7,3},{8,12},{12,8},{9,1... | collective-permute-start | bytes 11010056 | tf_op jit(solution)/shard_map/ppermute | solution.py:389
  7.5 44.6 %collective-permute-start.5 = (bf16[2,128,7168]{2,1,0:T(8,128)(2,1)}, bf16[2,128,7168]{2,1,0:T(8,128)(2,1)}, u32[]{:S(2)}, u32[]{:S(2)}) collective-permute-start(bf16[2,128,7168]{2,1,0:T(8,128)(2,1)} %wd0.1), channel_id=1, source_target_pairs={{0,4},{4,0},{1,5},{5,1},{2,6},{6,2},{3,7},{7,3},{8,12},{12,8},{9,1... | collective-permute-start | bytes 11010056 | tf_op jit(solution)/shard_map/ppermute | solution.py:389
  7.9 17.7 %collective-permute-start = (bf16[2048,224]{0,1:T(8,128)(2,1)S(1)}, bf16[2048,224]{0,1:T(8,128)(2,1)S(1)}, u32[]{:S(2)}, u32[]{:S(2)}) collective-permute-start(bf16[2048,224]{0,1:T(8,128)(2,1)S(1)} %copy-done), channel_id=1, source_target_pairs={{0,4},{4,0},{1,5},{5,1},{2,6},{6,2},{3,7},{7,3},{8,12},{12,8},{9,1... | collective-permute-start | bytes 2752520 | tf_op jit(solution)/shard_map/ppermute | solution.py:388
  8.0 17.3 %all-to-all-start = ((bf16[16,4,2304]{2,1,0:T(4,128)(2,1)}), bf16[16,4,2304]{2,1,0:T(4,128)(2,1)S(1)}, u32[]{:S(2)}, u32[]{:S(2)}) async-start(bf16[16,4,2304]{2,1,0:T(4,128)(2,1)} %attention.1), calls=%async_computation | async-start | bytes 589824 | tf_op jit(solution)/shard_map/all_to_all | solution.py:390
  26.6 4.2 %collective-permute-start.1 = (bf16[224,128]{1,0:T(8,128)(2,1)S(1)}, bf16[224,128]{1,0:T(8,128)(2,1)S(1)}, u32[]{:S(2)}, u32[]{:S(2)}) collective-permute-start(bf16[224,128]{1,0:T(8,128)(2,1)S(1)} %project.1), channel_id=1, source_target_pairs={{0,32},{32,0},{64,96},{96,64},{1,33},{33,1},{65,97},{97,65},{2,34}... | collective-permute-start | bytes 172040 | tf_op jit(solution)/shard_map/ppermute | solution.py:405
  30.8 5.5 %collective-permute-start.2 = (bf16[224,128]{1,0:T(8,128)(2,1)S(1)}, bf16[224,128]{1,0:T(8,128)(2,1)S(1)}, u32[]{:S(2)}, u32[]{:S(2)}) collective-permute-start(bf16[224,128]{1,0:T(8,128)(2,1)S(1)} %add_convert_fusion.1), channel_id=1, source_target_pairs={{32,64},{64,32},{96,0},{0,96},{33,65},{65,33},{97,1},{1,97},{34,66... | collective-permute-start | bytes 172040 | tf_op jit(solution)/shard_map/ppermute | solution.py:407
  61.3 20.5 %all-to-all-start.2 = ((bf16[64,8,896]{2,1,0:T(8,128)(2,1)}), bf16[64,8,896]{2,1,0:T(8,128)(2,1)S(1)}, u32[]{:S(2)}, u32[]{:S(2)}) async-start(bf16[64,8,896]{2,1,0:T(8,128)(2,1)} %get-tuple-element.24), calls=%async_computation.2 | async-start | bytes 1835008 | tf_op jit(solution)/shard_map/all_to_all | solution.py:415

commit v7 on v6

--- a/solution.py
+++ b/solution.py
@@ -198,7 +198,26 @@
     ))
 
 
-def experts_kernel(rows_ref, gain_ref, share_ref, wg0, wu0, wd0, wg1, wu1, wd1, out_ref, kept_ref,
+def fetch_kernel(w_ref, o_ref, sem):
+    copy = pltpu.make_async_copy(w_ref.at[:, pl.ds(0, o_ref.shape[1]), :], o_ref, sem)
+    copy.start()
+    copy.wait()
+
+
+def fetch(w, rows, name):
+    return pl.pallas_call(
+        fetch_kernel,
+        out_shape=pltpu.VMEM((w.shape[0], rows, w.shape[2]), w.dtype),
+        in_specs=[pl.BlockSpec(memory_space=pltpu.HBM)],
+        out_specs=pl.BlockSpec(memory_space=pl.ANY),
+        scratch_shapes=[pltpu.SemaphoreType.DMA],
+        cost_estimate=pl.CostEstimate(flops=0, bytes_accessed=4_000_000, transcendentals=0),
+        compiler_params=pltpu.CompilerParams(vmem_limit_bytes=4 * 1024 * 1024),
+        name=name,
+    )(pltpu.with_memory_space_constraint(w, pltpu.HBM))
+
+
+def experts_kernel(rows_ref, gain_ref, share_ref, pre_g, pre_u, wg0, wu0, wd0, wg1, wu1, wd1, out_ref, kept_ref,
                    wg, wu, wd, sem, sem_down, *, ahead):
     local, depth, units = wg0.shape
     experts = 2 * local
@@ -212,9 +231,11 @@
     for y in range(stripes):
         at = pl.ds(y * stripe, stripe)
         groups.append([
-            pltpu.make_async_copy(src.at[:, at, :], dst.at[pl.ds(k * local, local), at, :], sem.at[y * 4 + 2 * k + j])
+            pltpu.make_async_copy(
+                pre.at[:, at, :] if k == 0 and (y + 1) * stripe <= pre.shape[1] else src.at[:, at, :], dst.at[pl.ds(k * local, local), at, :], sem.at[y * 4 + 2 * k + j]
+            )
             for k in range(2)
-            for j, (src, dst) in enumerate((((wg0, wg1)[k], wg), ((wu0, wu1)[k], wu)))
+            for j, (src, dst, pre) in enumerate((((wg0, wg1)[k], wg, pre_g), ((wu0, wu1)[k], wu, pre_u)))
         ])
     messages, lines, tile = out_ref.shape
     toks = lines // 2
@@ -293,7 +314,7 @@
         kept_ref[s] = found.astype(BF)
 
 
-def run_experts(rows, gain, share, own, other, hgs, ahead=3):
+def run_experts(rows, gain, share, early, own, other, hgs, ahead=3):
     local, depth, units = own[0].shape
     experts = 2 * local
     blocks = rows.shape[0]
@@ -309,7 +330,7 @@
             pltpu.VMEM((hgs * blocks, 2 * toks, depth // hgs // 2), BF),
             jax.ShapeDtypeStruct((sides, toks, span), BF),
         ),
-        in_specs=[vmem] * 3 + [hbm] * 6,
+        in_specs=[vmem] * 3 + [pl.BlockSpec(memory_space=pl.ANY)] * 2 + [hbm] * 6,
         out_specs=[vmem] * 2,
         scratch_shapes=[
             pltpu.VMEM((experts, depth, units), BF),
@@ -321,7 +342,7 @@
         compiler_params=pltpu.CompilerParams(vmem_limit_bytes=32 * 1024 * 1024),
         cost_estimate=pl.CostEstimate(flops=count * depth * 3072, bytes_accessed=24_000_000, transcendentals=0),
         name="experts",
-    )(rows, gain, share, *weights)
+    )(rows, gain, share, *early, *weights)
 
 
 def project_kernel(here_ref, own_ref, oth_ref, out_ref, xs, ext, *, n_val):
@@ -402,12 +423,17 @@
     ) * (ROUTE_SCALE / total)
     gain = norm_gain.astype(F32).reshape(ys, cores, sides, cols)
     gain = jnp.where(core == 0, gain, gain[:, ::-1]).transpose(0, 2, 1, 3).reshape(ys, sides, cores * cols)
-    got, share, gain = lax.optimization_barrier((lax.ppermute(partial, "hg", PAIRS_A), share, gain))
+    partial, w_gate_ = lax.optimization_barrier((partial, w_gate))
+    gate_early = fetch(w_gate_, w_gate.shape[1], "fetch_gate")
+    got, share, gain, gate_early = lax.optimization_barrier((lax.ppermute(partial, "hg", PAIRS_A), share, gain, gate_early))
     pair = (partial.astype(F32) + got.astype(F32)).astype(BF)
-    hidden = (pair.astype(F32) + lax.ppermute(pair, "hg", PAIRS_B).astype(F32)).astype(BF)
+    pair, w_up_ = lax.optimization_barrier((pair, w_up))
+    up_early = fetch(w_up_, w_up.shape[1], "fetch_up")
+    got, up_early = lax.optimization_barrier((lax.ppermute(pair, "hg", PAIRS_B), up_early))
+    hidden = (pair.astype(F32) + got.astype(F32)).astype(BF)
 
     rows = lax.all_to_all(jnp.broadcast_to(hidden[None], (planes,) + hidden.shape), ("y", "side"), 0, 0, tiled=True)
-    summed, kept = run_experts(rows, gain, share, (w_gate, w_up, w_down), other, hgs)
+    summed, kept = run_experts(rows, gain, share, (gate_early, up_early), (w_gate, w_up, w_down), other, hgs)
     quarter = width // hgs
     own_piece, oth_piece = kept[..., :cols], kept[..., cols:]
     kept = jnp.where(core == 0, jnp.concatenate([own_piece, oth_piece]), jnp.concatenate([oth_piece, own_piece]))

time: 83.6 us -> 82 us (0.981)
  waiting for transfers between devices: 27.6 us -> 23.4 us
  Pallas kernels: 16.1 us -> 19.6 us
  starting transfers between devices: 21.4 us -> 20.1 us
    pallas_call x0 -> x2, Pallas kernels: none -> 4.1 us  [fetch(): pl.pallas_call(fetch_kernel, out_shape=pltpu.VMEM((w.shape[0], rows, w.sh...]
    ppermute x1, waiting for transfers between devices: 2.6 us -> 0.55 us  [body(): lax.ppermute(partial, 'hg', PAIRS_A)]
    ppermute x1, waiting for transfers between devices: 2.63 us -> 0.57 us  [body(): lax.ppermute(pair, 'hg', PAIRS_B)]
    pallas_call x1, Pallas kernels: 9.12 us -> 7.45 us  [run_experts(): pl.pallas_call(functools.partial(experts_kernel, ahead=ahead), out_shape=...]
    ppermute x3, starting transfers between devices: 1.96 us -> 0.68 us  [body(): lax.ppermute(w, 'c', SWAP)]
    pallas_call x1, Pallas kernels: 5.96 us -> 7.09 us  [attention(): pl.pallas_call(functools.partial(attention_kernel, span=span, ahead=ahead...]
  transfers between devices with their start and end apart: 8 -> 8, of which waited for: 4 -> 4; matrix products, arithmetic and copies ran while one was open for 1% -> 1% of each run, Pallas kernels for 1% -> 6%
where the time goes in v7:
time: 82 us; the launch traced here: 81.1 us
  waiting for transfers between devices  23.4 us (29%)
  starting transfers between devices  20.1 us (25%)
  Pallas kernels  19.6 us (24%)
  blocking collectives  16 us (20%)
  other arithmetic  1.06 us (1%)
    all_to_all x1, blocking collectives, body(): lax.all_to_all(jnp.broadcast_to(hidden[None], (planes,) + hidden.shape),...  16 us
    all_to_all x1, waiting for transfers between devices, body(): parts = lax.all_to_all(summed, ('hg', 'y', 'side'), 0, 0, tiled=True)  13.5 us
    all_to_all x1, waiting for transfers between devices, body(): here = lax.all_to_all(message, ('y', 'side'), 0, 0, tiled=True)  8.82 us
    all_to_all x1, starting transfers between devices, body(): here = lax.all_to_all(message, ('y', 'side'), 0, 0, tiled=True)  8.14 us
    pallas_call x1, Pallas kernels, run_experts(): pl.pallas_call(functools.partial(experts_kernel, ahead=ahead), out_shape=...  7.45 us
    pallas_call x1, Pallas kernels, attention(): pl.pallas_call(functools.partial(attention_kernel, span=span, ahead=ahead...  7.09 us
    all_to_all x1, starting transfers between devices, body(): parts = lax.all_to_all(summed, ('hg', 'y', 'side'), 0, 0, tiled=True)  6.49 us
    pallas_call x2, Pallas kernels, fetch(): pl.pallas_call(fetch_kernel, out_shape=pltpu.VMEM((w.shape[0], rows, w.sh...  4.1 us
  transfers between devices with their start and end apart: 8, of which 4 were waited for; matrix products, arithmetic and copies ran while one was open for 1% of the time, Pallas kernels for 6%

profile of v7, /device:TPU:0, one launch (start us, length us, event | category | flops | bytes accessed | tf_op | source)
XLA Modules:
  0.0 81.1 jit_solution(14221583418944049567)
XLA Ops:
  0.0 0.0 copy-start
  0.0 0.0 copy-start.1
  0.0 7.1 %attention.1 = bf16[16,4,2304]{2,1,0:T(4,128)(2,1)} custom-call(s32[2]{0:T(128)} %len_hbm.1, s32[4,4]{1,0:T(4,128)} %routes_hbm.1, s32[4,4]{1,0:T(4,128)} %ints_hbm.1, bf16[4,2048]{1,0:T(4,128)(2,1)} %qn_hbm.1, bf16[4,1024]{1,0:T(4,128)(2,1)} %qr_hbm.1, bf16[4,7168]{1,0:T(4,128)(2,1)} %res_hbm.1, bf16[16,128,512]{2,1,0:T(8,128)(2,1)} %wa_hbm.1, ...), custom_call_target="tpu_custom_call" | custom-call | tf_op jit(solution)/shard_map/attention/pallas_call | solution.py:167
  7.1 0.1 collective-permute-start.3
  7.2 0.5 collective-permute-start.4
  7.7 0.1 collective-permute-start.5
  7.8 0.0 copy-done
  7.8 0.4 collective-permute-start
  8.2 8.1 %all-to-all-start = ((bf16[16,4,2304]{2,1,0:T(4,128)(2,1)}), bf16[16,4,2304]{2,1,0:T(4,128)(2,1)S(1)}, u32[]{:S(2)}, u32[]{:S(2)}) async-start(bf16[16,4,2304]{2,1,0:T(4,128)(2,1)} %attention.1), calls=%async_computation | async-start | bytes 589824 | tf_op jit(solution)/shard_map/all_to_all | solution.py:411
  16.4 0.0 copy-done.1
  16.4 0.1 reshape.24
  16.5 0.1 reshape.21.gain_ref
  16.6 8.8 %all-to-all-done.here_ref = bf16[16,4,2304]{2,1,0:T(4,128)(2,1)S(1)} async-done(((bf16[16,4,2304]{2,1,0:T(4,128)(2,1)}), bf16[16,4,2304]{2,1,0:T(4,128)(2,1)S(1)}, u32[]{:S(2)}, u32[]{:S(2)}) %all-to-all-start) | async-done | bytes 294944 | tf_op jit(solution)/shard_map/all_to_all | solution.py:411
  25.5 0.1 reshape.22
  25.6 0.1 reduce_sum.18
  25.7 0.1 constant_dynamic-slice_fusion.1
  25.8 0.0 collective-permute-done
  25.8 1.0 %project.1 = bf16[224,128]{1,0:T(8,128)(2,1)S(1)} custom-call(bf16[16,4,2304]{2,1,0:T(4,128)(2,1)S(1)} %all-to-all-done.here_ref, bf16[224,2048]{1,0:T(8,128)(2,1)S(1)} %bitcast.6, bf16[224,2048]{1,0:T(8,128)(2,1)S(1)} %bitcast.7), custom_call_target="tpu_custom_call" | custom-call | flops 117440512 | bytes 2500000 | tf_op jit(solution)/shard_map/project/pallas_call | solution.py:382
  26.8 1.5 %collective-permute-start.1 = (bf16[224,128]{1,0:T(8,128)(2,1)S(1)}, bf16[224,128]{1,0:T(8,128)(2,1)S(1)}, u32[]{:S(2)}, u32[]{:S(2)}) collective-permute-start(bf16[224,128]{1,0:T(8,128)(2,1)S(1)} %project.1), channel_id=1, source_target_pairs={{0,32},{32,0},{64,96},{96,64},{1,33},{33,1},{65,97},{97,65},{2,34}... | collective-permute-start | bytes 172040 | tf_op jit(solution)/shard_map/ppermute | solution.py:428
  28.3 0.1 maximum_multiply_fusion.share_ref
  28.4 2.0 %fetch_gate.1.pre_g = bf16[2,7168,128]{2,1,0:T(8,128)(2,1)S(1)} custom-call(bf16[2,7168,128]{2,1,0:T(8,128)(2,1)} %wg0.1), custom_call_target="tpu_custom_call" | custom-call | bytes 4000000 | tf_op jit(solution)/shard_map/fetch_gate/pallas_call | solution.py:208
  30.4 0.5 collective-permute-done.1
  31.0 2.8 %collective-permute-start.2 = (bf16[224,128]{1,0:T(8,128)(2,1)S(1)}, bf16[224,128]{1,0:T(8,128)(2,1)S(1)}, u32[]{:S(2)}, u32[]{:S(2)}) collective-permute-start(bf16[224,128]{1,0:T(8,128)(2,1)S(1)} %add_convert_fusion.1), channel_id=1, source_target_pairs={{32,64},{64,32},{96,0},{0,96},{33,65},{65,33},{97,1},{1,97},{34,66... | collective-permute-start | bytes 172040 | tf_op jit(solution)/shard_map/ppermute | solution.py:432
  33.8 2.0 %fetch_up.1.pre_u = bf16[2,7168,128]{2,1,0:T(8,128)(2,1)S(1)} custom-call(bf16[2,7168,128]{2,1,0:T(8,128)(2,1)} %wu0.1), custom_call_target="tpu_custom_call" | custom-call | bytes 4000000 | tf_op jit(solution)/shard_map/fetch_up/pallas_call | solution.py:208
  35.9 0.6 collective-permute-done.2
  36.5 0.1 broadcast_in_dim.2
  36.6 16.0 %all_to_all.15.rows_ref = bf16[16,224,128]{2,1,0:T(8,128)(2,1)S(1)} all-to-all(bf16[16,224,128]{2,1,0:T(8,128)(2,1)S(1)} %broadcast_in_dim.2), channel_id=1, replica_groups=mesh['hg'=4,'y'=4,'c'=2,'side'=4] {'y','side'}, dimensions={0} | all-to-all | bytes 1835008 | tf_op jit(solution)/shard_map/all_to_all | solution.py:435
  52.7 0.0 collective-permute-done.3.wg1
  52.7 0.0 collective-permute-done.4.wu1
  52.7 0.0 collective-permute-done.5.wd1
  52.7 7.5 %experts.1 = (bf16[64,8,896]{2,1,0:T(8,128)(2,1)}, bf16[4,4,448]{2,1,0:T(4,128)(2,1)S(1)}) custom-call(bf16[16,224,128]{2,1,0:T(8,128)(2,1)S(1)} %all_to_all.15.rows_ref, f32[4,4,448]{2,1,0:T(4,128)S(1)} %reshape.21.gain_ref, f32[64,4]{1,0:T(8,128)S(1)} %maximum_multiply_fusion.share_ref, bf16[2,7168,128]{2,1,0:T(8,128)(2,1)S(1)} %fetch_gate.1.pre_g, ...), custom_call_target="tpu_custom_call" | custom-call | flops 1409286144 | bytes 24000000 | tf_op jit(solution)/shard_map/experts/pallas_call | solution.py:327
  60.1 6.5 %all-to-all-start.2 = ((bf16[64,8,896]{2,1,0:T(8,128)(2,1)}), bf16[64,8,896]{2,1,0:T(8,128)(2,1)S(1)}, u32[]{:S(2)}, u32[]{:S(2)}) async-start(bf16[64,8,896]{2,1,0:T(8,128)(2,1)} %get-tuple-element.38), calls=%async_computation.2 | async-start | bytes 1835008 | tf_op jit(solution)/shard_map/all_to_all | solution.py:441
  66.6 0.1 fusion.4
  66.7 0.1 reshape.25
  66.8 13.5 %all-to-all-done.2 = bf16[64,8,896]{2,1,0:T(8,128)(2,1)S(1)} async-done(((bf16[64,8,896]{2,1,0:T(8,128)(2,1)}), bf16[64,8,896]{2,1,0:T(8,128)(2,1)S(1)}, u32[]{:S(2)}, u32[]{:S(2)}) %all-to-all-start.2) | async-done | bytes 917536 | tf_op jit(solution)/shard_map/all_to_all | solution.py:441
  80.3 0.2 convert_reduce_fusion
  80.5 0.6 fusion.1
  (9 shorter events, 0.1 us)
Async XLA Ops:
  0.0 7.8 %copy-start = (bf16[2048,224]{0,1:T(8,128)(2,1)S(1)}, bf16[2048,224]{0,1:T(8,128)(2,1)}, u32[]{:S(2)}) copy-start(bf16[2048,224]{0,1:T(8,128)(2,1)} %param.22) | copy-start | bytes 2752516
  0.0 16.4 %copy-start.1 = (bf16[7168]{0:T(1024)(128)(2,1)S(1)}, bf16[7168]{0:T(1024)(128)(2,1)}, u32[]{:S(2)}) copy-start(bf16[7168]{0:T(1024)(128)(2,1)} %param.24) | copy-start | bytes 43012
  7.1 45.6 %collective-permute-start.3 = (bf16[2,7168,128]{2,1,0:T(8,128)(2,1)}, bf16[2,7168,128]{2,1,0:T(8,128)(2,1)}, u32[]{:S(2)}, u32[]{:S(2)}) collective-permute-start(bf16[2,7168,128]{2,1,0:T(8,128)(2,1)} %wg0.1), channel_id=1, source_target_pairs={{0,4},{4,0},{1,5},{5,1},{2,6},{6,2},{3,7},{7,3},{8,12},{12,8},{9,1... | collective-permute-start | bytes 11010056 | tf_op jit(solution)/shard_map/ppermute | solution.py:410
  7.2 45.5 %collective-permute-start.4 = (bf16[2,7168,128]{2,1,0:T(8,128)(2,1)}, bf16[2,7168,128]{2,1,0:T(8,128)(2,1)}, u32[]{:S(2)}, u32[]{:S(2)}) collective-permute-start(bf16[2,7168,128]{2,1,0:T(8,128)(2,1)} %wu0.1), channel_id=1, source_target_pairs={{0,4},{4,0},{1,5},{5,1},{2,6},{6,2},{3,7},{7,3},{8,12},{12,8},{9,1... | collective-permute-start | bytes 11010056 | tf_op jit(solution)/shard_map/ppermute | solution.py:410
  7.7 45.0 %collective-permute-start.5 = (bf16[2,128,7168]{2,1,0:T(8,128)(2,1)}, bf16[2,128,7168]{2,1,0:T(8,128)(2,1)}, u32[]{:S(2)}, u32[]{:S(2)}) collective-permute-start(bf16[2,128,7168]{2,1,0:T(8,128)(2,1)} %wd0.1), channel_id=1, source_target_pairs={{0,4},{4,0},{1,5},{5,1},{2,6},{6,2},{3,7},{7,3},{8,12},{12,8},{9,1... | collective-permute-start | bytes 11010056 | tf_op jit(solution)/shard_map/ppermute | solution.py:410
  7.8 18.0 %collective-permute-start = (bf16[2048,224]{0,1:T(8,128)(2,1)S(1)}, bf16[2048,224]{0,1:T(8,128)(2,1)S(1)}, u32[]{:S(2)}, u32[]{:S(2)}) collective-permute-start(bf16[2048,224]{0,1:T(8,128)(2,1)S(1)} %copy-done), channel_id=1, source_target_pairs={{0,4},{4,0},{1,5},{5,1},{2,6},{6,2},{3,7},{7,3},{8,12},{12,8},{9,1... | collective-permute-start | bytes 2752520 | tf_op jit(solution)/shard_map/ppermute | solution.py:409
  8.2 17.2 %all-to-all-start = ((bf16[16,4,2304]{2,1,0:T(4,128)(2,1)}), bf16[16,4,2304]{2,1,0:T(4,128)(2,1)S(1)}, u32[]{:S(2)}, u32[]{:S(2)}) async-start(bf16[16,4,2304]{2,1,0:T(4,128)(2,1)} %attention.1), calls=%async_computation | async-start | bytes 589824 | tf_op jit(solution)/shard_map/all_to_all | solution.py:411
  26.8 4.2 %collective-permute-start.1 = (bf16[224,128]{1,0:T(8,128)(2,1)S(1)}, bf16[224,128]{1,0:T(8,128)(2,1)S(1)}, u32[]{:S(2)}, u32[]{:S(2)}) collective-permute-start(bf16[224,128]{1,0:T(8,128)(2,1)S(1)} %project.1), channel_id=1, source_target_pairs={{0,32},{32,0},{64,96},{96,64},{1,33},{33,1},{65,97},{97,65},{2,34}... | collective-permute-start | bytes 172040 | tf_op jit(solution)/shard_map/ppermute | solution.py:428
  31.0 5.5 %collective-permute-start.2 = (bf16[224,128]{1,0:T(8,128)(2,1)S(1)}, bf16[224,128]{1,0:T(8,128)(2,1)S(1)}, u32[]{:S(2)}, u32[]{:S(2)}) collective-permute-start(bf16[224,128]{1,0:T(8,128)(2,1)S(1)} %add_convert_fusion.1), channel_id=1, source_target_pairs={{32,64},{64,32},{96,0},{0,96},{33,65},{65,33},{97,1},{1,97},{34,66... | collective-permute-start | bytes 172040 | tf_op jit(solution)/shard_map/ppermute | solution.py:432
  60.1 20.2 %all-to-all-start.2 = ((bf16[64,8,896]{2,1,0:T(8,128)(2,1)}), bf16[64,8,896]{2,1,0:T(8,128)(2,1)S(1)}, u32[]{:S(2)}, u32[]{:S(2)}) async-start(bf16[64,8,896]{2,1,0:T(8,128)(2,1)} %get-tuple-element.38), calls=%async_computation.2 | async-start | bytes 1835008 | tf_op jit(solution)/shard_map/all_to_all | solution.py:441

commit v8 on v7

--- a/solution.py
+++ b/solution.py
@@ -198,26 +198,29 @@
     ))
 
 
-def fetch_kernel(w_ref, o_ref, sem):
-    copy = pltpu.make_async_copy(w_ref.at[:, pl.ds(0, o_ref.shape[1]), :], o_ref, sem)
-    copy.start()
-    copy.wait()
-
-
-def fetch(w, rows, name):
+def fetch_kernel(*refs):
+    count = len(refs) // 2
+    copies = [pltpu.make_async_copy(refs[k], refs[count + k], refs[-1].at[k]) for k in range(count)]
+    for copy in copies:
+        copy.start()
+    for copy in copies:
+        copy.wait()
+
+
+def fetch(arrays, name):
     return pl.pallas_call(
         fetch_kernel,
-        out_shape=pltpu.VMEM((w.shape[0], rows, w.shape[2]), w.dtype),
-        in_specs=[pl.BlockSpec(memory_space=pltpu.HBM)],
-        out_specs=pl.BlockSpec(memory_space=pl.ANY),
-        scratch_shapes=[pltpu.SemaphoreType.DMA],
+        out_shape=tuple(pltpu.VMEM(w.shape, w.dtype) for w in arrays),
+        in_specs=[pl.BlockSpec(memory_space=pltpu.HBM)] * len(arrays),
+        out_specs=[pl.BlockSpec(memory_space=pl.ANY)] * len(arrays),
+        scratch_shapes=[pltpu.SemaphoreType.DMA((len(arrays),))],
         cost_estimate=pl.CostEstimate(flops=0, bytes_accessed=4_000_000, transcendentals=0),
         compiler_params=pltpu.CompilerParams(vmem_limit_bytes=4 * 1024 * 1024),
         name=name,
-    )(pltpu.with_memory_space_constraint(w, pltpu.HBM))
-
-
-def experts_kernel(rows_ref, gain_ref, share_ref, pre_g, pre_u, wg0, wu0, wd0, wg1, wu1, wd1, out_ref, kept_ref,
+    )(*(pltpu.with_memory_space_constraint(w, pltpu.HBM) for w in arrays))
+
+
+def experts_kernel(rows_ref, gain_ref, share_ref, pre_g, pre_u, pre_d, wg0, wu0, wd0, wg1, wu1, wd1, out_ref, kept_ref,
                    wg, wu, wd, sem, sem_down, *, ahead):
     local, depth, units = wg0.shape
     experts = 2 * local
@@ -245,7 +248,7 @@
         at = pl.ds(2 * n * tile, 2 * tile)
         downs.append([
             pltpu.make_async_copy(src.at[:, :, at], wd.at[pl.ds(k * local, local), :, at], sem_down.at[n * 2 + k])
-            for k, src in enumerate((wd0, wd1))
+            for k, src in enumerate((pre_d, wd1))
         ])
     queue = groups + downs
     for y in range(ahead):
@@ -330,7 +333,7 @@
             pltpu.VMEM((hgs * blocks, 2 * toks, depth // hgs // 2), BF),
             jax.ShapeDtypeStruct((sides, toks, span), BF),
         ),
-        in_specs=[vmem] * 3 + [pl.BlockSpec(memory_space=pl.ANY)] * 2 + [hbm] * 6,
+        in_specs=[vmem] * 3 + [pl.BlockSpec(memory_space=pl.ANY)] * 3 + [hbm] * 6,
         out_specs=[vmem] * 2,
         scratch_shapes=[
             pltpu.VMEM((experts, depth, units), BF),
@@ -424,16 +427,16 @@
     gain = norm_gain.astype(F32).reshape(ys, cores, sides, cols)
     gain = jnp.where(core == 0, gain, gain[:, ::-1]).transpose(0, 2, 1, 3).reshape(ys, sides, cores * cols)
     partial, w_gate_ = lax.optimization_barrier((partial, w_gate))
-    gate_early = fetch(w_gate_, w_gate.shape[1], "fetch_gate")
+    (gate_early,) = fetch((w_gate_,), "fetch_gate")
     got, share, gain, gate_early = lax.optimization_barrier((lax.ppermute(partial, "hg", PAIRS_A), share, gain, gate_early))
     pair = (partial.astype(F32) + got.astype(F32)).astype(BF)
-    pair, w_up_ = lax.optimization_barrier((pair, w_up))
-    up_early = fetch(w_up_, w_up.shape[1], "fetch_up")
-    got, up_early = lax.optimization_barrier((lax.ppermute(pair, "hg", PAIRS_B), up_early))
+    pair, w_up_, w_down_ = lax.optimization_barrier((pair, w_up, w_down))
+    up_early, down_early = fetch((w_up_, w_down_), "fetch_up_down")
+    got, up_early, down_early = lax.optimization_barrier((lax.ppermute(pair, "hg", PAIRS_B), up_early, down_early))
     hidden = (pair.astype(F32) + got.astype(F32)).astype(BF)
 
     rows = lax.all_to_all(jnp.broadcast_to(hidden[None], (planes,) + hidden.shape), ("y", "side"), 0, 0, tiled=True)
-    summed, kept = run_experts(rows, gain, share, (gate_early, up_early), (w_gate, w_up, w_down), other, hgs)
+    summed, kept = run_experts(rows, gain, share, (gate_early, up_early, down_early), (w_gate, w_up, w_down), other, hgs)
     quarter = width // hgs
     own_piece, oth_piece = kept[..., :cols], kept[..., cols:]
     kept = jnp.where(core == 0, jnp.concatenate([own_piece, oth_piece]), jnp.concatenate([oth_piece, own_piece]))

time: 82 us -> 82.7 us (level)
  Pallas kernels: 19.6 us -> 20.9 us
    pallas_call x2, Pallas kernels: 4.1 us -> 5.22 us  [fetch(): pl.pallas_call(fetch_kernel, out_shape=tuple((pltpu.VMEM(w.shape, w.dtype...]
    all_to_all x1, starting transfers between devices: 6.49 us -> 5.39 us  [body(): parts = lax.all_to_all(summed, ('hg', 'y', 'side'), 0, 0, tiled=True)]
    all_to_all x1, starting transfers between devices: 8.14 us -> 9.09 us  [body(): here = lax.all_to_all(message, ('y', 'side'), 0, 0, tiled=True)]
  transfers between devices with their start and end apart: 8 -> 8, of which waited for: 4 -> 3; matrix products, arithmetic and copies ran while one was open for 1% -> 1% of each run, Pallas kernels for 6% -> 8%
where the time goes in v8:
time: 82.7 us; the launch traced here: 82.2 us
  waiting for transfers between devices  22.9 us (28%)
  Pallas kernels  20.9 us (25%)
  starting transfers between devices  19.9 us (24%)
  blocking collectives  16.6 us (20%)
  other arithmetic  1.06 us (1%)
    all_to_all x1, blocking collectives, body(): lax.all_to_all(jnp.broadcast_to(hidden[None], (planes,) + hidden.shape),...  16.6 us
    all_to_all x1, waiting for transfers between devices, body(): parts = lax.all_to_all(summed, ('hg', 'y', 'side'), 0, 0, tiled=True)  13.5 us
    all_to_all x1, starting transfers between devices, body(): here = lax.all_to_all(message, ('y', 'side'), 0, 0, tiled=True)  9.09 us
    all_to_all x1, waiting for transfers between devices, body(): here = lax.all_to_all(message, ('y', 'side'), 0, 0, tiled=True)  8.82 us
    pallas_call x1, Pallas kernels, run_experts(): pl.pallas_call(functools.partial(experts_kernel, ahead=ahead), out_shape=...  7.6 us
    pallas_call x1, Pallas kernels, attention(): pl.pallas_call(functools.partial(attention_kernel, span=span, ahead=ahead...  7.12 us
    all_to_all x1, starting transfers between devices, body(): parts = lax.all_to_all(summed, ('hg', 'y', 'side'), 0, 0, tiled=True)  5.39 us
    pallas_call x2, Pallas kernels, fetch(): pl.pallas_call(fetch_kernel, out_shape=tuple((pltpu.VMEM(w.shape, w.dtype...  5.22 us
  transfers between devices with their start and end apart: 8, of which 3 were waited for; matrix products, arithmetic and copies ran while one was open for 1% of the time, Pallas kernels for 8%

profile of v8, /device:TPU:0, one launch (start us, length us, event | category | flops | bytes accessed | tf_op | source)
XLA Modules:
  0.0 82.2 jit_solution(11654302682448471570)
XLA Ops:
  0.0 0.0 copy-start
  0.0 0.0 copy-start.1
  0.0 7.1 %attention.1 = bf16[16,4,2304]{2,1,0:T(4,128)(2,1)} custom-call(s32[2]{0:T(128)} %len_hbm.1, s32[4,4]{1,0:T(4,128)} %routes_hbm.1, s32[4,4]{1,0:T(4,128)} %ints_hbm.1, bf16[4,2048]{1,0:T(4,128)(2,1)} %qn_hbm.1, bf16[4,1024]{1,0:T(4,128)(2,1)} %qr_hbm.1, bf16[4,7168]{1,0:T(4,128)(2,1)} %res_hbm.1, bf16[16,128,512]{2,1,0:T(8,128)(2,1)} %wa_hbm.1, ...), custom_call_target="tpu_custom_call" | custom-call | tf_op jit(solution)/shard_map/attention/pallas_call | solution.py:167
  7.1 0.1 collective-permute-start.3
  7.2 0.5 collective-permute-start.4
  7.7 0.1 collective-permute-start.5
  7.8 0.0 copy-done
  7.8 0.4 collective-permute-start
  8.2 9.1 %all-to-all-start = ((bf16[16,4,2304]{2,1,0:T(4,128)(2,1)}), bf16[16,4,2304]{2,1,0:T(4,128)(2,1)S(1)}, u32[]{:S(2)}, u32[]{:S(2)}) async-start(bf16[16,4,2304]{2,1,0:T(4,128)(2,1)} %attention.1), calls=%async_computation | async-start | bytes 589824 | tf_op jit(solution)/shard_map/all_to_all | solution.py:414
  17.3 0.0 copy-done.1
  17.4 0.1 reshape.24
  17.5 0.1 reshape.21.gain_ref
  17.6 8.8 %all-to-all-done.here_ref = bf16[16,4,2304]{2,1,0:T(4,128)(2,1)S(1)} async-done(((bf16[16,4,2304]{2,1,0:T(4,128)(2,1)}), bf16[16,4,2304]{2,1,0:T(4,128)(2,1)S(1)}, u32[]{:S(2)}, u32[]{:S(2)}) %all-to-all-start) | async-done | bytes 294944 | tf_op jit(solution)/shard_map/all_to_all | solution.py:414
  26.5 0.1 reshape.22
  26.5 0.1 reduce_sum.18
  26.6 0.1 constant_dynamic-slice_fusion.1
  26.7 0.0 collective-permute-done
  26.8 1.0 %project.1 = bf16[224,128]{1,0:T(8,128)(2,1)S(1)} custom-call(bf16[16,4,2304]{2,1,0:T(4,128)(2,1)S(1)} %all-to-all-done.here_ref, bf16[224,2048]{1,0:T(8,128)(2,1)S(1)} %bitcast.6, bf16[224,2048]{1,0:T(8,128)(2,1)S(1)} %bitcast.7), custom_call_target="tpu_custom_call" | custom-call | flops 117440512 | bytes 2500000 | tf_op jit(solution)/shard_map/project/pallas_call | solution.py:385
  27.7 1.5 %collective-permute-start.1 = (bf16[224,128]{1,0:T(8,128)(2,1)S(1)}, bf16[224,128]{1,0:T(8,128)(2,1)S(1)}, u32[]{:S(2)}, u32[]{:S(2)}) collective-permute-start(bf16[224,128]{1,0:T(8,128)(2,1)S(1)} %project.1), channel_id=1, source_target_pairs={{0,32},{32,0},{64,96},{96,64},{1,33},{33,1},{65,97},{97,65},{2,34}... | collective-permute-start | bytes 172040 | tf_op jit(solution)/shard_map/ppermute | solution.py:431
  29.3 0.1 maximum_multiply_fusion.share_ref
  29.3 2.0 %fetch_gate.1.pre_g = bf16[2,7168,128]{2,1,0:T(8,128)(2,1)S(1)} custom-call(bf16[2,7168,128]{2,1,0:T(8,128)(2,1)} %wg0.1), custom_call_target="tpu_custom_call" | custom-call | bytes 4000000 | tf_op jit(solution)/shard_map/fetch_gate/pallas_call | solution.py:211
  31.4 0.5 collective-permute-done.1
  32.0 2.8 %collective-permute-start.2 = (bf16[224,128]{1,0:T(8,128)(2,1)S(1)}, bf16[224,128]{1,0:T(8,128)(2,1)S(1)}, u32[]{:S(2)}, u32[]{:S(2)}) collective-permute-start(bf16[224,128]{1,0:T(8,128)(2,1)S(1)} %add_convert_fusion.1), channel_id=1, source_target_pairs={{32,64},{64,32},{96,0},{0,96},{33,65},{65,33},{97,1},{1,97},{34,66... | collective-permute-start | bytes 172040 | tf_op jit(solution)/shard_map/ppermute | solution.py:435
  34.8 3.2 %fetch_up_down.1 = (bf16[2,7168,128]{2,1,0:T(8,128)(2,1)S(1)}, bf16[2,128,7168]{2,1,0:T(8,128)(2,1)S(1)}) custom-call(bf16[2,7168,128]{2,1,0:T(8,128)(2,1)} %wu0.1, bf16[2,128,7168]{2,1,0:T(8,128)(2,1)} %wd0.1), custom_call_target="tpu_custom_call" | custom-call | bytes 4000000 | tf_op jit(solution)/shard_map/fetch_up_down/pallas_call | solution.py:211
  38.0 0.0 collective-permute-done.2
  38.0 0.1 broadcast_in_dim.2
  38.2 16.6 %all_to_all.15.rows_ref = bf16[16,224,128]{2,1,0:T(8,128)(2,1)S(1)} all-to-all(bf16[16,224,128]{2,1,0:T(8,128)(2,1)S(1)} %broadcast_in_dim.2), channel_id=1, replica_groups=mesh['hg'=4,'y'=4,'c'=2,'side'=4] {'y','side'}, dimensions={0} | all-to-all | bytes 1835008 | tf_op jit(solution)/shard_map/all_to_all | solution.py:438
  54.7 0.0 collective-permute-done.3.wg1
  54.7 0.0 collective-permute-done.4.wu1
  54.7 0.0 collective-permute-done.5.wd1
  54.7 7.6 %experts.1 = (bf16[64,8,896]{2,1,0:T(8,128)(2,1)}, bf16[4,4,448]{2,1,0:T(4,128)(2,1)S(1)}) custom-call(bf16[16,224,128]{2,1,0:T(8,128)(2,1)S(1)} %all_to_all.15.rows_ref, f32[4,4,448]{2,1,0:T(4,128)S(1)} %reshape.21.gain_ref, f32[64,4]{1,0:T(8,128)S(1)} %maximum_multiply_fusion.share_ref, bf16[2,7168,128]{2,1,0:T(8,128)(2,1)S(1)} %fetch_gate.1.pre_g, ...), custom_call_target="tpu_custom_call" | custom-call | flops 1409286144 | bytes 24000000 | tf_op jit(solution)/shard_map/experts/pallas_call | solution.py:330
  62.3 5.4 %all-to-all-start.2 = ((bf16[64,8,896]{2,1,0:T(8,128)(2,1)}), bf16[64,8,896]{2,1,0:T(8,128)(2,1)S(1)}, u32[]{:S(2)}, u32[]{:S(2)}) async-start(bf16[64,8,896]{2,1,0:T(8,128)(2,1)} %get-tuple-element.46), calls=%async_computation.2 | async-start | bytes 1835008 | tf_op jit(solution)/shard_map/all_to_all | solution.py:444
  67.7 0.1 fusion.4
  67.9 0.1 reshape.25
  67.9 13.5 %all-to-all-done.2 = bf16[64,8,896]{2,1,0:T(8,128)(2,1)S(1)} async-done(((bf16[64,8,896]{2,1,0:T(8,128)(2,1)}), bf16[64,8,896]{2,1,0:T(8,128)(2,1)S(1)}, u32[]{:S(2)}, u32[]{:S(2)}) %all-to-all-start.2) | async-done | bytes 917536 | tf_op jit(solution)/shard_map/all_to_all | solution.py:444
  81.4 0.2 convert_reduce_fusion
  81.6 0.6 fusion.1
  (9 shorter events, 0.1 us)
Async XLA Ops:
  0.0 7.8 %copy-start = (bf16[2048,224]{0,1:T(8,128)(2,1)S(1)}, bf16[2048,224]{0,1:T(8,128)(2,1)}, u32[]{:S(2)}) copy-start(bf16[2048,224]{0,1:T(8,128)(2,1)} %param.22) | copy-start | bytes 2752516
  0.0 17.3 %copy-start.1 = (bf16[7168]{0:T(1024)(128)(2,1)S(1)}, bf16[7168]{0:T(1024)(128)(2,1)}, u32[]{:S(2)}) copy-start(bf16[7168]{0:T(1024)(128)(2,1)} %param.24) | copy-start | bytes 43012
  7.1 47.6 %collective-permute-start.3 = (bf16[2,7168,128]{2,1,0:T(8,128)(2,1)}, bf16[2,7168,128]{2,1,0:T(8,128)(2,1)}, u32[]{:S(2)}, u32[]{:S(2)}) collective-permute-start(bf16[2,7168,128]{2,1,0:T(8,128)(2,1)} %wg0.1), channel_id=1, source_target_pairs={{0,4},{4,0},{1,5},{5,1},{2,6},{6,2},{3,7},{7,3},{8,12},{12,8},{9,1... | collective-permute-start | bytes 11010056 | tf_op jit(solution)/shard_map/ppermute | solution.py:413
  7.2 47.5 %collective-permute-start.4 = (bf16[2,7168,128]{2,1,0:T(8,128)(2,1)}, bf16[2,7168,128]{2,1,0:T(8,128)(2,1)}, u32[]{:S(2)}, u32[]{:S(2)}) collective-permute-start(bf16[2,7168,128]{2,1,0:T(8,128)(2,1)} %wu0.1), channel_id=1, source_target_pairs={{0,4},{4,0},{1,5},{5,1},{2,6},{6,2},{3,7},{7,3},{8,12},{12,8},{9,1... | collective-permute-start | bytes 11010056 | tf_op jit(solution)/shard_map/ppermute | solution.py:413
  7.7 47.0 %collective-permute-start.5 = (bf16[2,128,7168]{2,1,0:T(8,128)(2,1)}, bf16[2,128,7168]{2,1,0:T(8,128)(2,1)}, u32[]{:S(2)}, u32[]{:S(2)}) collective-permute-start(bf16[2,128,7168]{2,1,0:T(8,128)(2,1)} %wd0.1), channel_id=1, source_target_pairs={{0,4},{4,0},{1,5},{5,1},{2,6},{6,2},{3,7},{7,3},{8,12},{12,8},{9,1... | collective-permute-start | bytes 11010056 | tf_op jit(solution)/shard_map/ppermute | solution.py:413
  7.8 18.9 %collective-permute-start = (bf16[2048,224]{0,1:T(8,128)(2,1)S(1)}, bf16[2048,224]{0,1:T(8,128)(2,1)S(1)}, u32[]{:S(2)}, u32[]{:S(2)}) collective-permute-start(bf16[2048,224]{0,1:T(8,128)(2,1)S(1)} %copy-done), channel_id=1, source_target_pairs={{0,4},{4,0},{1,5},{5,1},{2,6},{6,2},{3,7},{7,3},{8,12},{12,8},{9,1... | collective-permute-start | bytes 2752520 | tf_op jit(solution)/shard_map/ppermute | solution.py:412
  8.2 18.2 %all-to-all-start = ((bf16[16,4,2304]{2,1,0:T(4,128)(2,1)}), bf16[16,4,2304]{2,1,0:T(4,128)(2,1)S(1)}, u32[]{:S(2)}, u32[]{:S(2)}) async-start(bf16[16,4,2304]{2,1,0:T(4,128)(2,1)} %attention.1), calls=%async_computation | async-start | bytes 589824 | tf_op jit(solution)/shard_map/all_to_all | solution.py:414
  27.7 4.2 %collective-permute-start.1 = (bf16[224,128]{1,0:T(8,128)(2,1)S(1)}, bf16[224,128]{1,0:T(8,128)(2,1)S(1)}, u32[]{:S(2)}, u32[]{:S(2)}) collective-permute-start(bf16[224,128]{1,0:T(8,128)(2,1)S(1)} %project.1), channel_id=1, source_target_pairs={{0,32},{32,0},{64,96},{96,64},{1,33},{33,1},{65,97},{97,65},{2,34}... | collective-permute-start | bytes 172040 | tf_op jit(solution)/shard_map/ppermute | solution.py:431
  32.0 6.0 %collective-permute-start.2 = (bf16[224,128]{1,0:T(8,128)(2,1)S(1)}, bf16[224,128]{1,0:T(8,128)(2,1)S(1)}, u32[]{:S(2)}, u32[]{:S(2)}) collective-permute-start(bf16[224,128]{1,0:T(8,128)(2,1)S(1)} %add_convert_fusion.1), channel_id=1, source_target_pairs={{32,64},{64,32},{96,0},{0,96},{33,65},{65,33},{97,1},{1,97},{34,66... | collective-permute-start | bytes 172040 | tf_op jit(solution)/shard_map/ppermute | solution.py:435
  62.3 19.1 %all-to-all-start.2 = ((bf16[64,8,896]{2,1,0:T(8,128)(2,1)}), bf16[64,8,896]{2,1,0:T(8,128)(2,1)S(1)}, u32[]{:S(2)}, u32[]{:S(2)}) async-start(bf16[64,8,896]{2,1,0:T(8,128)(2,1)} %get-tuple-element.46), calls=%async_computation.2 | async-start | bytes 1835008 | tf_op jit(solution)/shard_map/all_to_all | solution.py:444
